TPU v7x, 256 devices: a whole 4x4x8 slice. The times are simulated.
256 devices in a mesh: seq: 32 (over x, y, core), uly: 8 (over z).
Axes of the slice: x: 4, y: 4, z: 8, core: 2. Of those that a mesh axis runs over, the one named last changes fastest.
Arguments:
- queries: bfloat16 [32768, 5120], P(('seq', 'uly')), may hold values from -12 to 12
- keys: bfloat16 [32768, 5120], P(('seq', 'uly')), may hold values from -12 to 12
- values: bfloat16 [32768, 5120], P(('seq', 'uly')), may hold values from -6 to 6
- out_grad: bfloat16 [32768, 5120], P(('seq', 'uly')), may hold values from -6 to 6
- tile_offset: int32 [256], replicated, may hold values from 0 to 3, as said below
Outputs:
- attended: bfloat16 [32768, 5120], P(('seq', 'uly'))
- query_grad: bfloat16 [32768, 5120], P(('seq', 'uly'))
- key_grad: bfloat16 [32768, 5120], P(('seq', 'uly'))
- value_grad: bfloat16 [32768, 5120], P(('seq', 'uly'))
Inputs may be any that keep to these rules, and one draw needn't show every extreme that they name: Clips are packed in order, each of whole tiles of 128 rows, and tile_offset[t] counts the tiles of t's clip before tile t. A clip begins at tile 0 and at every tile t with t % 4 == 2, and at no other tile t > 0 with t % (8) == 0. No clip has more than 4 tiles and some clip has exactly 4.
All inputs are finite; a program needn't handle non-finite values.
Results may differ from a plain program's by a relative error of at most 0.02.
Values may be sent and summed in bfloat16 or wider, within the bound.
No kernel may reach another device: no remote copies, remote signals or barrier semaphores. Data moves between devices by JAX's collectives and lax.ppermute only.
A program may use at most 128 MiB of HBM per device.

v0:
```python
from functools import partial

import jax
import jax.numpy as jnp
from jax import lax
from jax.sharding import PartitionSpec as P

HD = 128
TILE = 128


def extended(cells, sides, width):
    for axis, dim in sides:
        count = lax.axis_size(axis)
        ends = count - 1
        head = lax.slice_in_dim(cells, 0, width, axis=dim)
        tail = lax.slice_in_dim(cells, cells.shape[dim] - width, cells.shape[dim], axis=dim)
        cells = jnp.concatenate(
            [
                lax.ppermute(tail, axis, [(i, (i + 1) % count) for i in range(ends)]),
                cells,
                lax.ppermute(head, axis, [((i + 1) % count, i) for i in range(ends)]),
            ],
            axis=dim,
        )
    return cells


def shifted(value, axis, steps):
    count = lax.axis_size(axis)
    first, last = (max(0, -steps), min(count, count - steps))
    return lax.ppermute(value, axis, [(source, source + steps) for source in range(first, last)])


def masked_scores(query_rows, key_rows, query_first, key_first, factor):
    raw_scores = jnp.dot(query_rows, key_rows.T, preferred_element_type=jnp.float32) * factor
    return jnp.where(query_first[:, None] == key_first[None, :], raw_scores, -jnp.inf)


def head_slice(matrix, row_begin, row_count, column):
    return lax.dynamic_slice(matrix, (row_begin, column), (row_count, HD))


def pair_slice(stacked, member, row_begin, row_count, column):
    return lax.dynamic_slice(stacked, (member, row_begin, column), (1, row_count, HD))[0]


def shards(queries, keys, values, out_grad, tile_offset):
    regrouped = (
        lax.all_to_all(queries, "uly", split_axis=1, concat_axis=0, tiled=True),
        lax.all_to_all(keys, "uly", split_axis=1, concat_axis=0, tiled=True),
        lax.all_to_all(values, "uly", split_axis=1, concat_axis=0, tiled=True),
        lax.all_to_all(out_grad, "uly", split_axis=1, concat_axis=0, tiled=True),
    )
    query_all, key_all, value_all, grad_all = regrouped
    group_rows, channels = query_all.shape
    reach_rows = group_rows // 2
    heads_here = channels // HD
    factor = HD ** (-0.5)
    key_value = extended(jnp.stack((key_all, value_all)), (("seq", 1),), reach_rows)
    group_tiles = group_rows // TILE
    reach_tiles = reach_rows // TILE
    tile_first = jnp.arange(tile_offset.shape[0], dtype=jnp.int32) - tile_offset
    outside = jnp.full((reach_tiles,), -1, jnp.int32)
    padded_first = jnp.concatenate((outside, tile_first, outside))
    window_first = lax.dynamic_slice_in_dim(
        padded_first, lax.axis_index("seq") * group_tiles, group_tiles + 2 * reach_tiles
    )
    ext_first = jnp.broadcast_to(window_first[:, None], (window_first.shape[0], TILE)).reshape(-1)
    zero_tile = jnp.zeros((reach_rows, HD), jnp.float32)

    def one_head(head_index, carried):
        out_all, grad_query, key_own, value_own, rim_low, rim_high, row_stats = carried
        column = head_index * HD
        key_sums = [zero_tile] * 4
        value_sums = [zero_tile] * 4
        block_outs = []
        block_dq = []
        block_lse = []
        block_delta = []
        for block_index in range(2):
            query_rows = head_slice(query_all, block_index * reach_rows, reach_rows, column)
            grad_rows = head_slice(grad_all, block_index * reach_rows, reach_rows, column)
            query_first = ext_first[(block_index + 1) * reach_rows : (block_index + 2) * reach_rows]
            key_tiles = [
                pair_slice(key_value, 0, (block_index + offset) * reach_rows, reach_rows, column)
                for offset in range(3)
            ]
            value_tiles = [
                pair_slice(key_value, 1, (block_index + offset) * reach_rows, reach_rows, column)
                for offset in range(3)
            ]
            key_firsts = [
                ext_first[
                    (block_index + offset) * reach_rows : (block_index + offset + 1) * reach_rows
                ]
                for offset in range(3)
            ]
            scores = []
            for offset in range(3):
                compute = partial(
                    masked_scores,
                    query_rows,
                    key_tiles[offset],
                    query_first,
                    key_firsts[offset],
                    factor,
                )
                if offset == 1:
                    scores.append(compute())
                else:
                    scores.append(compute())
            row_max = jnp.max(jnp.stack([jnp.max(scored, axis=1) for scored in scores]), axis=0)
            row_sum = jnp.sum(jnp.exp(scores[0] - row_max[:, None]), axis=1)
            row_sum = row_sum + jnp.sum(jnp.exp(scores[1] - row_max[:, None]), axis=1)
            row_sum = row_sum + jnp.sum(jnp.exp(scores[2] - row_max[:, None]), axis=1)
            log_total = row_max + jnp.log(row_sum)

            def forward_tile(scored, value_tile):
                weights_half = jnp.exp(scored - log_total[:, None]).astype(jnp.bfloat16)
                return (
                    weights_half,
                    jnp.dot(weights_half, value_tile, preferred_element_type=jnp.float32),
                )

            halves = []
            attended = zero_tile
            for offset in range(3):
                compute = partial(forward_tile, scores[offset], value_tiles[offset])
                if offset == 1:
                    result = compute()
                else:
                    result = compute()
                halves.append(result[0])
                attended = attended + result[1]
            attended = attended.astype(jnp.bfloat16)
            row_delta = jnp.sum(
                grad_rows.astype(jnp.float32) * attended.astype(jnp.float32), axis=1
            )

            def backward_tile(scored, weights_half, key_tile, value_tile, with_keys):
                dweights = jnp.dot(grad_rows, value_tile.T, preferred_element_type=jnp.float32)
                weights = jnp.exp(scored - log_total[:, None])
                dscores = (weights * (dweights - row_delta[:, None])).astype(jnp.bfloat16)
                query_part = jnp.dot(dscores, key_tile, preferred_element_type=jnp.float32)
                key_part = (
                    jnp.dot(dscores.T, query_rows, preferred_element_type=jnp.float32) * factor
                )
                value_part = jnp.dot(weights_half.T, grad_rows, preferred_element_type=jnp.float32)
                return (query_part, key_part, value_part)

            query_sum = zero_tile
            for offset in range(3):
                ext_tile = block_index + offset
                with_keys = True
                compute = partial(
                    backward_tile,
                    scores[offset],
                    halves[offset],
                    key_tiles[offset],
                    value_tiles[offset],
                    with_keys,
                )
                if offset == 1:
                    pieces = compute()
                else:
                    pieces = compute()
                query_sum = query_sum + pieces[0]
                key_sums[ext_tile] = key_sums[ext_tile] + pieces[1]
                value_sums[ext_tile] = value_sums[ext_tile] + pieces[2]
            block_dq.append((query_sum * factor).astype(jnp.bfloat16))
            block_outs.append(attended)
            block_lse.append(log_total)
            block_delta.append(row_delta)
        out_all = lax.dynamic_update_slice(
            out_all, jnp.concatenate(block_outs, axis=0), (0, column)
        )
        grad_query = lax.dynamic_update_slice(
            grad_query, jnp.concatenate(block_dq, axis=0), (0, column)
        )
        key_own = lax.dynamic_update_slice(
            key_own, jnp.concatenate((key_sums[1], key_sums[2]), axis=0), (0, column)
        )
        value_own = lax.dynamic_update_slice(
            value_own, jnp.concatenate((value_sums[1], value_sums[2]), axis=0), (0, column)
        )
        rim_low = lax.dynamic_update_slice(
            rim_low, jnp.stack((key_sums[0], value_sums[0])), (0, 0, column)
        )
        rim_high = lax.dynamic_update_slice(
            rim_high, jnp.stack((key_sums[3], value_sums[3])), (0, 0, column)
        )
        head_stats = jnp.stack((jnp.concatenate(block_lse), jnp.concatenate(block_delta)))[
            :, None, :
        ]
        row_stats = lax.dynamic_update_slice(row_stats, head_stats, (0, head_index, 0))
        return (out_all, grad_query, key_own, value_own, rim_low, rim_high, row_stats)

    start_state = (
        jnp.zeros((group_rows, channels), jnp.bfloat16),
        jnp.zeros((group_rows, channels), jnp.bfloat16),
        jnp.zeros((group_rows, channels), jnp.float32),
        jnp.zeros((group_rows, channels), jnp.float32),
        jnp.zeros((2, reach_rows, channels), jnp.float32),
        jnp.zeros((2, reach_rows, channels), jnp.float32),
        jnp.zeros((2, heads_here, group_rows), jnp.float32),
    )
    out_all, grad_query, key_own, value_own, rim_low, rim_high, row_stats = lax.fori_loop(
        0, heads_here, one_head, start_state
    )
    from_next = shifted(rim_low, "seq", -1)
    from_prev = shifted(rim_high, "seq", 1)
    incoming = jnp.concatenate((from_prev, from_next), axis=1)
    key_total = key_own + incoming[0]
    value_total = value_own + incoming[1]
    key_final = key_total.astype(jnp.bfloat16)
    value_final = value_total.astype(jnp.bfloat16)
    returned = (
        lax.all_to_all(out_all, "uly", split_axis=0, concat_axis=1, tiled=True),
        lax.all_to_all(grad_query, "uly", split_axis=0, concat_axis=1, tiled=True),
        lax.all_to_all(key_final, "uly", split_axis=0, concat_axis=1, tiled=True),
        lax.all_to_all(value_final, "uly", split_axis=0, concat_axis=1, tiled=True),
    )
    return (returned[0], returned[1], returned[2], returned[3])


def solution(mesh):
    return jax.shard_map(
        shards,
        mesh=mesh,
        in_specs=(
            P(("seq", "uly"), None),
            P(("seq", "uly"), None),
            P(("seq", "uly"), None),
            P(("seq", "uly"), None),
            P(),
        ),
        out_specs=(
            P(("seq", "uly"), None),
            P(("seq", "uly"), None),
            P(("seq", "uly"), None),
            P(("seq", "uly"), None),
        ),
        check_vma=False,
    )
```

profile of v0, /device:TPU:0, one launch (start us, length us, event | category | flops | bytes accessed | tf_op | source)
XLA Modules:
  0.0 424.8 jit_solution(8084660325597854526)
XLA Ops:
  0.6 2.6 copy.68
  3.2 6.7 %all-to-all-start = ((bf16[128,8,640]{2,0,1:T(8,128)(2,1)}), bf16[128,8,640]{2,0,1:T(8,128)(2,1)S(1)}, u32[]{:S(2)}, u32[]{:S(2)}) async-start(bf16[128,8,640]{2,0,1:T(8,128)(2,1)} %bitcast.147), calls=%async_computation | async-start | bytes 2621440 | tf_op jit(solution)/shard_map/all_to_all | solution.py:50
  10.0 1.2 copy.67
  11.2 33.2 %all-to-all-done = bf16[128,8,640]{2,0,1:T(8,128)(2,1)S(1)} async-done(((bf16[128,8,640]{2,0,1:T(8,128)(2,1)}), bf16[128,8,640]{2,0,1:T(8,128)(2,1)S(1)}, u32[]{:S(2)}, u32[]{:S(2)}) %all-to-all-start) | async-done | bytes 1310752 | tf_op jit(solution)/shard_map/all_to_all | solution.py:50
  44.4 3.6 all-to-all-start.1
  48.0 2.5 copy.66
  50.5 32.2 %all-to-all-done.1 = bf16[128,8,640]{2,0,1:T(8,128)(2,1)S(1)} async-done(((bf16[128,8,640]{2,0,1:T(8,128)(2,1)}), bf16[128,8,640]{2,0,1:T(8,128)(2,1)S(1)}, u32[]{:S(2)}, u32[]{:S(2)}) %all-to-all-start.1) | async-done | bytes 1310752 | tf_op jit(solution)/shard_map/all_to_all | solution.py:51
  82.7 4.3 %all-to-all-start.2 = ((bf16[128,8,640]{2,0,1:T(8,128)(2,1)}), bf16[128,8,640]{2,0,1:T(8,128)(2,1)}, u32[]{:S(2)}, u32[]{:S(2)}) async-start(bf16[128,8,640]{2,0,1:T(8,128)(2,1)} %bitcast.236), calls=%async_computation.2 | async-start | bytes 2621440 | tf_op jit(solution)/shard_map/all_to_all | solution.py:52
  87.0 2.5 copy.65
  89.5 32.3 %all-to-all-done.2 = bf16[128,8,640]{2,0,1:T(8,128)(2,1)} async-done(((bf16[128,8,640]{2,0,1:T(8,128)(2,1)}), bf16[128,8,640]{2,0,1:T(8,128)(2,1)}, u32[]{:S(2)}, u32[]{:S(2)}) %all-to-all-start.2) | async-done | bytes 1310752 | tf_op jit(solution)/shard_map/all_to_all | solution.py:52
  121.8 3.6 all-to-all-start.3
  125.4 3.4 fusion.194
  128.8 3.1 collective-permute-start
  131.9 1.3 collective-permute-start.1
  133.7 3.5 collective-permute-done.1
  137.1 5.3 %pad_maximum_fusion = bf16[2,2048,640]{2,1,0:T(8,128)(2,1)} fusion(bf16[2,512,640]{2,1,0:T(8,128)(2,1)} %collective-permute-done.1, bf16[1,1024,640]{2,1,0:T(8,128)(2,1)} %bitcast.18, bf16[1,1024,640]{2,1,0:T(8,128)(2,1)} %bitcast.231, bf16[2,512,640]{2,1,0:T(8,128)(2,1)} %collective-permute-done), kind=kLoop, calls=%fused_computation.230 | loop fusion | flops 20971520 | bytes 10485760 | tf_op jit(solution)/shard_map/concatenate | solution.py:18
  142.4 17.7 %all-to-all-done.3 = bf16[128,8,640]{2,0,1:T(8,128)(2,1)S(1)} async-done(((bf16[128,8,640]{2,0,1:T(8,128)(2,1)}), bf16[128,8,640]{2,0,1:T(8,128)(2,1)S(1)}, u32[]{:S(2)}, u32[]{:S(2)}) %all-to-all-start.3) | async-done | bytes 1310752 | tf_op jit(solution)/shard_map/all_to_all | solution.py:53
  162.4 1.6 broadcast.37.clone
  164.0 1.7 broadcast.36.clone
  165.8 1.7 broadcast.37
  167.5 1.7 broadcast.36
  169.1 103.9 %while.23 = (s32[]{:T(128)}, bf16[1024,640]{1,0:T(8,128)(2,1)}, bf16[1024,640]{1,0:T(8,128)(2,1)}, f32[1024,640]{1,0:T(8,128)}, f32[1024,640]{1,0:T(8,128)}, /*i...) while((s32[]{:T(128)}, bf16[1024,640]{1,0:T(8,128)(2,1)}, ...), condition=%wide.region_15.0_spmd, body=%wide.region_0.15_spmd.sunk | while | flops 2441476096 | bytes 82879760 | solution.py:208
  169.1 1.2 fusion.360
  170.4 1.2 fusion.364
  171.6 1.2 fusion.366
  172.8 1.2 fusion.365
  187.6 1.2 maximum_dynamic-update-slice_fusion.10
  189.9 1.2 fusion.360
  191.1 1.2 fusion.364
  192.4 1.2 fusion.366
  193.6 1.2 fusion.365
  210.7 1.2 fusion.360
  211.9 1.2 fusion.364
  213.1 1.2 fusion.366
  214.4 1.2 fusion.365
  229.2 1.2 maximum_dynamic-update-slice_fusion.10
  230.4 1.2 maximum_dynamic-update-slice_fusion.11
  231.6 1.2 fusion.360
  232.8 1.2 fusion.364
  234.0 1.2 fusion.366
  235.2 1.2 fusion.365
  252.4 1.2 fusion.360
  253.6 1.2 fusion.364
  254.9 1.2 fusion.366
  256.1 1.2 fusion.365
  273.1 3.6 all-to-all-start.4
  276.7 3.7 collective-permute-start.2
  280.3 1.3 collective-permute-start.3
  281.6 30.1 %all-to-all-done.4 = bf16[8,128,640]{2,1,0:T(8,128)(2,1)S(1)} async-done(((bf16[8,128,640]{2,1,0:T(8,128)(2,1)}), bf16[8,128,640]{2,1,0:T(8,128)(2,1)S(1)}, u32[]{:S(2)}, u32[]{:S(2)}) %all-to-all-start.4) | async-done | bytes 1310752 | tf_op jit(solution)/shard_map/all_to_all | solution.py:219
  311.7 4.5 %all-to-all-start.5 = ((bf16[8,128,640]{2,1,0:T(8,128)(2,1)}), bf16[8,128,640]{2,1,0:T(8,128)(2,1)}, u32[]{:S(2)}, u32[]{:S(2)}) async-start(bf16[8,128,640]{2,1,0:T(8,128)(2,1)} %bitcast.24), calls=%async_computation.5 | async-start | bytes 2621440 | tf_op jit(solution)/shard_map/all_to_all | solution.py:220
  316.2 1.9 constant_dynamic-update-slice_fusion.1
  318.2 2.1 constant_dynamic-update-slice_fusion
  321.4 1.6 fusion.191
  323.0 27.9 %all-to-all-done.5 = bf16[8,128,640]{2,1,0:T(8,128)(2,1)} async-done(((bf16[8,128,640]{2,1,0:T(8,128)(2,1)}), bf16[8,128,640]{2,1,0:T(8,128)(2,1)}, u32[]{:S(2)}, u32[]{:S(2)}) %all-to-all-start.5) | async-done | bytes 1310752 | tf_op jit(solution)/shard_map/all_to_all | solution.py:220
  350.9 36.6 %all_to_all.146 = bf16[8,128,640]{2,1,0:T(8,128)(2,1)} all-to-all(bf16[8,128,640]{2,1,0:T(8,128)(2,1)S(1)} %bitcast.232), channel_id=1, replica_groups=mesh['seq'=32,'uly'=8] {'uly'}, dimensions={0} | all-to-all | bytes 2621440 | tf_op jit(solution)/shard_map/all_to_all | solution.py:221
  387.4 3.6 all-to-all-start.7
  391.0 1.5 copy.43
  392.5 2.4 copy.47
  394.9 2.5 copy.44
  397.4 2.4 copy.48
  399.9 1.5 copy.45
  401.3 2.4 copy.49
  403.7 18.8 %all-to-all-done.7 = bf16[8,128,640]{2,1,0:T(8,128)(2,1)S(1)} async-done(((bf16[8,128,640]{2,1,0:T(8,128)(2,1)}), bf16[8,128,640]{2,1,0:T(8,128)(2,1)S(1)}, u32[]{:S(2)}, u32[]{:S(2)}) %all-to-all-start.7) | async-done | bytes 1310752 | tf_op jit(solution)/shard_map/all_to_all | solution.py:222
  423.4 1.4 copy.50
  (240 shorter events, 79.5 us)
Async XLA Ops:
  0.6 9.3 %copy-start.5 = (bf16[128,5120]{1,0:T(8,128)(2,1)S(1)}, bf16[128,5120]{1,0:T(8,128)(2,1)}, u32[]{:S(2)}) copy-start(bf16[128,5120]{1,0:T(8,128)(2,1)} %param.8) | copy-start | bytes 3932164
  3.2 41.2 %all-to-all-start = ((bf16[128,8,640]{2,0,1:T(8,128)(2,1)}), bf16[128,8,640]{2,0,1:T(8,128)(2,1)S(1)}, u32[]{:S(2)}, u32[]{:S(2)}) async-start(bf16[128,8,640]{2,0,1:T(8,128)(2,1)} %bitcast.147), calls=%async_computation | async-start | bytes 2621440 | tf_op jit(solution)/shard_map/all_to_all | solution.py:50
  44.4 38.3 %all-to-all-start.1 = ((bf16[128,8,640]{2,0,1:T(8,128)(2,1)}), bf16[128,8,640]{2,0,1:T(8,128)(2,1)S(1)}, u32[]{:S(2)}, u32[]{:S(2)}) async-start(bf16[128,8,640]{2,0,1:T(8,128)(2,1)} %bitcast.235), calls=%async_computation.1 | async-start | bytes 2621440 | tf_op jit(solution)/shard_map/all_to_all | solution.py:51
  82.7 6.8 %copy-start.1 = (bf16[128,8,640]{2,0,1:T(8,128)(2,1)}, bf16[128,8,640]{2,0,1:T(8,128)(2,1)S(1)}, u32[]{:S(2)}) copy-start(bf16[128,8,640]{2,0,1:T(8,128)(2,1)S(1)} %all-to-all-done.1) | copy-start | bytes 3932164
  82.7 39.1 %all-to-all-start.2 = ((bf16[128,8,640]{2,0,1:T(8,128)(2,1)}), bf16[128,8,640]{2,0,1:T(8,128)(2,1)}, u32[]{:S(2)}, u32[]{:S(2)}) async-start(bf16[128,8,640]{2,0,1:T(8,128)(2,1)} %bitcast.236), calls=%async_computation.2 | async-start | bytes 2621440 | tf_op jit(solution)/shard_map/all_to_all | solution.py:52
  121.8 38.3 %all-to-all-start.3 = ((bf16[128,8,640]{2,0,1:T(8,128)(2,1)}), bf16[128,8,640]{2,0,1:T(8,128)(2,1)S(1)}, u32[]{:S(2)}, u32[]{:S(2)}) async-start(bf16[128,8,640]{2,0,1:T(8,128)(2,1)} %bitcast.233), calls=%async_computation.3 | async-start | bytes 2621440 | tf_op jit(solution)/shard_map/all_to_all | solution.py:53
  125.4 7.8 %copy-start.6 = (s32[256]{0:T(256)S(1)}, s32[256]{0:T(256)}, u32[]{:S(2)}) copy-start(s32[256]{0:T(256)} %param.11) | copy-start | bytes 3076
  128.8 4.9 %collective-permute-start = (bf16[2,512,640]{2,1,0:T(8,128)(2,1)}, bf16[2,512,640]{2,1,0:T(8,128)(2,1)}, u32[]{:S(2)}, u32[]{:S(2)}) collective-permute-start(bf16[2,512,640]{2,1,0:T(8,128)(2,1)} %get-tuple-element.258), channel_id=1, source_target_pairs={{0,8},{8,16},{16,24},{24,32},{32,40},{40,48},{48,56},{56,64},{64,7... | collective-permute-start | bytes 3932168 | tf_op jit(solution)/shard_map/ppermute | solution.py:20
  131.9 5.3 %collective-permute-start.1 = (bf16[2,512,640]{2,1,0:T(8,128)(2,1)}, bf16[2,512,640]{2,1,0:T(8,128)(2,1)}, u32[]{:S(2)}, u32[]{:S(2)}) collective-permute-start(bf16[2,512,640]{2,1,0:T(8,128)(2,1)} %get-tuple-element.259), channel_id=1, source_target_pairs={{8,0},{16,8},{24,16},{32,24},{40,32},{48,40},{56,48},{64,56},{72,6... | collective-permute-start | bytes 3932168 | tf_op jit(solution)/shard_map/ppermute | solution.py:22
  174.1 2.5 copy-start
  194.8 2.5 copy-start
  215.6 2.5 copy-start
  236.5 2.5 copy-start
  257.3 2.5 copy-start
  273.1 38.6 %all-to-all-start.4 = ((bf16[8,128,640]{2,1,0:T(8,128)(2,1)}), bf16[8,128,640]{2,1,0:T(8,128)(2,1)S(1)}, u32[]{:S(2)}, u32[]{:S(2)}) async-start(bf16[8,128,640]{2,1,0:T(8,128)(2,1)} %bitcast.234), calls=%async_computation.4 | async-start | bytes 2621440 | tf_op jit(solution)/shard_map/all_to_all | solution.py:219
  276.7 39.5 %collective-permute-start.2 = (f32[2,512,640]{2,1,0:T(8,128)}, f32[2,512,640]{2,1,0:T(8,128)}, u32[]{:S(2)}, u32[]{:S(2)}) collective-permute-start(f32[2,512,640]{2,1,0:T(8,128)} %get-tuple-element.196), channel_id=1, source_target_pairs={{0,8},{8,16},{16,24},{24,32},{32,40},{40,48},{48,56},{56,64},{64,7... | collective-permute-start | bytes 7864328 | tf_op jit(solution)/shard_map/ppermute | solution.py:32
  280.3 37.8 %collective-permute-start.3 = (f32[2,512,640]{2,1,0:T(8,128)}, f32[2,512,640]{2,1,0:T(8,128)}, u32[]{:S(2)}, u32[]{:S(2)}) collective-permute-start(f32[2,512,640]{2,1,0:T(8,128)} %get-tuple-element.197), channel_id=1, source_target_pairs={{8,0},{16,8},{24,16},{32,24},{40,32},{48,40},{56,48},{64,56},{72,6... | collective-permute-start | bytes 7864328 | tf_op jit(solution)/shard_map/ppermute | solution.py:32
  311.7 39.2 %all-to-all-start.5 = ((bf16[8,128,640]{2,1,0:T(8,128)(2,1)}), bf16[8,128,640]{2,1,0:T(8,128)(2,1)}, u32[]{:S(2)}, u32[]{:S(2)}) async-start(bf16[8,128,640]{2,1,0:T(8,128)(2,1)} %bitcast.24), calls=%async_computation.5 | async-start | bytes 2621440 | tf_op jit(solution)/shard_map/all_to_all | solution.py:220
  318.1 2.5 copy-start.2
  318.1 3.3 copy-start.3
  387.4 35.1 %all-to-all-start.7 = ((bf16[8,128,640]{2,1,0:T(8,128)(2,1)}), bf16[8,128,640]{2,1,0:T(8,128)(2,1)S(1)}, u32[]{:S(2)}, u32[]{:S(2)}) async-start(bf16[8,128,640]{2,1,0:T(8,128)(2,1)} %bitcast.32), calls=%async_computation.7 | async-start | bytes 2621440 | tf_op jit(solution)/shard_map/all_to_all | solution.py:222
  394.9 4.9 %copy-start.4 = (bf16[8,128,640]{2,1,0:T(8,128)(2,1)S(1)}, bf16[8,128,640]{2,1,0:T(8,128)(2,1)}, u32[]{:S(2)}) copy-start(bf16[8,128,640]{2,1,0:T(8,128)(2,1)} %all_to_all.146) | copy-start | bytes 3932164
where the time goes:
time: 429 us; the launch traced here: 425 us
  waiting for transfers between devices  196 us (46%)
  matrix products  77.3 us (18%)
  local copies, waits for them, and re-layouts  43.5 us (10%)
  starting transfers between devices  39.1 us (9%)
  blocking collectives  36.6 us (9%)
  other arithmetic  30.5 us (7%)
    all_to_all x1, blocking collectives, shards(): lax.all_to_all(key_final, 'uly', split_axis=0, concat_axis=1, tiled=True)  36.6 us
    all_to_all x1, waiting for transfers between devices, shards(): lax.all_to_all(queries, 'uly', split_axis=1, concat_axis=0, tiled=True)  33.2 us
    all_to_all x1, waiting for transfers between devices, shards(): lax.all_to_all(values, 'uly', split_axis=1, concat_axis=0, tiled=True)  32.3 us
    all_to_all x1, waiting for transfers between devices, shards(): lax.all_to_all(keys, 'uly', split_axis=1, concat_axis=0, tiled=True)  32.2 us
    all_to_all x1, waiting for transfers between devices, shards(): lax.all_to_all(out_all, 'uly', split_axis=0, concat_axis=1, tiled=True)  30.1 us
    all_to_all x1, waiting for transfers between devices, shards(): lax.all_to_all(grad_query, 'uly', split_axis=0, concat_axis=1, tiled=True)  27.9 us
    dot_general x30, matrix products, masked_scores(): jnp.dot(query_rows, key_rows.T, preferred_element_type=jnp.float32) * factor  27.8 us
    all_to_all x1, waiting for transfers between devices, shards(): lax.all_to_all(value_final, 'uly', split_axis=0, concat_axis=1, tiled=True)  18.8 us
  transfers between devices with their start and end apart: 11, of which 9 were waited for; matrix products, arithmetic and copies ran while one was open for 8% of the time, Pallas kernels for 0%

commit v1 on v0

v1 whole, which is shorter than its diff:
```python
from functools import partial

import jax
import jax.numpy as jnp
from jax import lax
from jax.experimental import pallas as pl
from jax.experimental.pallas import tpu as pltpu
from jax.sharding import PartitionSpec as P

HD = 128
TILE = 128
MOST = 4
AXES = ("seq", "uly")
CHUNKS = (2, 2, 2, 2, 2)
ORDER = (1, 2, 3)


def turns(step, tiles):
    def tile_at(window, place):
        return (MOST * window + place - MOST // 2) % tiles

    return [
        (tile_at(window, place), tile_at(window, (place + step) % MOST))
        for window in range(tiles // MOST)
        for place in range(MOST)
    ]


def place_at(step):
    return (lax.axis_index("uly") + MOST // 2 + step) % MOST


def pack_kernel(begin, heads_each, width, q_ref, k_ref, v_ref, g_ref, *rest):
    outs, sems = rest[-4:-1], rest[-1]
    copies = []
    for step in range(1, MOST):
        column = pl.multiple_of((place_at(step) * heads_each + begin) * HD, HD)
        for member, source in enumerate((q_ref, k_ref, v_ref, g_ref)):
            copies.append(
                pltpu.make_async_copy(
                    source.at[:, pl.ds(column, width)],
                    outs[step - 1].at[member],
                    sems.at[step - 1, member],
                )
            )
    for copy in copies:
        copy.start()
    for copy in copies:
        copy.wait()


def pack(arrays, after, begin, heads, heads_each):
    width = heads * HD
    piece = jax.ShapeDtypeStruct((4, TILE, width), jnp.bfloat16)
    return pl.pallas_call(
        partial(pack_kernel, begin, heads_each, width),
        out_shape=(piece,) * 3,
        in_specs=[pl.BlockSpec(memory_space=pl.ANY)] * (4 + len(after)),
        out_specs=(pl.BlockSpec(memory_space=pltpu.VMEM),) * 3,
        scratch_shapes=[pltpu.SemaphoreType.DMA((3, 4))],
        cost_estimate=pl.CostEstimate(flops=0, bytes_accessed=24 * TILE * width * 2, transcendentals=0),
        name="pack",
    )(*arrays, *after)


def unpack_kernel(begin, heads_each, width, *rest):
    pieces = rest[:4]
    outs, sems = rest[-5:-1], rest[-1]
    copies = []
    for step in range(MOST):
        column = pl.multiple_of((place_at(step) * heads_each + begin) * HD, HD)
        for member, target in enumerate(outs):
            copies.append(
                pltpu.make_async_copy(
                    pieces[step].at[member],
                    target.at[:, pl.ds(column, width)],
                    sems.at[step, member],
                )
            )
    for copy in copies:
        copy.start()
    for copy in copies:
        copy.wait()


def unpack(pieces, held, begin, heads, heads_each, columns):
    width = heads * HD
    whole = jax.ShapeDtypeStruct((TILE, columns), jnp.bfloat16)
    held = () if held is None else tuple(held)
    return pl.pallas_call(
        partial(unpack_kernel, begin, heads_each, width),
        out_shape=(whole,) * 4,
        in_specs=[pl.BlockSpec(memory_space=pltpu.VMEM)] * 4
        + [pl.BlockSpec(memory_space=pl.ANY)] * len(held),
        out_specs=(pl.BlockSpec(memory_space=pl.ANY),) * 4,
        scratch_shapes=[pltpu.SemaphoreType.DMA((4, 4))],
        input_output_aliases={4 + i: i for i in range(len(held))},
        cost_estimate=pl.CostEstimate(flops=0, bytes_accessed=32 * TILE * width * 2, transcendentals=0),
        name="unpack",
    )(*pieces, *held)


def matmul(left, right, left_dim, right_dim):
    return lax.dot_general(
        left, right, (((left_dim,), (right_dim,)), ((), ())), preferred_element_type=jnp.float32
    )


def attend_kernel(info, q_ref, k_ref, v_ref, g_ref, one, two, three, *rest):
    outs = rest[-4:]
    factor = HD ** -0.5
    rows = MOST * TILE

    def gather(own, member):
        return jnp.concatenate((own[...], one[member], two[member], three[member]), axis=0)

    q, k, v, g = (gather(own, i) for i, own in enumerate((q_ref, k_ref, v_ref, g_ref)))
    place = lax.broadcasted_iota(jnp.int32, (1, rows), 1) // TILE
    key_first = jnp.where(
        place < 2,
        jnp.where(place == 0, info[1], info[2]),
        jnp.where(place == 2, info[3], info[4]),
    )
    weights_all = []
    dscores_all = []
    for tile in range(MOST):
        part = slice(tile * TILE, (tile + 1) * TILE)
        query_rows, grad_rows = q[part], g[part]
        scores = matmul(query_rows, k, 1, 1) * factor
        scores = jnp.where(key_first == info[1 + tile], scores, -jnp.inf)
        row_max = jnp.max(scores, axis=1, keepdims=True)
        raised = jnp.exp(scores - row_max)
        weights = raised * (1.0 / jnp.sum(raised, axis=1, keepdims=True))
        half = weights.astype(jnp.bfloat16)
        attended = matmul(half, v, 1, 0).astype(jnp.bfloat16)
        delta = jnp.sum(
            grad_rows.astype(jnp.float32) * attended.astype(jnp.float32), axis=1, keepdims=True
        )
        dweights = matmul(grad_rows, v, 1, 1)
        dscores = (weights * (dweights - delta)).astype(jnp.bfloat16)
        outs[tile][0] = attended
        outs[tile][1] = (matmul(dscores, k, 1, 0) * factor).astype(jnp.bfloat16)
        weights_all.append(half)
        dscores_all.append(dscores)
    key_grad = (matmul(jnp.concatenate(dscores_all, axis=0), q, 0, 0) * factor).astype(jnp.bfloat16)
    value_grad = matmul(jnp.concatenate(weights_all, axis=0), g, 0, 0).astype(jnp.bfloat16)
    for tile in range(MOST):
        part = slice(tile * TILE, (tile + 1) * TILE)
        outs[tile][2] = key_grad[part]
        outs[tile][3] = value_grad[part]


def attend(info, arrays, received, after, begin, heads, heads_each):
    width = heads * HD
    piece = jax.ShapeDtypeStruct((4, TILE, width), jnp.bfloat16)
    own_spec = pl.BlockSpec((TILE, HD), lambda h, info: (0, info[0] * heads_each + begin + h))
    piece_spec = pl.BlockSpec((4, TILE, HD), lambda h, info: (0, 0, h))
    rows = MOST * TILE
    return pl.pallas_call(
        attend_kernel,
        out_shape=(piece,) * 4,
        grid_spec=pltpu.PrefetchScalarGridSpec(
            num_scalar_prefetch=1,
            grid=(heads,),
            in_specs=[own_spec] * 4
            + [piece_spec] * 3
            + [pl.BlockSpec(memory_space=pl.ANY)] * len(after),
            out_specs=(piece_spec,) * 4,
        ),
        cost_estimate=pl.CostEstimate(
            flops=12 * rows * rows * HD * heads,
            bytes_accessed=16 * rows * HD * heads,
            transcendentals=rows * rows * heads,
        ),
        name="attend",
    )(info, *arrays, *received, *after)


def shards(queries, keys, values, out_grad, tile_offset):
    arrays = (queries, keys, values, out_grad)
    columns = queries.shape[1]
    heads_each = columns // HD // MOST
    tiles = tile_offset.shape[0]
    device = lax.axis_index(AXES)
    place = (device + MOST // 2) % MOST
    places = (place - jnp.arange(MOST)) % MOST
    members = (device - place + places + tiles) % tiles
    firsts = members - tile_offset[members]
    info = jnp.concatenate((place[None], firsts)).astype(jnp.int32)

    def exchange(pieces, sign):
        done = {}
        for step in ORDER:
            done[step] = lax.ppermute(pieces[step - 1], AXES, turns(sign * step, tiles))
        return tuple(done[step] for step in (1, 2, 3))

    begins = [sum(CHUNKS[:i]) for i in range(len(CHUNKS))]
    received, after = [], ()
    for begin, heads in zip(begins, CHUNKS):
        pieces = pack(arrays, after, begin, heads, heads_each)
        after = pieces[:1]
        received.append(exchange(pieces, 1))
    results, after = [], ()
    for begin, heads, pieces in zip(begins, CHUNKS, received):
        own, *others = attend(info, arrays, pieces, after, begin, heads, heads_each)
        after = (own,)
        results.append((own, exchange(others, -1)))
    held = None
    for begin, heads, (own, others) in zip(begins, CHUNKS, results):
        held = unpack((own, *others), held, begin, heads, heads_each, columns)
    return tuple(held)


def solution(mesh):
    spec = P(AXES, None)
    return jax.shard_map(
        shards,
        mesh=mesh,
        in_specs=(spec, spec, spec, spec, P()),
        out_specs=(spec, spec, spec, spec),
        check_vma=False,
    )
```

time: 429 us -> 241 us (0.56)
  waiting for transfers between devices: 196 us -> 43.4 us
  starting transfers between devices: 39.1 us -> 130 us
  matrix products: 77.3 us -> 0 us
  Pallas kernels: 0 us -> 62.6 us
  local copies, waits for them, and re-layouts: 43.5 us -> 2.94 us
  blocking collectives: 36.6 us -> 0 us
  other arithmetic: 30.5 us -> 0.65 us
    all_to_all x7 -> x0, waiting for transfers between devices: 192 us -> none  [the longest x1 33.2 us: shards(): lax.all_to_all(queries, 'uly', split_axis=1, concat_axis=0, tiled=True)]
    ppermute x4 -> x30, starting transfers between devices: 9.33 us -> 130 us  [exchange(): done[step] = lax.ppermute(pieces[step - 1], AXES, turns(sign * step, tiles))]
    dot_general x180 -> x0, matrix products: 77.3 us -> none  [the longest x30 27.8 us: masked_scores(): jnp.dot(query_rows, key_rows.T, preferred_element_type=jnp.float32) * factor]
    pallas_call x0 -> x15, Pallas kernels: none -> 62.6 us  [the longest x5 40.3 us: attend(): pl.pallas_call(attend_kernel, out_shape=(piece,) * 4, grid_spec=pltpu.Pre...]
    ppermute x4 -> x30, waiting for transfers between devices: 3.74 us -> 43.4 us  [exchange(): done[step] = lax.ppermute(pieces[step - 1], AXES, turns(sign * step, tiles))]
    all_to_all x1 -> x0, blocking collectives: 36.6 us -> none  [shards(): lax.all_to_all(key_final, 'uly', split_axis=0, concat_axis=1, tiled=True)]
    all_to_all x7 -> x0, starting transfers between devices: 29.8 us -> none  [the longest x1 6.73 us: shards(): lax.all_to_all(queries, 'uly', split_axis=1, concat_axis=0, tiled=True)]
    dynamic_update_slice x15 -> x0, other arithmetic: 15.7 us -> none  [the longest x5 5.82 us: one_head(): lax.dynamic_update_slice(key_own, jnp.concatenate((key_sums[1], key_sums[...]
  transfers between devices with their start and end apart: 11 -> 30, of which waited for: 9 -> 12; matrix products, arithmetic and copies ran while one was open for 8% -> 1% of each run, Pallas kernels for 0% -> 24%
where the time goes in v1:
time: 241 us
  starting transfers between devices  130 us (54%)
  Pallas kernels  62.6 us (26%)
  waiting for transfers between devices  43.4 us (18%)
  local copies, waits for them, and re-layouts  2.94 us (1%)
    ppermute x30, starting transfers between devices, exchange(): done[step] = lax.ppermute(pieces[step - 1], AXES, turns(sign * step, tiles))  130 us
    ppermute x30, waiting for transfers between devices, exchange(): done[step] = lax.ppermute(pieces[step - 1], AXES, turns(sign * step, tiles))  43.4 us
    pallas_call x5, Pallas kernels, attend(): pl.pallas_call(attend_kernel, out_shape=(piece,) * 4, grid_spec=pltpu.Pre...  40.3 us
    pallas_call x5, Pallas kernels, unpack(): pl.pallas_call(partial(unpack_kernel, begin, heads_each, width), out_shap...  11.4 us
    pallas_call x5, Pallas kernels, pack(): pl.pallas_call(partial(pack_kernel, begin, heads_each, width), out_shape=...  10.9 us
  transfers between devices with their start and end apart: 30, of which 12 were waited for; matrix products, arithmetic and copies ran while one was open for 1% of the time, Pallas kernels for 24%

profile of v1, /device:TPU:0, one launch (start us, length us, event | category | flops | bytes accessed | tf_op | source)
XLA Modules:
  0.0 240.6 jit_solution(2398222697483225366)
XLA Ops:
  0.6 0.0 copy-start
  0.6 2.2 pack.5
  2.8 0.3 collective-permute-start.12
  3.1 9.2 %collective-permute-start.13 = (bf16[4,128,256]{2,1,0:T(8,128)(2,1)}, bf16[4,128,256]{2,1,0:T(8,128)(2,1)S(1)}, u32[]{:S(2)}, u32[]{:S(2)}) collective-permute-start(bf16[4,128,256]{2,1,0:T(8,128)(2,1)} %get-tuple-element.68), channel_id=1, source_target_pairs={{254,0},{255,1},{0,254},{1,255},{2,4},{3,5},{4,2},{5,3},{6,8},{7,9... | collective-permute-start | bytes 786440 | tf_op jit(solution)/shard_map/ppermute | solution.py:194
  12.3 7.3 %collective-permute-start.14 = (bf16[4,128,256]{2,1,0:T(8,128)(2,1)}, bf16[4,128,256]{2,1,0:T(8,128)(2,1)S(1)}, u32[]{:S(2)}, u32[]{:S(2)}) collective-permute-start(bf16[4,128,256]{2,1,0:T(8,128)(2,1)} %get-tuple-element.69), channel_id=1, source_target_pairs={{254,1},{255,254},{0,255},{1,0},{2,5},{3,2},{4,3},{5,4},{6,9},{7,6... | collective-permute-start | bytes 786440 | tf_op jit(solution)/shard_map/ppermute | solution.py:194
  19.6 2.2 pack.6
  21.8 0.1 collective-permute-start.9
  21.9 1.2 collective-permute-start.10
  23.1 2.2 pack.7
  25.3 2.2 pack.8
  27.6 0.0 collective-permute-done.12.one
  27.6 7.5 %collective-permute-start.6 = (bf16[4,128,256]{2,1,0:T(8,128)(2,1)S(1)}, bf16[4,128,256]{2,1,0:T(8,128)(2,1)S(1)}, u32[]{:S(2)}, u32[]{:S(2)}) collective-permute-start(bf16[4,128,256]{2,1,0:T(8,128)(2,1)S(1)} %copy-done.31), channel_id=1, source_target_pairs={{254,255},{255,0},{0,1},{1,254},{2,3},{3,4},{4,5},{5,2},{6,7},{7,8... | collective-permute-start | bytes 786440 | tf_op jit(solution)/shard_map/ppermute | solution.py:194
  35.1 1.4 collective-permute-start.11
  36.6 12.1 %collective-permute-done.14.three = bf16[4,128,256]{2,1,0:T(8,128)(2,1)S(1)} collective-permute-done((bf16[4,128,256]{2,1,0:T(8,128)(2,1)}, bf16[4,128,256]{2,1,0:T(8,128)(2,1)S(1)}, u32[]{:S(2)}, u32[]{:S(2)}) %collective-permute-start.14) | collective-permute-done | bytes 262176 | tf_op jit(solution)/shard_map/ppermute | solution.py:194
  48.6 1.3 collective-permute-start.7
  49.9 6.0 %collective-permute-start.8 = (bf16[4,128,256]{2,1,0:T(8,128)(2,1)S(1)}, bf16[4,128,256]{2,1,0:T(8,128)(2,1)S(1)}, u32[]{:S(2)}, u32[]{:S(2)}) collective-permute-start(bf16[4,128,256]{2,1,0:T(8,128)(2,1)S(1)} %copy-done.35), channel_id=1, source_target_pairs={{254,1},{255,254},{0,255},{1,0},{2,5},{3,2},{4,3},{5,4},{6,9},{7,6... | collective-permute-start | bytes 786440 | tf_op jit(solution)/shard_map/ppermute | solution.py:194
  56.0 1.0 collective-permute-done.10.two
  57.0 14.6 %collective-permute-start.3 = (bf16[4,128,256]{2,1,0:T(8,128)(2,1)}, bf16[4,128,256]{2,1,0:T(8,128)(2,1)S(1)}, u32[]{:S(2)}, u32[]{:S(2)}) collective-permute-start(bf16[4,128,256]{2,1,0:T(8,128)(2,1)} %get-tuple-element.58.rest_0_), channel_id=1, source_target_pairs={{254,255},{255,0},{0,1},{1,254},{2,3},{3,4},{4,5},{5,2},{6,7},{7,8... | collective-permute-start | bytes 786440 | tf_op jit(solution)/shard_map/ppermute | solution.py:194
  71.6 2.2 pack.9
  73.9 0.6 gather_fusion
  74.6 0.0 collective-permute-done.11.three
  74.6 0.1 collective-permute-start.4
  74.7 1.1 collective-permute-done.6.one
  75.8 5.7 %collective-permute-start.5 = (bf16[4,128,256]{2,1,0:T(8,128)(2,1)S(1)}, bf16[4,128,256]{2,1,0:T(8,128)(2,1)S(1)}, u32[]{:S(2)}, u32[]{:S(2)}) collective-permute-start(bf16[4,128,256]{2,1,0:T(8,128)(2,1)S(1)} %copy-done.33), channel_id=1, source_target_pairs={{254,1},{255,254},{0,255},{1,0},{2,5},{3,2},{4,3},{5,4},{6,9},{7,6... | collective-permute-start | bytes 786440 | tf_op jit(solution)/shard_map/ppermute | solution.py:194
  81.5 12.6 %collective-permute-start = (bf16[4,128,256]{2,1,0:T(8,128)(2,1)}, bf16[4,128,256]{2,1,0:T(8,128)(2,1)S(1)}, u32[]{:S(2)}, u32[]{:S(2)}) collective-permute-start(bf16[4,128,256]{2,1,0:T(8,128)(2,1)} %get-tuple-element.59), channel_id=1, source_target_pairs={{254,255},{255,0},{0,1},{1,254},{2,3},{3,4},{4,5},{5,2},{6,7},{7,8... | collective-permute-start | bytes 786440 | tf_op jit(solution)/shard_map/ppermute | solution.py:194
  94.1 4.2 %collective-permute-done.3.one = bf16[4,128,256]{2,1,0:T(8,128)(2,1)S(1)} collective-permute-done((bf16[4,128,256]{2,1,0:T(8,128)(2,1)}, bf16[4,128,256]{2,1,0:T(8,128)(2,1)S(1)}, u32[]{:S(2)}, u32[]{:S(2)}) %collective-permute-start.3) | collective-permute-done | bytes 262176 | tf_op jit(solution)/shard_map/ppermute | solution.py:194
  98.3 2.5 %collective-permute-start.2 = (bf16[4,128,256]{2,1,0:T(8,128)(2,1)}, bf16[4,128,256]{2,1,0:T(8,128)(2,1)S(1)}, u32[]{:S(2)}, u32[]{:S(2)}) collective-permute-start(bf16[4,128,256]{2,1,0:T(8,128)(2,1)} %get-tuple-element.61), channel_id=1, source_target_pairs={{254,1},{255,254},{0,255},{1,0},{2,5},{3,2},{4,3},{5,4},{6,9},{7,6... | collective-permute-start | bytes 786440 | tf_op jit(solution)/shard_map/ppermute | solution.py:194
  100.8 0.6 pad_add_fusion.info
  101.4 7.9 %attend.5 = (bf16[4,128,256]{2,1,0:T(8,128)(2,1)}, bf16[4,128,256]{2,1,0:T(8,128)(2,1)}, bf16[4,128,256]{2,1,0:T(8,128)(2,1)}, bf16[4,128,256]{2,1,0:T(8,128)(2,1)}) custom-call(s32[5]{0:T(128)} %pad_add_fusion.info, bf16[128,5120]{1,0:T(8,128)(2,1)} %q_ref.19, bf16[128,5120]{1,0:T(8,128)(2,1)} %k_ref.19, bf16[128,5120]{1,0:T(8,128)(2,1)} %v_ref.19, ...), custom_call_target="tpu_custom_call" | custom-call | flops 805306368 | bytes 2097152 | tf_op jit(solution)/shard_map/attend/pallas_call | solution.py:159
  109.4 8.1 %attend.6 = (bf16[4,128,256]{2,1,0:T(8,128)(2,1)}, bf16[4,128,256]{2,1,0:T(8,128)(2,1)}, bf16[4,128,256]{2,1,0:T(8,128)(2,1)}, bf16[4,128,256]{2,1,0:T(8,128)(2,1)}) custom-call(s32[5]{0:T(128)} %pad_add_fusion.info, bf16[128,5120]{1,0:T(8,128)(2,1)} %q_ref.19, bf16[128,5120]{1,0:T(8,128)(2,1)} %k_ref.19, bf16[128,5120]{1,0:T(8,128)(2,1)} %v_ref.19, ...), custom_call_target="tpu_custom_call" | custom-call | flops 805306368 | bytes 2097152 | tf_op jit(solution)/shard_map/attend/pallas_call | solution.py:159
  117.6 1.7 collective-permute-start.27
  119.3 5.5 %collective-permute-start.28 = (bf16[4,128,256]{2,1,0:T(8,128)(2,1)S(1)}, bf16[4,128,256]{2,1,0:T(8,128)(2,1)S(1)}, u32[]{:S(2)}, u32[]{:S(2)}) collective-permute-start(bf16[4,128,256]{2,1,0:T(8,128)(2,1)S(1)} %copy-done.38), channel_id=1, source_target_pairs={{254,0},{255,1},{0,254},{1,255},{2,4},{3,5},{4,2},{5,3},{6,8},{7,9... | collective-permute-start | bytes 786440 | tf_op jit(solution)/shard_map/ppermute | solution.py:194
  124.8 1.9 collective-permute-done.one
  126.7 0.0 copy-start.9
  126.7 10.3 %collective-permute-start.24 = (bf16[4,128,256]{2,1,0:T(8,128)(2,1)}, bf16[4,128,256]{2,1,0:T(8,128)(2,1)S(1)}, u32[]{:S(2)}, u32[]{:S(2)}) collective-permute-start(bf16[4,128,256]{2,1,0:T(8,128)(2,1)} %get-tuple-element.84), channel_id=1, source_target_pairs={{254,1},{255,254},{0,255},{1,0},{2,5},{3,2},{4,3},{5,4},{6,9},{7,6... | collective-permute-start | bytes 786440 | tf_op jit(solution)/shard_map/ppermute | solution.py:194
  137.0 9.6 %collective-permute-start.25 = (bf16[4,128,256]{2,1,0:T(8,128)(2,1)}, bf16[4,128,256]{2,1,0:T(8,128)(2,1)S(1)}, u32[]{:S(2)}, u32[]{:S(2)}) collective-permute-start(bf16[4,128,256]{2,1,0:T(8,128)(2,1)} %get-tuple-element.85), channel_id=1, source_target_pairs={{254,0},{255,1},{0,254},{1,255},{2,4},{3,5},{4,2},{5,3},{6,8},{7,9... | collective-permute-start | bytes 786440 | tf_op jit(solution)/shard_map/ppermute | solution.py:194
  146.6 8.0 %attend.7 = (bf16[4,128,256]{2,1,0:T(8,128)(2,1)}, bf16[4,128,256]{2,1,0:T(8,128)(2,1)}, bf16[4,128,256]{2,1,0:T(8,128)(2,1)}, bf16[4,128,256]{2,1,0:T(8,128)(2,1)}) custom-call(s32[5]{0:T(128)} %pad_add_fusion.info, bf16[128,5120]{1,0:T(8,128)(2,1)} %q_ref.19, bf16[128,5120]{1,0:T(8,128)(2,1)} %k_ref.19, bf16[128,5120]{1,0:T(8,128)(2,1)} %v_ref.19, ...), custom_call_target="tpu_custom_call" | custom-call | flops 805306368 | bytes 2097152 | tf_op jit(solution)/shard_map/attend/pallas_call | solution.py:159
  154.6 8.1 %attend.8 = (bf16[4,128,256]{2,1,0:T(8,128)(2,1)}, bf16[4,128,256]{2,1,0:T(8,128)(2,1)}, bf16[4,128,256]{2,1,0:T(8,128)(2,1)}, bf16[4,128,256]{2,1,0:T(8,128)(2,1)}) custom-call(s32[5]{0:T(128)} %pad_add_fusion.info, bf16[128,5120]{1,0:T(8,128)(2,1)} %q_ref.19, bf16[128,5120]{1,0:T(8,128)(2,1)} %k_ref.19, bf16[128,5120]{1,0:T(8,128)(2,1)} %v_ref.19, ...), custom_call_target="tpu_custom_call" | custom-call | flops 805306368 | bytes 2097152 | tf_op jit(solution)/shard_map/attend/pallas_call | solution.py:159
  162.8 0.1 collective-permute-start.26
  162.9 7.1 %collective-permute-start.21 = (bf16[4,128,256]{2,1,0:T(8,128)(2,1)}, bf16[4,128,256]{2,1,0:T(8,128)(2,1)S(1)}, u32[]{:S(2)}, u32[]{:S(2)}) collective-permute-start(bf16[4,128,256]{2,1,0:T(8,128)(2,1)} %get-tuple-element.81), channel_id=1, source_target_pairs={{254,1},{255,254},{0,255},{1,0},{2,5},{3,2},{4,3},{5,4},{6,9},{7,6... | collective-permute-start | bytes 786440 | tf_op jit(solution)/shard_map/ppermute | solution.py:194
  170.0 0.7 copy-done.30
  170.8 1.8 collective-permute-start.22
  172.6 0.1 collective-permute-start.23
  172.7 7.1 %collective-permute-start.18 = (bf16[4,128,256]{2,1,0:T(8,128)(2,1)}, bf16[4,128,256]{2,1,0:T(8,128)(2,1)S(1)}, u32[]{:S(2)}, u32[]{:S(2)}) collective-permute-start(bf16[4,128,256]{2,1,0:T(8,128)(2,1)} %get-tuple-element.78), channel_id=1, source_target_pairs={{254,1},{255,254},{0,255},{1,0},{2,5},{3,2},{4,3},{5,4},{6,9},{7,6... | collective-permute-start | bytes 786440 | tf_op jit(solution)/shard_map/ppermute | solution.py:194
  179.8 8.1 %attend.9 = (bf16[4,128,256]{2,1,0:T(8,128)(2,1)}, bf16[4,128,256]{2,1,0:T(8,128)(2,1)}, bf16[4,128,256]{2,1,0:T(8,128)(2,1)}, bf16[4,128,256]{2,1,0:T(8,128)(2,1)}) custom-call(s32[5]{0:T(128)} %pad_add_fusion.info, bf16[128,5120]{1,0:T(8,128)(2,1)} %q_ref.19, bf16[128,5120]{1,0:T(8,128)(2,1)} %k_ref.19, bf16[128,5120]{1,0:T(8,128)(2,1)} %v_ref.19, ...), custom_call_target="tpu_custom_call" | custom-call | flops 805306368 | bytes 2097152 | tf_op jit(solution)/shard_map/attend/pallas_call | solution.py:159
  188.0 8.2 %collective-permute-start.19 = (bf16[4,128,256]{2,1,0:T(8,128)(2,1)}, bf16[4,128,256]{2,1,0:T(8,128)(2,1)S(1)}, u32[]{:S(2)}, u32[]{:S(2)}) collective-permute-start(bf16[4,128,256]{2,1,0:T(8,128)(2,1)} %get-tuple-element.79), channel_id=1, source_target_pairs={{254,0},{255,1},{0,254},{1,255},{2,4},{3,5},{4,2},{5,3},{6,8},{7,9... | collective-permute-start | bytes 786440 | tf_op jit(solution)/shard_map/ppermute | solution.py:194
  196.2 0.1 collective-permute-start.20
  196.3 1.5 collective-permute-done.22.rest_2_
  197.8 5.7 %collective-permute-start.15 = (bf16[4,128,256]{2,1,0:T(8,128)(2,1)}, bf16[4,128,256]{2,1,0:T(8,128)(2,1)S(1)}, u32[]{:S(2)}, u32[]{:S(2)}) collective-permute-start(bf16[4,128,256]{2,1,0:T(8,128)(2,1)} %get-tuple-element.75), channel_id=1, source_target_pairs={{254,1},{255,254},{0,255},{1,0},{2,5},{3,2},{4,3},{5,4},{6,9},{7,6... | collective-permute-start | bytes 786440 | tf_op jit(solution)/shard_map/ppermute | solution.py:194
  203.4 1.0 collective-permute-done.23.rest_3_
  204.4 1.6 collective-permute-start.16
  206.0 0.8 collective-permute-done.18.rest_1_
  206.8 0.8 collective-permute-start.17
  207.7 2.3 unpack.5
  210.0 2.3 unpack.6
  212.3 2.3 unpack.7
  214.6 8.5 %collective-permute-done.19.rest_2_ = bf16[4,128,256]{2,1,0:T(8,128)(2,1)S(1)} collective-permute-done((bf16[4,128,256]{2,1,0:T(8,128)(2,1)}, bf16[4,128,256]{2,1,0:T(8,128)(2,1)S(1)}, u32[]{:S(2)}, u32[]{:S(2)}) %collective-permute-start.19) | collective-permute-done | bytes 262176 | tf_op jit(solution)/shard_map/ppermute | solution.py:194
  223.0 3.9 %collective-permute-done.20.rest_3_ = bf16[4,128,256]{2,1,0:T(8,128)(2,1)S(1)} collective-permute-done((bf16[4,128,256]{2,1,0:T(8,128)(2,1)S(1)}, bf16[4,128,256]{2,1,0:T(8,128)(2,1)S(1)}, u32[]{:S(2)}, u32[]{:S(2)}) %collective-permute-start.20) | collective-permute-done | bytes 262176 | tf_op jit(solution)/shard_map/ppermute | solution.py:194
  226.9 0.7 copy-done.27
  227.6 2.3 unpack.8
  229.9 4.3 %collective-permute-done.16.rest_2_ = bf16[4,128,256]{2,1,0:T(8,128)(2,1)S(1)} collective-permute-done((bf16[4,128,256]{2,1,0:T(8,128)(2,1)}, bf16[4,128,256]{2,1,0:T(8,128)(2,1)S(1)}, u32[]{:S(2)}, u32[]{:S(2)}) %collective-permute-start.16) | collective-permute-done | bytes 262176 | tf_op jit(solution)/shard_map/ppermute | solution.py:194
  234.2 3.2 %collective-permute-done.17.rest_3_ = bf16[4,128,256]{2,1,0:T(8,128)(2,1)S(1)} collective-permute-done((bf16[4,128,256]{2,1,0:T(8,128)(2,1)}, bf16[4,128,256]{2,1,0:T(8,128)(2,1)S(1)}, u32[]{:S(2)}, u32[]{:S(2)}) %collective-permute-start.17) | collective-permute-done | bytes 262176 | tf_op jit(solution)/shard_map/ppermute | solution.py:194
  237.4 0.7 copy-done.26
  238.1 2.3 unpack.9
  (96 shorter events, 0.2 us)
Async XLA Ops:
  0.6 73.3 %copy-start = (s32[256]{0:T(256)S(1)}, s32[256]{0:T(256)}, u32[]{:S(2)}) copy-start(s32[256]{0:T(256)} %param.9) | copy-start | bytes 3076
  2.8 24.7 %collective-permute-start.12 = (bf16[4,128,256]{2,1,0:T(8,128)(2,1)}, bf16[4,128,256]{2,1,0:T(8,128)(2,1)S(1)}, u32[]{:S(2)}, u32[]{:S(2)}) collective-permute-start(bf16[4,128,256]{2,1,0:T(8,128)(2,1)} %get-tuple-element.55.rest_0_), channel_id=1, source_target_pairs={{254,255},{255,0},{0,1},{1,254},{2,3},{3,4},{4,5},{5,2},{6,7},{7,8... | collective-permute-start | bytes 786440 | tf_op jit(solution)/shard_map/ppermute | solution.py:194
  3.1 32.0 %collective-permute-start.13 = (bf16[4,128,256]{2,1,0:T(8,128)(2,1)}, bf16[4,128,256]{2,1,0:T(8,128)(2,1)S(1)}, u32[]{:S(2)}, u32[]{:S(2)}) collective-permute-start(bf16[4,128,256]{2,1,0:T(8,128)(2,1)} %get-tuple-element.68), channel_id=1, source_target_pairs={{254,0},{255,1},{0,254},{1,255},{2,4},{3,5},{4,2},{5,3},{6,8},{7,9... | collective-permute-start | bytes 786440 | tf_op jit(solution)/shard_map/ppermute | solution.py:194
  12.3 36.4 %collective-permute-start.14 = (bf16[4,128,256]{2,1,0:T(8,128)(2,1)}, bf16[4,128,256]{2,1,0:T(8,128)(2,1)S(1)}, u32[]{:S(2)}, u32[]{:S(2)}) collective-permute-start(bf16[4,128,256]{2,1,0:T(8,128)(2,1)} %get-tuple-element.69), channel_id=1, source_target_pairs={{254,1},{255,254},{0,255},{1,0},{2,5},{3,2},{4,3},{5,4},{6,9},{7,6... | collective-permute-start | bytes 786440 | tf_op jit(solution)/shard_map/ppermute | solution.py:194
  21.8 28.1 %collective-permute-start.9 = (bf16[4,128,256]{2,1,0:T(8,128)(2,1)}, bf16[4,128,256]{2,1,0:T(8,128)(2,1)S(1)}, u32[]{:S(2)}, u32[]{:S(2)}) collective-permute-start(bf16[4,128,256]{2,1,0:T(8,128)(2,1)} %get-tuple-element.56.rest_0_), channel_id=1, source_target_pairs={{254,255},{255,0},{0,1},{1,254},{2,3},{3,4},{4,5},{5,2},{6,7},{7,8... | collective-permute-start | bytes 786440 | tf_op jit(solution)/shard_map/ppermute | solution.py:194
  21.9 35.1 %collective-permute-start.10 = (bf16[4,128,256]{2,1,0:T(8,128)(2,1)}, bf16[4,128,256]{2,1,0:T(8,128)(2,1)S(1)}, u32[]{:S(2)}, u32[]{:S(2)}) collective-permute-start(bf16[4,128,256]{2,1,0:T(8,128)(2,1)} %get-tuple-element.66), channel_id=1, source_target_pairs={{254,0},{255,1},{0,254},{1,255},{2,4},{3,5},{4,2},{5,3},{6,8},{7,9... | collective-permute-start | bytes 786440 | tf_op jit(solution)/shard_map/ppermute | solution.py:194
  25.3 24.7 %copy-start.35 = (bf16[4,128,256]{2,1,0:T(8,128)(2,1)S(1)}, bf16[4,128,256]{2,1,0:T(8,128)(2,1)}, u32[]{:S(2)}) copy-start(bf16[4,128,256]{2,1,0:T(8,128)(2,1)} %get-tuple-element.65) | copy-start | bytes 786436
  27.6 46.3 %copy-start.1 = (bf16[4,128,256]{2,1,0:T(8,128)(2,1)}, bf16[4,128,256]{2,1,0:T(8,128)(2,1)S(1)}, u32[]{:S(2)}) copy-start(bf16[4,128,256]{2,1,0:T(8,128)(2,1)S(1)} %collective-permute-done.12.one) | copy-start | bytes 786436
  27.6 48.2 %collective-permute-start.6 = (bf16[4,128,256]{2,1,0:T(8,128)(2,1)S(1)}, bf16[4,128,256]{2,1,0:T(8,128)(2,1)S(1)}, u32[]{:S(2)}, u32[]{:S(2)}) collective-permute-start(bf16[4,128,256]{2,1,0:T(8,128)(2,1)S(1)} %copy-done.31), channel_id=1, source_target_pairs={{254,255},{255,0},{0,1},{1,254},{2,3},{3,4},{4,5},{5,2},{6,7},{7,8... | collective-permute-start | bytes 786440 | tf_op jit(solution)/shard_map/ppermute | solution.py:194
  35.1 38.7 %copy-start.2 = (bf16[4,128,256]{2,1,0:T(8,128)(2,1)}, bf16[4,128,256]{2,1,0:T(8,128)(2,1)S(1)}, u32[]{:S(2)}) copy-start(bf16[4,128,256]{2,1,0:T(8,128)(2,1)S(1)} %collective-permute-done.13.two) | copy-start | bytes 786436
  35.1 39.4 %collective-permute-start.11 = (bf16[4,128,256]{2,1,0:T(8,128)(2,1)}, bf16[4,128,256]{2,1,0:T(8,128)(2,1)S(1)}, u32[]{:S(2)}, u32[]{:S(2)}) collective-permute-start(bf16[4,128,256]{2,1,0:T(8,128)(2,1)} %get-tuple-element.67), channel_id=1, source_target_pairs={{254,1},{255,254},{0,255},{1,0},{2,5},{3,2},{4,3},{5,4},{6,9},{7,6... | collective-permute-start | bytes 786440 | tf_op jit(solution)/shard_map/ppermute | solution.py:194
  48.6 25.2 %copy-start.3 = (bf16[4,128,256]{2,1,0:T(8,128)(2,1)}, bf16[4,128,256]{2,1,0:T(8,128)(2,1)S(1)}, u32[]{:S(2)}) copy-start(bf16[4,128,256]{2,1,0:T(8,128)(2,1)S(1)} %collective-permute-done.14.three) | copy-start | bytes 786436
  48.6 32.8 %collective-permute-start.7 = (bf16[4,128,256]{2,1,0:T(8,128)(2,1)}, bf16[4,128,256]{2,1,0:T(8,128)(2,1)S(1)}, u32[]{:S(2)}, u32[]{:S(2)}) collective-permute-start(bf16[4,128,256]{2,1,0:T(8,128)(2,1)} %get-tuple-element.64), channel_id=1, source_target_pairs={{254,0},{255,1},{0,254},{1,255},{2,4},{3,5},{4,2},{5,3},{6,8},{7,9... | collective-permute-start | bytes 786440 | tf_op jit(solution)/shard_map/ppermute | solution.py:194
  49.9 23.9 %copy-start.4 = (bf16[4,128,256]{2,1,0:T(8,128)(2,1)}, bf16[4,128,256]{2,1,0:T(8,128)(2,1)S(1)}, u32[]{:S(2)}) copy-start(bf16[4,128,256]{2,1,0:T(8,128)(2,1)S(1)} %collective-permute-done.9.one) | copy-start | bytes 786436
  49.9 44.2 %collective-permute-start.8 = (bf16[4,128,256]{2,1,0:T(8,128)(2,1)S(1)}, bf16[4,128,256]{2,1,0:T(8,128)(2,1)S(1)}, u32[]{:S(2)}, u32[]{:S(2)}) collective-permute-start(bf16[4,128,256]{2,1,0:T(8,128)(2,1)S(1)} %copy-done.35), channel_id=1, source_target_pairs={{254,1},{255,254},{0,255},{1,0},{2,5},{3,2},{4,3},{5,4},{6,9},{7,6... | collective-permute-start | bytes 786440 | tf_op jit(solution)/shard_map/ppermute | solution.py:194
  57.0 16.9 %copy-start.5 = (bf16[4,128,256]{2,1,0:T(8,128)(2,1)}, bf16[4,128,256]{2,1,0:T(8,128)(2,1)S(1)}, u32[]{:S(2)}) copy-start(bf16[4,128,256]{2,1,0:T(8,128)(2,1)S(1)} %collective-permute-done.10.two) | copy-start | bytes 786436
  57.0 41.3 %collective-permute-start.3 = (bf16[4,128,256]{2,1,0:T(8,128)(2,1)}, bf16[4,128,256]{2,1,0:T(8,128)(2,1)S(1)}, u32[]{:S(2)}, u32[]{:S(2)}) collective-permute-start(bf16[4,128,256]{2,1,0:T(8,128)(2,1)} %get-tuple-element.58.rest_0_), channel_id=1, source_target_pairs={{254,255},{255,0},{0,1},{1,254},{2,3},{3,4},{4,5},{5,2},{6,7},{7,8... | collective-permute-start | bytes 786440 | tf_op jit(solution)/shard_map/ppermute | solution.py:194
  71.6 4.2 %copy-start.33 = (bf16[4,128,256]{2,1,0:T(8,128)(2,1)S(1)}, bf16[4,128,256]{2,1,0:T(8,128)(2,1)}, u32[]{:S(2)}) copy-start(bf16[4,128,256]{2,1,0:T(8,128)(2,1)} %get-tuple-element.63) | copy-start | bytes 786436
  74.6 34.8 %copy-start.21 = (bf16[4,128,256]{2,1,0:T(8,128)(2,1)}, bf16[4,128,256]{2,1,0:T(8,128)(2,1)S(1)}, u32[]{:S(2)}) copy-start(bf16[4,128,256]{2,1,0:T(8,128)(2,1)S(1)} %collective-permute-done.11.three) | copy-start | bytes 786436
  74.6 43.0 %collective-permute-start.4 = (bf16[4,128,256]{2,1,0:T(8,128)(2,1)}, bf16[4,128,256]{2,1,0:T(8,128)(2,1)S(1)}, u32[]{:S(2)}, u32[]{:S(2)}) collective-permute-start(bf16[4,128,256]{2,1,0:T(8,128)(2,1)} %get-tuple-element.62), channel_id=1, source_target_pairs={{254,0},{255,1},{0,254},{1,255},{2,4},{3,5},{4,2},{5,3},{6,8},{7,9... | collective-permute-start | bytes 786440 | tf_op jit(solution)/shard_map/ppermute | solution.py:194
  75.8 33.6 %copy-start.6 = (bf16[4,128,256]{2,1,0:T(8,128)(2,1)}, bf16[4,128,256]{2,1,0:T(8,128)(2,1)S(1)}, u32[]{:S(2)}) copy-start(bf16[4,128,256]{2,1,0:T(8,128)(2,1)S(1)} %collective-permute-done.6.one) | copy-start | bytes 786436
  75.8 43.5 %collective-permute-start.5 = (bf16[4,128,256]{2,1,0:T(8,128)(2,1)S(1)}, bf16[4,128,256]{2,1,0:T(8,128)(2,1)S(1)}, u32[]{:S(2)}, u32[]{:S(2)}) collective-permute-start(bf16[4,128,256]{2,1,0:T(8,128)(2,1)S(1)} %copy-done.33), channel_id=1, source_target_pairs={{254,1},{255,254},{0,255},{1,0},{2,5},{3,2},{4,3},{5,4},{6,9},{7,6... | collective-permute-start | bytes 786440 | tf_op jit(solution)/shard_map/ppermute | solution.py:194
  81.5 27.9 %copy-start.8 = (bf16[4,128,256]{2,1,0:T(8,128)(2,1)}, bf16[4,128,256]{2,1,0:T(8,128)(2,1)S(1)}, u32[]{:S(2)}) copy-start(bf16[4,128,256]{2,1,0:T(8,128)(2,1)S(1)} %collective-permute-done.7.two) | copy-start | bytes 786436
  81.5 45.2 %collective-permute-start = (bf16[4,128,256]{2,1,0:T(8,128)(2,1)}, bf16[4,128,256]{2,1,0:T(8,128)(2,1)S(1)}, u32[]{:S(2)}, u32[]{:S(2)}) collective-permute-start(bf16[4,128,256]{2,1,0:T(8,128)(2,1)} %get-tuple-element.59), channel_id=1, source_target_pairs={{254,255},{255,0},{0,1},{1,254},{2,3},{3,4},{4,5},{5,2},{6,7},{7,8... | collective-permute-start | bytes 786440 | tf_op jit(solution)/shard_map/ppermute | solution.py:194
  94.1 15.3 %copy-start.11 = (bf16[4,128,256]{2,1,0:T(8,128)(2,1)}, bf16[4,128,256]{2,1,0:T(8,128)(2,1)S(1)}, u32[]{:S(2)}) copy-start(bf16[4,128,256]{2,1,0:T(8,128)(2,1)S(1)} %collective-permute-done.8.three) | copy-start | bytes 786436
  94.1 32.6 %collective-permute-start.1 = (bf16[4,128,256]{2,1,0:T(8,128)(2,1)}, bf16[4,128,256]{2,1,0:T(8,128)(2,1)S(1)}, u32[]{:S(2)}, u32[]{:S(2)}) collective-permute-start(bf16[4,128,256]{2,1,0:T(8,128)(2,1)} %get-tuple-element.60), channel_id=1, source_target_pairs={{254,0},{255,1},{0,254},{1,255},{2,4},{3,5},{4,2},{5,3},{6,8},{7,9... | collective-permute-start | bytes 786440 | tf_op jit(solution)/shard_map/ppermute | solution.py:194
  98.3 11.1 %copy-start.12 = (bf16[4,128,256]{2,1,0:T(8,128)(2,1)}, bf16[4,128,256]{2,1,0:T(8,128)(2,1)S(1)}, u32[]{:S(2)}) copy-start(bf16[4,128,256]{2,1,0:T(8,128)(2,1)S(1)} %collective-permute-done.3.one) | copy-start | bytes 786436
  98.3 38.6 %collective-permute-start.2 = (bf16[4,128,256]{2,1,0:T(8,128)(2,1)}, bf16[4,128,256]{2,1,0:T(8,128)(2,1)S(1)}, u32[]{:S(2)}, u32[]{:S(2)}) collective-permute-start(bf16[4,128,256]{2,1,0:T(8,128)(2,1)} %get-tuple-element.61), channel_id=1, source_target_pairs={{254,1},{255,254},{0,255},{1,0},{2,5},{3,2},{4,3},{5,4},{6,9},{7,6... | collective-permute-start | bytes 786440 | tf_op jit(solution)/shard_map/ppermute | solution.py:194
  109.4 8.2 %copy-start.39 = (bf16[4,128,256]{2,1,0:T(8,128)(2,1)S(1)}, bf16[4,128,256]{2,1,0:T(8,128)(2,1)}, u32[]{:S(2)}) copy-start(bf16[4,128,256]{2,1,0:T(8,128)(2,1)} %get-tuple-element.87) | copy-start | bytes 786436
  109.4 9.9 %copy-start.38 = (bf16[4,128,256]{2,1,0:T(8,128)(2,1)S(1)}, bf16[4,128,256]{2,1,0:T(8,128)(2,1)}, u32[]{:S(2)}) copy-start(bf16[4,128,256]{2,1,0:T(8,128)(2,1)} %get-tuple-element.88) | copy-start | bytes 786436
  109.4 17.2 %copy-start.37 = (bf16[4,128,256]{2,1,0:T(8,128)(2,1)S(1)}, bf16[4,128,256]{2,1,0:T(8,128)(2,1)}, u32[]{:S(2)}) copy-start(bf16[4,128,256]{2,1,0:T(8,128)(2,1)} %get-tuple-element.89) | copy-start | bytes 786436
  117.6 37.0 %copy-start.15 = (bf16[4,128,256]{2,1,0:T(8,128)(2,1)}, bf16[4,128,256]{2,1,0:T(8,128)(2,1)S(1)}, u32[]{:S(2)}) copy-start(bf16[4,128,256]{2,1,0:T(8,128)(2,1)S(1)} %collective-permute-done.4.two) | copy-start | bytes 786436
  117.6 45.1 %collective-permute-start.27 = (bf16[4,128,256]{2,1,0:T(8,128)(2,1)S(1)}, bf16[4,128,256]{2,1,0:T(8,128)(2,1)S(1)}, u32[]{:S(2)}, u32[]{:S(2)}) collective-permute-start(bf16[4,128,256]{2,1,0:T(8,128)(2,1)S(1)} %copy-done.39), channel_id=1, source_target_pairs={{254,1},{255,254},{0,255},{1,0},{2,5},{3,2},{4,3},{5,4},{6,9},{7,6... | collective-permute-start | bytes 786440 | tf_op jit(solution)/shard_map/ppermute | solution.py:194
  119.3 35.2 %copy-start.19 = (bf16[4,128,256]{2,1,0:T(8,128)(2,1)}, bf16[4,128,256]{2,1,0:T(8,128)(2,1)S(1)}, u32[]{:S(2)}) copy-start(bf16[4,128,256]{2,1,0:T(8,128)(2,1)S(1)} %collective-permute-done.5.three) | copy-start | bytes 786436
  119.3 43.5 %collective-permute-start.28 = (bf16[4,128,256]{2,1,0:T(8,128)(2,1)S(1)}, bf16[4,128,256]{2,1,0:T(8,128)(2,1)S(1)}, u32[]{:S(2)}, u32[]{:S(2)}) collective-permute-start(bf16[4,128,256]{2,1,0:T(8,128)(2,1)S(1)} %copy-done.38), channel_id=1, source_target_pairs={{254,0},{255,1},{0,254},{1,255},{2,4},{3,5},{4,2},{5,3},{6,8},{7,9... | collective-permute-start | bytes 786440 | tf_op jit(solution)/shard_map/ppermute | solution.py:194
  126.7 27.9 %copy-start.7 = (bf16[4,128,256]{2,1,0:T(8,128)(2,1)}, bf16[4,128,256]{2,1,0:T(8,128)(2,1)S(1)}, u32[]{:S(2)}) copy-start(bf16[4,128,256]{2,1,0:T(8,128)(2,1)S(1)} %collective-permute-done.one) | copy-start | bytes 786436
  126.7 43.4 %collective-permute-start.29 = (bf16[4,128,256]{2,1,0:T(8,128)(2,1)S(1)}, bf16[4,128,256]{2,1,0:T(8,128)(2,1)S(1)}, u32[]{:S(2)}, u32[]{:S(2)}) collective-permute-start(bf16[4,128,256]{2,1,0:T(8,128)(2,1)S(1)} %copy-done.37), channel_id=1, source_target_pairs={{254,255},{255,0},{0,1},{1,254},{2,3},{3,4},{4,5},{5,2},{6,7},{7,8... | collective-permute-start | bytes 786440 | tf_op jit(solution)/shard_map/ppermute | solution.py:194
  126.7 27.9 %copy-start.9 = (bf16[4,128,256]{2,1,0:T(8,128)(2,1)}, bf16[4,128,256]{2,1,0:T(8,128)(2,1)S(1)}, u32[]{:S(2)}) copy-start(bf16[4,128,256]{2,1,0:T(8,128)(2,1)S(1)} %collective-permute-done.1.two) | copy-start | bytes 786436
  126.7 45.9 %collective-permute-start.24 = (bf16[4,128,256]{2,1,0:T(8,128)(2,1)}, bf16[4,128,256]{2,1,0:T(8,128)(2,1)S(1)}, u32[]{:S(2)}, u32[]{:S(2)}) collective-permute-start(bf16[4,128,256]{2,1,0:T(8,128)(2,1)} %get-tuple-element.84), channel_id=1, source_target_pairs={{254,1},{255,254},{0,255},{1,0},{2,5},{3,2},{4,3},{5,4},{6,9},{7,6... | collective-permute-start | bytes 786440 | tf_op jit(solution)/shard_map/ppermute | solution.py:194
  137.0 17.6 %copy-start.13 = (bf16[4,128,256]{2,1,0:T(8,128)(2,1)}, bf16[4,128,256]{2,1,0:T(8,128)(2,1)S(1)}, u32[]{:S(2)}) copy-start(bf16[4,128,256]{2,1,0:T(8,128)(2,1)S(1)} %collective-permute-done.2.three) | copy-start | bytes 786436
  137.0 35.7 %collective-permute-start.25 = (bf16[4,128,256]{2,1,0:T(8,128)(2,1)}, bf16[4,128,256]{2,1,0:T(8,128)(2,1)S(1)}, u32[]{:S(2)}, u32[]{:S(2)}) collective-permute-start(bf16[4,128,256]{2,1,0:T(8,128)(2,1)} %get-tuple-element.85), channel_id=1, source_target_pairs={{254,0},{255,1},{0,254},{1,255},{2,4},{3,5},{4,2},{5,3},{6,8},{7,9... | collective-permute-start | bytes 786440 | tf_op jit(solution)/shard_map/ppermute | solution.py:194
  154.6 8.2 %copy-start.34 = (bf16[4,128,256]{2,1,0:T(8,128)(2,1)S(1)}, bf16[4,128,256]{2,1,0:T(8,128)(2,1)}, u32[]{:S(2)}) copy-start(bf16[4,128,256]{2,1,0:T(8,128)(2,1)} %get-tuple-element.86) | copy-start | bytes 786436
  154.6 18.0 %copy-start.36 = (bf16[4,128,256]{2,1,0:T(8,128)(2,1)S(1)}, bf16[4,128,256]{2,1,0:T(8,128)(2,1)}, u32[]{:S(2)}) copy-start(bf16[4,128,256]{2,1,0:T(8,128)(2,1)} %get-tuple-element.83) | copy-start | bytes 786436
  162.7 25.2 %copy-start.28 = (bf16[4,128,256]{2,1,0:T(8,128)(2,1)}, bf16[4,128,256]{2,1,0:T(8,128)(2,1)S(1)}, u32[]{:S(2)}) copy-start(bf16[4,128,256]{2,1,0:T(8,128)(2,1)S(1)} %collective-permute-done.27.rest_1_) | copy-start | bytes 786436
  162.8 25.2 %collective-permute-start.26 = (bf16[4,128,256]{2,1,0:T(8,128)(2,1)S(1)}, bf16[4,128,256]{2,1,0:T(8,128)(2,1)S(1)}, u32[]{:S(2)}, u32[]{:S(2)}) collective-permute-start(bf16[4,128,256]{2,1,0:T(8,128)(2,1)S(1)} %copy-done.34), channel_id=1, source_target_pairs={{254,255},{255,0},{0,1},{1,254},{2,3},{3,4},{4,5},{5,2},{6,7},{7,8... | collective-permute-start | bytes 786440 | tf_op jit(solution)/shard_map/ppermute | solution.py:194
  162.9 25.1 %copy-start.29 = (bf16[4,128,256]{2,1,0:T(8,128)(2,1)}, bf16[4,128,256]{2,1,0:T(8,128)(2,1)S(1)}, u32[]{:S(2)}) copy-start(bf16[4,128,256]{2,1,0:T(8,128)(2,1)S(1)} %collective-permute-done.28.rest_2_) | copy-start | bytes 786436
  162.9 33.3 %collective-permute-start.21 = (bf16[4,128,256]{2,1,0:T(8,128)(2,1)}, bf16[4,128,256]{2,1,0:T(8,128)(2,1)S(1)}, u32[]{:S(2)}, u32[]{:S(2)}) collective-permute-start(bf16[4,128,256]{2,1,0:T(8,128)(2,1)} %get-tuple-element.81), channel_id=1, source_target_pairs={{254,1},{255,254},{0,255},{1,0},{2,5},{3,2},{4,3},{5,4},{6,9},{7,6... | collective-permute-start | bytes 786440 | tf_op jit(solution)/shard_map/ppermute | solution.py:194
  170.8 27.0 %collective-permute-start.22 = (bf16[4,128,256]{2,1,0:T(8,128)(2,1)}, bf16[4,128,256]{2,1,0:T(8,128)(2,1)S(1)}, u32[]{:S(2)}, u32[]{:S(2)}) collective-permute-start(bf16[4,128,256]{2,1,0:T(8,128)(2,1)} %get-tuple-element.82), channel_id=1, source_target_pairs={{254,0},{255,1},{0,254},{1,255},{2,4},{3,5},{4,2},{5,3},{6,8},{7,9... | collective-permute-start | bytes 786440 | tf_op jit(solution)/shard_map/ppermute | solution.py:194
  172.6 15.4 %copy-start.10 = (bf16[4,128,256]{2,1,0:T(8,128)(2,1)}, bf16[4,128,256]{2,1,0:T(8,128)(2,1)S(1)}, u32[]{:S(2)}) copy-start(bf16[4,128,256]{2,1,0:T(8,128)(2,1)S(1)} %collective-permute-done.24.rest_1_) | copy-start | bytes 786436
  172.6 31.8 %collective-permute-start.23 = (bf16[4,128,256]{2,1,0:T(8,128)(2,1)S(1)}, bf16[4,128,256]{2,1,0:T(8,128)(2,1)S(1)}, u32[]{:S(2)}, u32[]{:S(2)}) collective-permute-start(bf16[4,128,256]{2,1,0:T(8,128)(2,1)S(1)} %copy-done.36), channel_id=1, source_target_pairs={{254,255},{255,0},{0,1},{1,254},{2,3},{3,4},{4,5},{5,2},{6,7},{7,8... | collective-permute-start | bytes 786440 | tf_op jit(solution)/shard_map/ppermute | solution.py:194
  172.7 15.3 %copy-start.14 = (bf16[4,128,256]{2,1,0:T(8,128)(2,1)}, bf16[4,128,256]{2,1,0:T(8,128)(2,1)S(1)}, u32[]{:S(2)}) copy-start(bf16[4,128,256]{2,1,0:T(8,128)(2,1)S(1)} %collective-permute-done.25.rest_2_) | copy-start | bytes 786436
  172.7 34.1 %collective-permute-start.18 = (bf16[4,128,256]{2,1,0:T(8,128)(2,1)}, bf16[4,128,256]{2,1,0:T(8,128)(2,1)S(1)}, u32[]{:S(2)}, u32[]{:S(2)}) collective-permute-start(bf16[4,128,256]{2,1,0:T(8,128)(2,1)} %get-tuple-element.78), channel_id=1, source_target_pairs={{254,1},{255,254},{0,255},{1,0},{2,5},{3,2},{4,3},{5,4},{6,9},{7,6... | collective-permute-start | bytes 786440 | tf_op jit(solution)/shard_map/ppermute | solution.py:194
  179.8 16.3 %copy-start.32 = (bf16[4,128,256]{2,1,0:T(8,128)(2,1)S(1)}, bf16[4,128,256]{2,1,0:T(8,128)(2,1)}, u32[]{:S(2)}) copy-start(bf16[4,128,256]{2,1,0:T(8,128)(2,1)} %get-tuple-element.80) | copy-start | bytes 786436
  188.0 22.0 %copy-start.18 = (bf16[4,128,256]{2,1,0:T(8,128)(2,1)}, bf16[4,128,256]{2,1,0:T(8,128)(2,1)S(1)}, u32[]{:S(2)}) copy-start(bf16[4,128,256]{2,1,0:T(8,128)(2,1)S(1)} %collective-permute-done.26.rest_3_) | copy-start | bytes 786436
  188.0 35.0 %collective-permute-start.19 = (bf16[4,128,256]{2,1,0:T(8,128)(2,1)}, bf16[4,128,256]{2,1,0:T(8,128)(2,1)S(1)}, u32[]{:S(2)}, u32[]{:S(2)}) collective-permute-start(bf16[4,128,256]{2,1,0:T(8,128)(2,1)} %get-tuple-element.79), channel_id=1, source_target_pairs={{254,0},{255,1},{0,254},{1,255},{2,4},{3,5},{4,2},{5,3},{6,8},{7,9... | collective-permute-start | bytes 786440 | tf_op jit(solution)/shard_map/ppermute | solution.py:194
  196.2 16.1 %copy-start.16 = (bf16[4,128,256]{2,1,0:T(8,128)(2,1)}, bf16[4,128,256]{2,1,0:T(8,128)(2,1)S(1)}, u32[]{:S(2)}) copy-start(bf16[4,128,256]{2,1,0:T(8,128)(2,1)S(1)} %collective-permute-done.21.rest_1_) | copy-start | bytes 786436
  196.2 30.7 %collective-permute-start.20 = (bf16[4,128,256]{2,1,0:T(8,128)(2,1)S(1)}, bf16[4,128,256]{2,1,0:T(8,128)(2,1)S(1)}, u32[]{:S(2)}, u32[]{:S(2)}) collective-permute-start(bf16[4,128,256]{2,1,0:T(8,128)(2,1)S(1)} %copy-done.32), channel_id=1, source_target_pairs={{254,255},{255,0},{0,1},{1,254},{2,3},{3,4},{4,5},{5,2},{6,7},{7,8... | collective-permute-start | bytes 786440 | tf_op jit(solution)/shard_map/ppermute | solution.py:194
  197.8 14.5 %copy-start.20 = (bf16[4,128,256]{2,1,0:T(8,128)(2,1)}, bf16[4,128,256]{2,1,0:T(8,128)(2,1)S(1)}, u32[]{:S(2)}) copy-start(bf16[4,128,256]{2,1,0:T(8,128)(2,1)S(1)} %collective-permute-done.22.rest_2_) | copy-start | bytes 786436
  197.8 32.1 %collective-permute-start.15 = (bf16[4,128,256]{2,1,0:T(8,128)(2,1)}, bf16[4,128,256]{2,1,0:T(8,128)(2,1)S(1)}, u32[]{:S(2)}, u32[]{:S(2)}) collective-permute-start(bf16[4,128,256]{2,1,0:T(8,128)(2,1)} %get-tuple-element.75), channel_id=1, source_target_pairs={{254,1},{255,254},{0,255},{1,0},{2,5},{3,2},{4,3},{5,4},{6,9},{7,6... | collective-permute-start | bytes 786440 | tf_op jit(solution)/shard_map/ppermute | solution.py:194
  204.4 7.9 %copy-start.23 = (bf16[4,128,256]{2,1,0:T(8,128)(2,1)}, bf16[4,128,256]{2,1,0:T(8,128)(2,1)S(1)}, u32[]{:S(2)}) copy-start(bf16[4,128,256]{2,1,0:T(8,128)(2,1)S(1)} %collective-permute-done.23.rest_3_) | copy-start | bytes 786436
  204.4 29.8 %collective-permute-start.16 = (bf16[4,128,256]{2,1,0:T(8,128)(2,1)}, bf16[4,128,256]{2,1,0:T(8,128)(2,1)S(1)}, u32[]{:S(2)}, u32[]{:S(2)}) collective-permute-start(bf16[4,128,256]{2,1,0:T(8,128)(2,1)} %get-tuple-element.76), channel_id=1, source_target_pairs={{254,0},{255,1},{0,254},{1,255},{2,4},{3,5},{4,2},{5,3},{6,8},{7,9... | collective-permute-start | bytes 786440 | tf_op jit(solution)/shard_map/ppermute | solution.py:194
  206.8 5.5 %copy-start.17 = (bf16[4,128,256]{2,1,0:T(8,128)(2,1)}, bf16[4,128,256]{2,1,0:T(8,128)(2,1)S(1)}, u32[]{:S(2)}) copy-start(bf16[4,128,256]{2,1,0:T(8,128)(2,1)S(1)} %collective-permute-done.18.rest_1_) | copy-start | bytes 786436
  206.8 30.6 %collective-permute-start.17 = (bf16[4,128,256]{2,1,0:T(8,128)(2,1)}, bf16[4,128,256]{2,1,0:T(8,128)(2,1)S(1)}, u32[]{:S(2)}, u32[]{:S(2)}) collective-permute-start(bf16[4,128,256]{2,1,0:T(8,128)(2,1)} %get-tuple-element.77), channel_id=1, source_target_pairs={{254,255},{255,0},{0,1},{1,254},{2,3},{3,4},{4,5},{5,2},{6,7},{7,8... | collective-permute-start | bytes 786440 | tf_op jit(solution)/shard_map/ppermute | solution.py:194
  229.9 7.5 %copy-start.22 = (bf16[4,128,256]{2,1,0:T(8,128)(2,1)}, bf16[4,128,256]{2,1,0:T(8,128)(2,1)S(1)}, u32[]{:S(2)}) copy-start(bf16[4,128,256]{2,1,0:T(8,128)(2,1)S(1)} %collective-permute-done.15.rest_1_) | copy-start | bytes 786436
  (6 other events, 11.5 us)

commit v2 on v1

--- a/solution.py
+++ b/solution.py
@@ -12,33 +12,43 @@
 MOST = 4
 AXES = ("seq", "uly")
 CHUNKS = (2, 2, 2, 2, 2)
-ORDER = (1, 2, 3)
-
-
-def turns(step, tiles):
+TURNING = (True, False, False, False, False)
+LAST = [(0, 1), (2,), (3,)]
+
+
+def partner(place, step, turning):
+    return (place + step) % MOST if turning else place ^ step
+
+
+def routes(step, tiles, turning):
     def tile_at(window, place):
         return (MOST * window + place - MOST // 2) % tiles
 
     return [
-        (tile_at(window, place), tile_at(window, (place + step) % MOST))
+        (tile_at(window, place), tile_at(window, partner(place, step, turning)))
         for window in range(tiles // MOST)
         for place in range(MOST)
     ]
 
 
-def place_at(step):
-    return (lax.axis_index("uly") + MOST // 2 + step) % MOST
-
-
-def pack_kernel(begin, heads_each, width, q_ref, k_ref, v_ref, g_ref, *rest):
+def head_columns(step, turning, begin, heads_each, width):
+    place = (lax.axis_index("uly") + MOST // 2) % MOST
+    return pl.ds(pl.multiple_of((partner(place, step, turning) * heads_each + begin) * HD, HD), width)
+
+
+def small_grant():
+    return pltpu.CompilerParams(vmem_limit_bytes=16 * 1024 * 1024)
+
+
+def pack_kernel(turning, begin, heads_each, width, q_ref, k_ref, v_ref, g_ref, *rest):
     outs, sems = rest[-4:-1], rest[-1]
     copies = []
     for step in range(1, MOST):
-        column = pl.multiple_of((place_at(step) * heads_each + begin) * HD, HD)
+        columns = head_columns(step, turning, begin, heads_each, width)
         for member, source in enumerate((q_ref, k_ref, v_ref, g_ref)):
             copies.append(
                 pltpu.make_async_copy(
-                    source.at[:, pl.ds(column, width)],
+                    source.at[:, columns],
                     outs[step - 1].at[member],
                     sems.at[step - 1, member],
                 )
@@ -49,32 +59,34 @@
         copy.wait()
 
 
-def pack(arrays, after, begin, heads, heads_each):
+def pack(turning, arrays, after, begin, heads, heads_each):
     width = heads * HD
-    piece = jax.ShapeDtypeStruct((4, TILE, width), jnp.bfloat16)
+    piece = pltpu.VMEM((4, TILE, width), jnp.bfloat16)
+    arrays = [pltpu.with_memory_space_constraint(array, pltpu.HBM) for array in arrays]
     return pl.pallas_call(
-        partial(pack_kernel, begin, heads_each, width),
+        partial(pack_kernel, turning, begin, heads_each, width),
         out_shape=(piece,) * 3,
         in_specs=[pl.BlockSpec(memory_space=pl.ANY)] * (4 + len(after)),
         out_specs=(pl.BlockSpec(memory_space=pltpu.VMEM),) * 3,
         scratch_shapes=[pltpu.SemaphoreType.DMA((3, 4))],
+        compiler_params=small_grant(),
         cost_estimate=pl.CostEstimate(flops=0, bytes_accessed=24 * TILE * width * 2, transcendentals=0),
         name="pack",
     )(*arrays, *after)
 
 
-def unpack_kernel(begin, heads_each, width, *rest):
-    pieces = rest[:4]
+def unpack_kernel(turning, steps, begin, heads_each, width, *rest):
+    pieces = rest[: len(steps)]
     outs, sems = rest[-5:-1], rest[-1]
     copies = []
-    for step in range(MOST):
-        column = pl.multiple_of((place_at(step) * heads_each + begin) * HD, HD)
+    for index, step in enumerate(steps):
+        columns = head_columns(step, turning, begin, heads_each, width)
         for member, target in enumerate(outs):
             copies.append(
                 pltpu.make_async_copy(
-                    pieces[step].at[member],
-                    target.at[:, pl.ds(column, width)],
-                    sems.at[step, member],
+                    pieces[index].at[member],
+                    target.at[:, columns],
+                    sems.at[index, member],
                 )
             )
     for copy in copies:
@@ -83,19 +95,19 @@
         copy.wait()
 
 
-def unpack(pieces, held, begin, heads, heads_each, columns):
+def unpack(turning, steps, pieces, held, begin, heads, heads_each, columns):
     width = heads * HD
     whole = jax.ShapeDtypeStruct((TILE, columns), jnp.bfloat16)
-    held = () if held is None else tuple(held)
     return pl.pallas_call(
-        partial(unpack_kernel, begin, heads_each, width),
+        partial(unpack_kernel, turning, steps, begin, heads_each, width),
         out_shape=(whole,) * 4,
-        in_specs=[pl.BlockSpec(memory_space=pltpu.VMEM)] * 4
+        in_specs=[pl.BlockSpec(memory_space=pltpu.VMEM)] * len(steps)
         + [pl.BlockSpec(memory_space=pl.ANY)] * len(held),
         out_specs=(pl.BlockSpec(memory_space=pl.ANY),) * 4,
-        scratch_shapes=[pltpu.SemaphoreType.DMA((4, 4))],
-        input_output_aliases={4 + i: i for i in range(len(held))},
-        cost_estimate=pl.CostEstimate(flops=0, bytes_accessed=32 * TILE * width * 2, transcendentals=0),
+        scratch_shapes=[pltpu.SemaphoreType.DMA((len(steps), 4))],
+        compiler_params=small_grant(),
+        input_output_aliases={len(steps) + i: i for i in range(len(held))},
+        cost_estimate=pl.CostEstimate(flops=0, bytes_accessed=8 * len(steps) * TILE * width * 2, transcendentals=0),
         name="unpack",
     )(*pieces, *held)
 
@@ -167,6 +179,7 @@
             + [pl.BlockSpec(memory_space=pl.ANY)] * len(after),
             out_specs=(piece_spec,) * 4,
         ),
+        compiler_params=small_grant(),
         cost_estimate=pl.CostEstimate(
             flops=12 * rows * rows * HD * heads,
             bytes_accessed=16 * rows * HD * heads,
@@ -183,31 +196,37 @@
     tiles = tile_offset.shape[0]
     device = lax.axis_index(AXES)
     place = (device + MOST // 2) % MOST
-    places = (place - jnp.arange(MOST)) % MOST
-    members = (device - place + places + tiles) % tiles
-    firsts = members - tile_offset[members]
-    info = jnp.concatenate((place[None], firsts)).astype(jnp.int32)
-
-    def exchange(pieces, sign):
-        done = {}
-        for step in ORDER:
-            done[step] = lax.ppermute(pieces[step - 1], AXES, turns(sign * step, tiles))
-        return tuple(done[step] for step in (1, 2, 3))
+    firsts = jnp.arange(tiles, dtype=jnp.int32) - tile_offset
+
+    def describe(turning):
+        slots = jnp.arange(MOST)
+        sources = (place - slots) % MOST if turning else place ^ slots
+        return jnp.concatenate((place[None], firsts[(device - place + sources + tiles) % tiles])).astype(jnp.int32)
+
+    infos = {turning: describe(turning) for turning in set(TURNING)}
+
+    def exchange(pieces, turning, sign):
+        return [
+            lax.ppermute(piece, AXES, routes(sign * step if turning else step, tiles, turning))
+            for step, piece in zip((1, 2, 3), pieces)
+        ]
 
     begins = [sum(CHUNKS[:i]) for i in range(len(CHUNKS))]
     received, after = [], ()
-    for begin, heads in zip(begins, CHUNKS):
-        pieces = pack(arrays, after, begin, heads, heads_each)
+    for turning, begin, heads in zip(TURNING, begins, CHUNKS):
+        pieces = pack(turning, arrays, after, begin, heads, heads_each)
         after = pieces[:1]
-        received.append(exchange(pieces, 1))
+        received.append(exchange(pieces, turning, 1))
     results, after = [], ()
-    for begin, heads, pieces in zip(begins, CHUNKS, received):
-        own, *others = attend(info, arrays, pieces, after, begin, heads, heads_each)
+    for turning, begin, heads, pieces in zip(TURNING, begins, CHUNKS, received):
+        own, *others = attend(infos[turning], arrays, pieces, after, begin, heads, heads_each)
         after = (own,)
-        results.append((own, exchange(others, -1)))
-    held = None
-    for begin, heads, (own, others) in zip(begins, CHUNKS, results):
-        held = unpack((own, *others), held, begin, heads, heads_each, columns)
+        results.append((own, *exchange(others, turning, -1)))
+    held = ()
+    for index, (turning, begin, heads, pieces) in enumerate(zip(TURNING, begins, CHUNKS, results)):
+        for steps in [(0, 1, 2, 3)] if index < len(CHUNKS) - 1 else LAST:
+            parts = [pieces[step] for step in steps]
+            held = unpack(turning, steps, parts, held, begin, heads, heads_each, columns)
     return tuple(held)
 
 

time: 241 us -> 238 us (0.988)
  waiting for transfers between devices: 43.4 us -> 75.9 us
  starting transfers between devices: 130 us -> 99.9 us
  Pallas kernels: 62.6 us -> 50 us
  local copies, waits for them, and re-layouts: 2.94 us -> 10.1 us
    ppermute x30, waiting for transfers between devices: 43.4 us -> 75.9 us  [exchange(): lax.ppermute(piece, AXES, routes(sign * step if turning else step, tiles,...]
    ppermute x30, starting transfers between devices: 130 us -> 99.9 us  [exchange(): lax.ppermute(piece, AXES, routes(sign * step if turning else step, tiles,...]
    pallas_call x10 -> x12, Pallas kernels: 22.3 us -> 15.6 us  [the longest x5 8.84 us: pack(): pl.pallas_call(partial(pack_kernel, turning, begin, heads_each, width), o...]
    unnamed x80 -> x28, local copies, waits for them, and re-layouts: 2.3 us -> 8.78 us
    pallas_call x5, Pallas kernels: 40.3 us -> 34.5 us  [attend(): pl.pallas_call(attend_kernel, out_shape=(piece,) * 4, grid_spec=pltpu.Pre...]
  transfers between devices with their start and end apart: 30 -> 30, of which waited for: 12 -> 12; matrix products, arithmetic and copies ran while one was open for 1% -> 1% of each run, Pallas kernels for 24% -> 20%
where the time goes in v2:
time: 238 us; the launch traced here: 237 us
  starting transfers between devices  99.9 us (42%)
  waiting for transfers between devices  75.9 us (32%)
  Pallas kernels  50 us (21%)
  local copies, waits for them, and re-layouts  10.1 us (4%)
    ppermute x30, starting transfers between devices, exchange(): lax.ppermute(piece, AXES, routes(sign * step if turning else step, tiles,...  99.9 us
    ppermute x30, waiting for transfers between devices, exchange(): lax.ppermute(piece, AXES, routes(sign * step if turning else step, tiles,...  75.9 us
    pallas_call x5, Pallas kernels, attend(): pl.pallas_call(attend_kernel, out_shape=(piece,) * 4, grid_spec=pltpu.Pre...  34.5 us
    pallas_call x5, Pallas kernels, pack(): pl.pallas_call(partial(pack_kernel, turning, begin, heads_each, width), o...  8.84 us
    unnamed x28, local copies, waits for them, and re-layouts  8.78 us
    pallas_call x7, Pallas kernels, unpack(): pl.pallas_call(partial(unpack_kernel, turning, steps, begin, heads_each,...  6.73 us
  transfers between devices with their start and end apart: 30, of which 12 were waited for; matrix products, arithmetic and copies ran while one was open for 1% of the time, Pallas kernels for 20%

profile of v2, /device:TPU:0, one launch (start us, length us, event | category | flops | bytes accessed | tf_op | source)
XLA Modules:
  0.0 237.3 jit_solution(2986439407716298835)
XLA Ops:
  0.6 1.3 pack.5
  1.9 0.3 collective-permute-start.12
  2.2 9.2 %collective-permute-start.13 = (bf16[4,128,256]{2,1,0:T(8,128)(2,1)S(1)}, bf16[4,128,256]{2,1,0:T(8,128)(2,1)S(1)}, u32[]{:S(2)}, u32[]{:S(2)}) collective-permute-start(bf16[4,128,256]{2,1,0:T(8,128)(2,1)S(1)} %get-tuple-element.76), channel_id=1, source_target_pairs={{254,0},{255,1},{0,254},{1,255},{2,4},{3,5},{4,2},{5,3},{6,8},{7,9... | collective-permute-start | bytes 786440 | tf_op jit(solution)/shard_map/ppermute | solution.py:210
  11.4 7.3 %collective-permute-start.14 = (bf16[4,128,256]{2,1,0:T(8,128)(2,1)S(1)}, bf16[4,128,256]{2,1,0:T(8,128)(2,1)S(1)}, u32[]{:S(2)}, u32[]{:S(2)}) collective-permute-start(bf16[4,128,256]{2,1,0:T(8,128)(2,1)S(1)} %get-tuple-element.77), channel_id=1, source_target_pairs={{254,1},{255,254},{0,255},{1,0},{2,5},{3,2},{4,3},{5,4},{6,9},{7,6... | collective-permute-start | bytes 786440 | tf_op jit(solution)/shard_map/ppermute | solution.py:210
  18.7 2.0 pack.6
  20.8 1.2 collective-permute-start.10
  22.0 2.2 pack.7
  24.2 7.5 %collective-permute-start.11 = (bf16[4,128,256]{2,1,0:T(8,128)(2,1)}, bf16[4,128,256]{2,1,0:T(8,128)(2,1)}, u32[]{:S(2)}, u32[]{:S(2)}) collective-permute-start(bf16[4,128,256]{2,1,0:T(8,128)(2,1)} %get-tuple-element.75), channel_id=1, source_target_pairs={{254,1},{255,0},{0,255},{1,254},{2,5},{3,4},{4,3},{5,2},{6,9},{7,8... | collective-permute-start | bytes 786440 | tf_op jit(solution)/shard_map/ppermute | solution.py:210
  31.7 15.3 %collective-permute-start.6 = (bf16[4,128,256]{2,1,0:T(8,128)(2,1)}, bf16[4,128,256]{2,1,0:T(8,128)(2,1)}, u32[]{:S(2)}, u32[]{:S(2)}) collective-permute-start(bf16[4,128,256]{2,1,0:T(8,128)(2,1)} %get-tuple-element.65.rest_0_), channel_id=1, source_target_pairs={{254,255},{255,254},{0,1},{1,0},{2,3},{3,2},{4,5},{5,4},{6,7},{7,6... | collective-permute-start | bytes 786440 | tf_op jit(solution)/shard_map/ppermute | solution.py:210
  47.1 2.0 pack.8
  49.1 0.7 copy-done.9
  49.8 0.7 copy-done.11
  50.5 0.7 copy-done.6
  51.2 6.7 %collective-permute-start.8 = (bf16[4,128,256]{2,1,0:T(8,128)(2,1)}, bf16[4,128,256]{2,1,0:T(8,128)(2,1)}, u32[]{:S(2)}, u32[]{:S(2)}) collective-permute-start(bf16[4,128,256]{2,1,0:T(8,128)(2,1)} %get-tuple-element.73), channel_id=1, source_target_pairs={{254,1},{255,0},{0,255},{1,254},{2,5},{3,4},{4,3},{5,2},{6,9},{7,8... | collective-permute-start | bytes 786440 | tf_op jit(solution)/shard_map/ppermute | solution.py:210
  57.9 2.9 %collective-permute-start.3 = (bf16[4,128,256]{2,1,0:T(8,128)(2,1)}, bf16[4,128,256]{2,1,0:T(8,128)(2,1)}, u32[]{:S(2)}, u32[]{:S(2)}) collective-permute-start(bf16[4,128,256]{2,1,0:T(8,128)(2,1)} %get-tuple-element.66.rest_0_), channel_id=1, source_target_pairs={{254,255},{255,254},{0,1},{1,0},{2,3},{3,2},{4,5},{5,4},{6,7},{7,6... | collective-permute-start | bytes 786440 | tf_op jit(solution)/shard_map/ppermute | solution.py:210
  60.8 1.4 pack.9
  62.2 0.7 copy-done.8
  62.9 0.7 copy-done.10
  63.6 0.7 copy-done.12
  64.3 0.6 gather_fusion.1
  65.0 0.6 gather_fusion
  65.6 3.6 %collective-permute-done.11.three = bf16[4,128,256]{2,1,0:T(8,128)(2,1)} collective-permute-done((bf16[4,128,256]{2,1,0:T(8,128)(2,1)}, bf16[4,128,256]{2,1,0:T(8,128)(2,1)}, u32[]{:S(2)}, u32[]{:S(2)}) %collective-permute-start.11) | collective-permute-done | bytes 262176 | tf_op jit(solution)/shard_map/ppermute | solution.py:210
  69.2 3.1 %collective-permute-start.5 = (bf16[4,128,256]{2,1,0:T(8,128)(2,1)}, bf16[4,128,256]{2,1,0:T(8,128)(2,1)S(1)}, u32[]{:S(2)}, u32[]{:S(2)}) collective-permute-start(bf16[4,128,256]{2,1,0:T(8,128)(2,1)} %copy-done.9), channel_id=1, source_target_pairs={{254,1},{255,0},{0,255},{1,254},{2,5},{3,4},{4,3},{5,2},{6,9},{7,8... | collective-permute-start | bytes 786440 | tf_op jit(solution)/shard_map/ppermute | solution.py:210
  72.4 6.1 %collective-permute-done.7.two = bf16[4,128,256]{2,1,0:T(8,128)(2,1)} collective-permute-done((bf16[4,128,256]{2,1,0:T(8,128)(2,1)}, bf16[4,128,256]{2,1,0:T(8,128)(2,1)}, u32[]{:S(2)}, u32[]{:S(2)}) %collective-permute-start.7) | collective-permute-done | bytes 262176 | tf_op jit(solution)/shard_map/ppermute | solution.py:210
  78.5 0.3 collective-permute-start
  78.8 12.8 %collective-permute-done.8.three = bf16[4,128,256]{2,1,0:T(8,128)(2,1)} collective-permute-done((bf16[4,128,256]{2,1,0:T(8,128)(2,1)}, bf16[4,128,256]{2,1,0:T(8,128)(2,1)}, u32[]{:S(2)}, u32[]{:S(2)}) %collective-permute-start.8) | collective-permute-done | bytes 262176 | tf_op jit(solution)/shard_map/ppermute | solution.py:210
  91.7 2.6 %collective-permute-start.2 = (bf16[4,128,256]{2,1,0:T(8,128)(2,1)}, bf16[4,128,256]{2,1,0:T(8,128)(2,1)S(1)}, u32[]{:S(2)}, u32[]{:S(2)}) collective-permute-start(bf16[4,128,256]{2,1,0:T(8,128)(2,1)} %copy-done.8), channel_id=1, source_target_pairs={{254,1},{255,0},{0,255},{1,254},{2,5},{3,4},{4,3},{5,2},{6,9},{7,8... | collective-permute-start | bytes 786440 | tf_op jit(solution)/shard_map/ppermute | solution.py:210
  94.3 1.3 copy-done.2
  95.7 1.3 copy-done.3
  97.0 0.9 copy-done.5
  97.9 0.9 copy-done.7
  98.9 6.5 %attend.5 = (bf16[4,128,256]{2,1,0:T(8,128)(2,1)S(1)}, bf16[4,128,256]{2,1,0:T(8,128)(2,1)S(1)}, bf16[4,128,256]{2,1,0:T(8,128)(2,1)S(1)}, bf16[4,128,256]{2,1,0:T(8,128)(2,1)S(1)}) custom-call(s32[5]{0:T(128)S(1)} %pad_add_fusion.1.info, bf16[128,5120]{1,0:T(8,128)(2,1)S(1)} %copy-done, bf16[128,5120]{1,0:T(8,128)(2,1)S(1)} %copy-done.1, ...), custom_call_target="tpu_custom_call" | custom-call | flops 805306368 | bytes 2097152 | tf_op jit(solution)/shard_map/attend/pallas_call | solution.py:171
  105.4 4.8 %collective-permute-start.27 = (bf16[4,128,256]{2,1,0:T(8,128)(2,1)S(1)}, bf16[4,128,256]{2,1,0:T(8,128)(2,1)S(1)}, u32[]{:S(2)}, u32[]{:S(2)}) collective-permute-start(bf16[4,128,256]{2,1,0:T(8,128)(2,1)S(1)} %get-tuple-element.95), channel_id=1, source_target_pairs={{254,1},{255,254},{0,255},{1,0},{2,5},{3,2},{4,3},{5,4},{6,9},{7,6... | collective-permute-start | bytes 786440 | tf_op jit(solution)/shard_map/ppermute | solution.py:210
  110.2 3.8 %collective-permute-done.5.three = bf16[4,128,256]{2,1,0:T(8,128)(2,1)S(1)} collective-permute-done((bf16[4,128,256]{2,1,0:T(8,128)(2,1)}, bf16[4,128,256]{2,1,0:T(8,128)(2,1)S(1)}, u32[]{:S(2)}, u32[]{:S(2)}) %collective-permute-start.5) | collective-permute-done | bytes 262176 | tf_op jit(solution)/shard_map/ppermute | solution.py:210
  114.0 6.1 %collective-permute-start.28 = (bf16[4,128,256]{2,1,0:T(8,128)(2,1)S(1)}, bf16[4,128,256]{2,1,0:T(8,128)(2,1)S(1)}, u32[]{:S(2)}, u32[]{:S(2)}) collective-permute-start(bf16[4,128,256]{2,1,0:T(8,128)(2,1)S(1)} %get-tuple-element.96), channel_id=1, source_target_pairs={{254,0},{255,1},{0,254},{1,255},{2,4},{3,5},{4,2},{5,3},{6,8},{7,9... | collective-permute-start | bytes 786440 | tf_op jit(solution)/shard_map/ppermute | solution.py:210
  120.1 7.2 %attend.6 = (bf16[4,128,256]{2,1,0:T(8,128)(2,1)S(1)}, bf16[4,128,256]{2,1,0:T(8,128)(2,1)S(1)}, bf16[4,128,256]{2,1,0:T(8,128)(2,1)S(1)}, bf16[4,128,256]{2,1,0:T(8,128)(2,1)S(1)}) custom-call(s32[5]{0:T(128)S(1)} %pad_add_fusion.info, bf16[128,5120]{1,0:T(8,128)(2,1)S(1)} %copy-done, bf16[128,5120]{1,0:T(8,128)(2,1)S(1)} %copy-done.1, ...), custom_call_target="tpu_custom_call" | custom-call | flops 805306368 | bytes 2097152 | tf_op jit(solution)/shard_map/attend/pallas_call | solution.py:171
  127.3 0.1 collective-permute-start.29
  127.4 5.0 %collective-permute-start.24 = (bf16[4,128,256]{2,1,0:T(8,128)(2,1)S(1)}, bf16[4,128,256]{2,1,0:T(8,128)(2,1)S(1)}, u32[]{:S(2)}, u32[]{:S(2)}) collective-permute-start(bf16[4,128,256]{2,1,0:T(8,128)(2,1)S(1)} %get-tuple-element.92), channel_id=1, source_target_pairs={{254,255},{255,254},{0,1},{1,0},{2,3},{3,2},{4,5},{5,4},{6,7},{7,6... | collective-permute-start | bytes 786440 | tf_op jit(solution)/shard_map/ppermute | solution.py:210
  132.3 4.2 %collective-permute-done.2.three = bf16[4,128,256]{2,1,0:T(8,128)(2,1)S(1)} collective-permute-done((bf16[4,128,256]{2,1,0:T(8,128)(2,1)}, bf16[4,128,256]{2,1,0:T(8,128)(2,1)S(1)}, u32[]{:S(2)}, u32[]{:S(2)}) %collective-permute-start.2) | collective-permute-done | bytes 262176 | tf_op jit(solution)/shard_map/ppermute | solution.py:210
  136.5 7.2 %attend.7 = (bf16[4,128,256]{2,1,0:T(8,128)(2,1)S(1)}, bf16[4,128,256]{2,1,0:T(8,128)(2,1)S(1)}, bf16[4,128,256]{2,1,0:T(8,128)(2,1)S(1)}, bf16[4,128,256]{2,1,0:T(8,128)(2,1)S(1)}) custom-call(s32[5]{0:T(128)S(1)} %pad_add_fusion.info, bf16[128,5120]{1,0:T(8,128)(2,1)S(1)} %copy-done, bf16[128,5120]{1,0:T(8,128)(2,1)S(1)} %copy-done.1, ...), custom_call_target="tpu_custom_call" | custom-call | flops 805306368 | bytes 2097152 | tf_op jit(solution)/shard_map/attend/pallas_call | solution.py:171
  143.8 3.8 %collective-permute-start.26 = (bf16[4,128,256]{2,1,0:T(8,128)(2,1)S(1)}, bf16[4,128,256]{2,1,0:T(8,128)(2,1)S(1)}, u32[]{:S(2)}, u32[]{:S(2)}) collective-permute-start(bf16[4,128,256]{2,1,0:T(8,128)(2,1)S(1)} %get-tuple-element.94), channel_id=1, source_target_pairs={{254,1},{255,0},{0,255},{1,254},{2,5},{3,4},{4,3},{5,2},{6,9},{7,8... | collective-permute-start | bytes 786440 | tf_op jit(solution)/shard_map/ppermute | solution.py:210
  147.6 3.9 %collective-permute-done.28.rest_2_ = bf16[4,128,256]{2,1,0:T(8,128)(2,1)S(1)} collective-permute-done((bf16[4,128,256]{2,1,0:T(8,128)(2,1)S(1)}, bf16[4,128,256]{2,1,0:T(8,128)(2,1)S(1)}, u32[]{:S(2)}, u32[]{:S(2)}) %collective-permute-start.28) | collective-permute-done | bytes 262176 | tf_op jit(solution)/shard_map/ppermute | solution.py:210
  151.5 1.9 collective-permute-start.21
  153.4 6.3 %collective-permute-start.22 = (bf16[4,128,256]{2,1,0:T(8,128)(2,1)S(1)}, bf16[4,128,256]{2,1,0:T(8,128)(2,1)S(1)}, u32[]{:S(2)}, u32[]{:S(2)}) collective-permute-start(bf16[4,128,256]{2,1,0:T(8,128)(2,1)S(1)} %get-tuple-element.90), channel_id=1, source_target_pairs={{254,0},{255,1},{0,254},{1,255},{2,4},{3,5},{4,2},{5,3},{6,8},{7,9... | collective-permute-start | bytes 786440 | tf_op jit(solution)/shard_map/ppermute | solution.py:210
  159.7 0.4 collective-permute-start.23
  160.1 7.1 %attend.8 = (bf16[4,128,256]{2,1,0:T(8,128)(2,1)S(1)}, bf16[4,128,256]{2,1,0:T(8,128)(2,1)S(1)}, bf16[4,128,256]{2,1,0:T(8,128)(2,1)S(1)}, bf16[4,128,256]{2,1,0:T(8,128)(2,1)S(1)}) custom-call(s32[5]{0:T(128)S(1)} %pad_add_fusion.info, bf16[128,5120]{1,0:T(8,128)(2,1)S(1)} %copy-done, bf16[128,5120]{1,0:T(8,128)(2,1)S(1)} %copy-done.1, ...), custom_call_target="tpu_custom_call" | custom-call | flops 805306368 | bytes 2097152 | tf_op jit(solution)/shard_map/attend/pallas_call | solution.py:171
  167.2 2.9 %collective-permute-start.18 = (bf16[4,128,256]{2,1,0:T(8,128)(2,1)S(1)}, bf16[4,128,256]{2,1,0:T(8,128)(2,1)S(1)}, u32[]{:S(2)}, u32[]{:S(2)}) collective-permute-start(bf16[4,128,256]{2,1,0:T(8,128)(2,1)S(1)} %get-tuple-element.86), channel_id=1, source_target_pairs={{254,255},{255,254},{0,1},{1,0},{2,3},{3,2},{4,5},{5,4},{6,7},{7,6... | collective-permute-start | bytes 786440 | tf_op jit(solution)/shard_map/ppermute | solution.py:210
  170.1 11.3 %collective-permute-done.26.rest_3_ = bf16[4,128,256]{2,1,0:T(8,128)(2,1)S(1)} collective-permute-done((bf16[4,128,256]{2,1,0:T(8,128)(2,1)S(1)}, bf16[4,128,256]{2,1,0:T(8,128)(2,1)S(1)}, u32[]{:S(2)}, u32[]{:S(2)}) %collective-permute-start.26) | collective-permute-done | bytes 262176 | tf_op jit(solution)/shard_map/ppermute | solution.py:210
  181.5 2.6 %collective-permute-start.20 = (bf16[4,128,256]{2,1,0:T(8,128)(2,1)S(1)}, bf16[4,128,256]{2,1,0:T(8,128)(2,1)S(1)}, u32[]{:S(2)}, u32[]{:S(2)}) collective-permute-start(bf16[4,128,256]{2,1,0:T(8,128)(2,1)S(1)} %get-tuple-element.88), channel_id=1, source_target_pairs={{254,1},{255,0},{0,255},{1,254},{2,5},{3,4},{4,3},{5,2},{6,9},{7,8... | collective-permute-start | bytes 786440 | tf_op jit(solution)/shard_map/ppermute | solution.py:210
  184.1 6.5 %attend.9 = (bf16[4,128,256]{2,1,0:T(8,128)(2,1)S(1)}, bf16[4,128,256]{2,1,0:T(8,128)(2,1)S(1)}, bf16[4,128,256]{2,1,0:T(8,128)(2,1)S(1)}, bf16[4,128,256]{2,1,0:T(8,128)(2,1)S(1)}) custom-call(s32[5]{0:T(128)S(1)} %pad_add_fusion.info, bf16[128,5120]{1,0:T(8,128)(2,1)S(1)} %copy-done, bf16[128,5120]{1,0:T(8,128)(2,1)S(1)} %copy-done.1, ...), custom_call_target="tpu_custom_call" | custom-call | flops 805306368 | bytes 2097152 | tf_op jit(solution)/shard_map/attend/pallas_call | solution.py:171
  190.6 0.2 collective-permute-done.22.rest_2_
  190.8 6.8 %collective-permute-start.17 = (bf16[4,128,256]{2,1,0:T(8,128)(2,1)S(1)}, bf16[4,128,256]{2,1,0:T(8,128)(2,1)S(1)}, u32[]{:S(2)}, u32[]{:S(2)}) collective-permute-start(bf16[4,128,256]{2,1,0:T(8,128)(2,1)S(1)} %get-tuple-element.85), channel_id=1, source_target_pairs={{254,255},{255,254},{0,1},{1,0},{2,3},{3,2},{4,5},{5,4},{6,7},{7,6... | collective-permute-start | bytes 786440 | tf_op jit(solution)/shard_map/ppermute | solution.py:210
  197.6 6.4 %collective-permute-done.23.rest_3_ = bf16[4,128,256]{2,1,0:T(8,128)(2,1)S(1)} collective-permute-done((bf16[4,128,256]{2,1,0:T(8,128)(2,1)S(1)}, bf16[4,128,256]{2,1,0:T(8,128)(2,1)S(1)}, u32[]{:S(2)}, u32[]{:S(2)}) %collective-permute-start.23) | collective-permute-done | bytes 262176 | tf_op jit(solution)/shard_map/ppermute | solution.py:210
  203.9 2.6 %collective-permute-start.15 = (bf16[4,128,256]{2,1,0:T(8,128)(2,1)S(1)}, bf16[4,128,256]{2,1,0:T(8,128)(2,1)S(1)}, u32[]{:S(2)}, u32[]{:S(2)}) collective-permute-start(bf16[4,128,256]{2,1,0:T(8,128)(2,1)S(1)} %get-tuple-element.82), channel_id=1, source_target_pairs={{254,1},{255,0},{0,255},{1,254},{2,5},{3,4},{4,3},{5,2},{6,9},{7,8... | collective-permute-start | bytes 786440 | tf_op jit(solution)/shard_map/ppermute | solution.py:210
  206.6 1.1 unpack.7
  207.7 1.1 unpack.8
  208.8 1.1 unpack.9
  209.9 3.4 %collective-permute-done.19.rest_2_ = bf16[4,128,256]{2,1,0:T(8,128)(2,1)S(1)} collective-permute-done((bf16[4,128,256]{2,1,0:T(8,128)(2,1)S(1)}, bf16[4,128,256]{2,1,0:T(8,128)(2,1)S(1)}, u32[]{:S(2)}, u32[]{:S(2)}) %collective-permute-start.19) | collective-permute-done | bytes 262176 | tf_op jit(solution)/shard_map/ppermute | solution.py:210
  213.3 13.2 %collective-permute-done.20.rest_3_ = bf16[4,128,256]{2,1,0:T(8,128)(2,1)S(1)} collective-permute-done((bf16[4,128,256]{2,1,0:T(8,128)(2,1)S(1)}, bf16[4,128,256]{2,1,0:T(8,128)(2,1)S(1)}, u32[]{:S(2)}, u32[]{:S(2)}) %collective-permute-start.20) | collective-permute-done | bytes 262176 | tf_op jit(solution)/shard_map/ppermute | solution.py:210
  226.5 1.1 unpack.10
  227.6 0.9 unpack.11
  228.4 0.7 unpack.12
  229.2 7.2 %collective-permute-done.15.rest_0_ = bf16[4,128,256]{2,1,0:T(8,128)(2,1)S(1)} collective-permute-done((bf16[4,128,256]{2,1,0:T(8,128)(2,1)S(1)}, bf16[4,128,256]{2,1,0:T(8,128)(2,1)S(1)}, u32[]{:S(2)}, u32[]{:S(2)}) %collective-permute-start.15) | collective-permute-done | bytes 262176 | tf_op jit(solution)/shard_map/ppermute | solution.py:210
  236.3 0.7 unpack.13
  (49 shorter events, 0.4 us)
Async XLA Ops:
  1.9 22.3 %collective-permute-start.12 = (bf16[4,128,256]{2,1,0:T(8,128)(2,1)S(1)}, bf16[4,128,256]{2,1,0:T(8,128)(2,1)S(1)}, u32[]{:S(2)}, u32[]{:S(2)}) collective-permute-start(bf16[4,128,256]{2,1,0:T(8,128)(2,1)S(1)} %get-tuple-element.63.rest_0_), channel_id=1, source_target_pairs={{254,255},{255,0},{0,1},{1,254},{2,3},{3,4},{4,5},{5,2},{6,7},{7,8... | collective-permute-start | bytes 786440 | tf_op jit(solution)/shard_map/ppermute | solution.py:210
  2.2 29.5 %collective-permute-start.13 = (bf16[4,128,256]{2,1,0:T(8,128)(2,1)S(1)}, bf16[4,128,256]{2,1,0:T(8,128)(2,1)S(1)}, u32[]{:S(2)}, u32[]{:S(2)}) collective-permute-start(bf16[4,128,256]{2,1,0:T(8,128)(2,1)S(1)} %get-tuple-element.76), channel_id=1, source_target_pairs={{254,0},{255,1},{0,254},{1,255},{2,4},{3,5},{4,2},{5,3},{6,8},{7,9... | collective-permute-start | bytes 786440 | tf_op jit(solution)/shard_map/ppermute | solution.py:210
  11.4 39.1 %collective-permute-start.14 = (bf16[4,128,256]{2,1,0:T(8,128)(2,1)S(1)}, bf16[4,128,256]{2,1,0:T(8,128)(2,1)S(1)}, u32[]{:S(2)}, u32[]{:S(2)}) collective-permute-start(bf16[4,128,256]{2,1,0:T(8,128)(2,1)S(1)} %get-tuple-element.77), channel_id=1, source_target_pairs={{254,1},{255,254},{0,255},{1,0},{2,5},{3,2},{4,3},{5,4},{6,9},{7,6... | collective-permute-start | bytes 786440 | tf_op jit(solution)/shard_map/ppermute | solution.py:210
  20.7 30.5 %collective-permute-start.9 = (bf16[4,128,256]{2,1,0:T(8,128)(2,1)S(1)}, bf16[4,128,256]{2,1,0:T(8,128)(2,1)S(1)}, u32[]{:S(2)}, u32[]{:S(2)}) collective-permute-start(bf16[4,128,256]{2,1,0:T(8,128)(2,1)S(1)} %get-tuple-element.64.rest_0_), channel_id=1, source_target_pairs={{254,255},{255,254},{0,1},{1,0},{2,3},{3,2},{4,5},{5,4},{6,7},{7,6... | collective-permute-start | bytes 786440 | tf_op jit(solution)/shard_map/ppermute | solution.py:210
  20.8 37.1 %collective-permute-start.10 = (bf16[4,128,256]{2,1,0:T(8,128)(2,1)S(1)}, bf16[4,128,256]{2,1,0:T(8,128)(2,1)S(1)}, u32[]{:S(2)}, u32[]{:S(2)}) collective-permute-start(bf16[4,128,256]{2,1,0:T(8,128)(2,1)S(1)} %get-tuple-element.74), channel_id=1, source_target_pairs={{254,0},{255,1},{0,254},{1,255},{2,4},{3,5},{4,2},{5,3},{6,8},{7,9... | collective-permute-start | bytes 786440 | tf_op jit(solution)/shard_map/ppermute | solution.py:210
  22.0 2.2 copy-start.13
  24.2 45.0 %collective-permute-start.11 = (bf16[4,128,256]{2,1,0:T(8,128)(2,1)}, bf16[4,128,256]{2,1,0:T(8,128)(2,1)}, u32[]{:S(2)}, u32[]{:S(2)}) collective-permute-start(bf16[4,128,256]{2,1,0:T(8,128)(2,1)} %get-tuple-element.75), channel_id=1, source_target_pairs={{254,1},{255,0},{0,255},{1,254},{2,5},{3,4},{4,3},{5,2},{6,9},{7,8... | collective-permute-start | bytes 786440 | tf_op jit(solution)/shard_map/ppermute | solution.py:210
  31.7 17.3 %copy-start.4 = (bf16[4,128,256]{2,1,0:T(8,128)(2,1)}, bf16[4,128,256]{2,1,0:T(8,128)(2,1)S(1)}, u32[]{:S(2)}) copy-start(bf16[4,128,256]{2,1,0:T(8,128)(2,1)S(1)} %collective-permute-done.13.two) | copy-start | bytes 786436
  31.7 37.4 %collective-permute-start.6 = (bf16[4,128,256]{2,1,0:T(8,128)(2,1)}, bf16[4,128,256]{2,1,0:T(8,128)(2,1)}, u32[]{:S(2)}, u32[]{:S(2)}) collective-permute-start(bf16[4,128,256]{2,1,0:T(8,128)(2,1)} %get-tuple-element.65.rest_0_), channel_id=1, source_target_pairs={{254,255},{255,254},{0,1},{1,0},{2,3},{3,2},{4,5},{5,4},{6,7},{7,6... | collective-permute-start | bytes 786440 | tf_op jit(solution)/shard_map/ppermute | solution.py:210
  49.1 0.7 copy-start.9
  49.8 0.7 copy-start.11
  50.5 0.7 copy-start.6
  51.2 27.3 %collective-permute-start.7 = (bf16[4,128,256]{2,1,0:T(8,128)(2,1)}, bf16[4,128,256]{2,1,0:T(8,128)(2,1)}, u32[]{:S(2)}, u32[]{:S(2)}) collective-permute-start(bf16[4,128,256]{2,1,0:T(8,128)(2,1)} %get-tuple-element.72), channel_id=1, source_target_pairs={{254,0},{255,1},{0,254},{1,255},{2,4},{3,5},{4,2},{5,3},{6,8},{7,9... | collective-permute-start | bytes 786440 | tf_op jit(solution)/shard_map/ppermute | solution.py:210
  51.2 40.4 %collective-permute-start.8 = (bf16[4,128,256]{2,1,0:T(8,128)(2,1)}, bf16[4,128,256]{2,1,0:T(8,128)(2,1)}, u32[]{:S(2)}, u32[]{:S(2)}) collective-permute-start(bf16[4,128,256]{2,1,0:T(8,128)(2,1)} %get-tuple-element.73), channel_id=1, source_target_pairs={{254,1},{255,0},{0,255},{1,254},{2,5},{3,4},{4,3},{5,2},{6,9},{7,8... | collective-permute-start | bytes 786440 | tf_op jit(solution)/shard_map/ppermute | solution.py:210
  57.9 33.7 %collective-permute-start.3 = (bf16[4,128,256]{2,1,0:T(8,128)(2,1)}, bf16[4,128,256]{2,1,0:T(8,128)(2,1)}, u32[]{:S(2)}, u32[]{:S(2)}) collective-permute-start(bf16[4,128,256]{2,1,0:T(8,128)(2,1)} %get-tuple-element.66.rest_0_), channel_id=1, source_target_pairs={{254,255},{255,254},{0,1},{1,0},{2,3},{3,2},{4,5},{5,4},{6,7},{7,6... | collective-permute-start | bytes 786440 | tf_op jit(solution)/shard_map/ppermute | solution.py:210
  60.8 33.6 %copy-start = (bf16[128,5120]{1,0:T(8,128)(2,1)S(1)}, bf16[128,5120]{1,0:T(8,128)(2,1)}, u32[]{:S(2)}) copy-start(bf16[128,5120]{1,0:T(8,128)(2,1)} %q_ref.19) | copy-start | bytes 3932164
  60.8 33.6 %copy-start.1 = (bf16[128,5120]{1,0:T(8,128)(2,1)S(1)}, bf16[128,5120]{1,0:T(8,128)(2,1)}, u32[]{:S(2)}) copy-start(bf16[128,5120]{1,0:T(8,128)(2,1)} %k_ref.19) | copy-start | bytes 3932164
  62.2 0.7 copy-start.8
  62.9 0.7 copy-start.10
  63.6 0.7 copy-start.12
  69.2 36.2 %collective-permute-start.4 = (bf16[4,128,256]{2,1,0:T(8,128)(2,1)}, bf16[4,128,256]{2,1,0:T(8,128)(2,1)S(1)}, u32[]{:S(2)}, u32[]{:S(2)}) collective-permute-start(bf16[4,128,256]{2,1,0:T(8,128)(2,1)} %copy-done.11), channel_id=1, source_target_pairs={{254,0},{255,1},{0,254},{1,255},{2,4},{3,5},{4,2},{5,3},{6,8},{7,9... | collective-permute-start | bytes 786440 | tf_op jit(solution)/shard_map/ppermute | solution.py:210
  69.2 44.8 %collective-permute-start.5 = (bf16[4,128,256]{2,1,0:T(8,128)(2,1)}, bf16[4,128,256]{2,1,0:T(8,128)(2,1)S(1)}, u32[]{:S(2)}, u32[]{:S(2)}) collective-permute-start(bf16[4,128,256]{2,1,0:T(8,128)(2,1)} %copy-done.9), channel_id=1, source_target_pairs={{254,1},{255,0},{0,255},{1,254},{2,5},{3,4},{4,3},{5,2},{6,9},{7,8... | collective-permute-start | bytes 786440 | tf_op jit(solution)/shard_map/ppermute | solution.py:210
  78.5 48.8 %collective-permute-start = (bf16[4,128,256]{2,1,0:T(8,128)(2,1)}, bf16[4,128,256]{2,1,0:T(8,128)(2,1)S(1)}, u32[]{:S(2)}, u32[]{:S(2)}) collective-permute-start(bf16[4,128,256]{2,1,0:T(8,128)(2,1)} %copy-done.12), channel_id=1, source_target_pairs={{254,255},{255,254},{0,1},{1,0},{2,3},{3,2},{4,5},{5,4},{6,7},{7,6... | collective-permute-start | bytes 786440 | tf_op jit(solution)/shard_map/ppermute | solution.py:210
  91.6 35.7 %collective-permute-start.1 = (bf16[4,128,256]{2,1,0:T(8,128)(2,1)}, bf16[4,128,256]{2,1,0:T(8,128)(2,1)S(1)}, u32[]{:S(2)}, u32[]{:S(2)}) collective-permute-start(bf16[4,128,256]{2,1,0:T(8,128)(2,1)} %copy-done.10), channel_id=1, source_target_pairs={{254,0},{255,1},{0,254},{1,255},{2,4},{3,5},{4,2},{5,3},{6,8},{7,9... | collective-permute-start | bytes 786440 | tf_op jit(solution)/shard_map/ppermute | solution.py:210
  91.7 44.8 %collective-permute-start.2 = (bf16[4,128,256]{2,1,0:T(8,128)(2,1)}, bf16[4,128,256]{2,1,0:T(8,128)(2,1)S(1)}, u32[]{:S(2)}, u32[]{:S(2)}) collective-permute-start(bf16[4,128,256]{2,1,0:T(8,128)(2,1)} %copy-done.8), channel_id=1, source_target_pairs={{254,1},{255,0},{0,255},{1,254},{2,5},{3,4},{4,3},{5,2},{6,9},{7,8... | collective-permute-start | bytes 786440 | tf_op jit(solution)/shard_map/ppermute | solution.py:210
  94.3 1.3 copy-start.2
  95.7 1.3 copy-start.3
  97.0 0.9 copy-start.5
  97.9 0.9 copy-start.7
  105.4 38.4 %collective-permute-start.27 = (bf16[4,128,256]{2,1,0:T(8,128)(2,1)S(1)}, bf16[4,128,256]{2,1,0:T(8,128)(2,1)S(1)}, u32[]{:S(2)}, u32[]{:S(2)}) collective-permute-start(bf16[4,128,256]{2,1,0:T(8,128)(2,1)S(1)} %get-tuple-element.95), channel_id=1, source_target_pairs={{254,1},{255,254},{0,255},{1,0},{2,5},{3,2},{4,3},{5,4},{6,9},{7,6... | collective-permute-start | bytes 786440 | tf_op jit(solution)/shard_map/ppermute | solution.py:210
  114.0 37.4 %collective-permute-start.28 = (bf16[4,128,256]{2,1,0:T(8,128)(2,1)S(1)}, bf16[4,128,256]{2,1,0:T(8,128)(2,1)S(1)}, u32[]{:S(2)}, u32[]{:S(2)}) collective-permute-start(bf16[4,128,256]{2,1,0:T(8,128)(2,1)S(1)} %get-tuple-element.96), channel_id=1, source_target_pairs={{254,0},{255,1},{0,254},{1,255},{2,4},{3,5},{4,2},{5,3},{6,8},{7,9... | collective-permute-start | bytes 786440 | tf_op jit(solution)/shard_map/ppermute | solution.py:210
  127.3 26.1 %collective-permute-start.29 = (bf16[4,128,256]{2,1,0:T(8,128)(2,1)S(1)}, bf16[4,128,256]{2,1,0:T(8,128)(2,1)S(1)}, u32[]{:S(2)}, u32[]{:S(2)}) collective-permute-start(bf16[4,128,256]{2,1,0:T(8,128)(2,1)S(1)} %get-tuple-element.97), channel_id=1, source_target_pairs={{254,255},{255,0},{0,1},{1,254},{2,3},{3,4},{4,5},{5,2},{6,7},{7,8... | collective-permute-start | bytes 786440 | tf_op jit(solution)/shard_map/ppermute | solution.py:210
  127.4 32.3 %collective-permute-start.24 = (bf16[4,128,256]{2,1,0:T(8,128)(2,1)S(1)}, bf16[4,128,256]{2,1,0:T(8,128)(2,1)S(1)}, u32[]{:S(2)}, u32[]{:S(2)}) collective-permute-start(bf16[4,128,256]{2,1,0:T(8,128)(2,1)S(1)} %get-tuple-element.92), channel_id=1, source_target_pairs={{254,255},{255,254},{0,1},{1,0},{2,3},{3,2},{4,5},{5,4},{6,7},{7,6... | collective-permute-start | bytes 786440 | tf_op jit(solution)/shard_map/ppermute | solution.py:210
  136.5 30.7 %collective-permute-start.25 = (bf16[4,128,256]{2,1,0:T(8,128)(2,1)S(1)}, bf16[4,128,256]{2,1,0:T(8,128)(2,1)S(1)}, u32[]{:S(2)}, u32[]{:S(2)}) collective-permute-start(bf16[4,128,256]{2,1,0:T(8,128)(2,1)S(1)} %get-tuple-element.93), channel_id=1, source_target_pairs={{254,0},{255,1},{0,254},{1,255},{2,4},{3,5},{4,2},{5,3},{6,8},{7,9... | collective-permute-start | bytes 786440 | tf_op jit(solution)/shard_map/ppermute | solution.py:210
  143.8 37.7 %collective-permute-start.26 = (bf16[4,128,256]{2,1,0:T(8,128)(2,1)S(1)}, bf16[4,128,256]{2,1,0:T(8,128)(2,1)S(1)}, u32[]{:S(2)}, u32[]{:S(2)}) collective-permute-start(bf16[4,128,256]{2,1,0:T(8,128)(2,1)S(1)} %get-tuple-element.94), channel_id=1, source_target_pairs={{254,1},{255,0},{0,255},{1,254},{2,5},{3,4},{4,3},{5,2},{6,9},{7,8... | collective-permute-start | bytes 786440 | tf_op jit(solution)/shard_map/ppermute | solution.py:210
  151.5 30.0 %collective-permute-start.21 = (bf16[4,128,256]{2,1,0:T(8,128)(2,1)S(1)}, bf16[4,128,256]{2,1,0:T(8,128)(2,1)S(1)}, u32[]{:S(2)}, u32[]{:S(2)}) collective-permute-start(bf16[4,128,256]{2,1,0:T(8,128)(2,1)S(1)} %get-tuple-element.89), channel_id=1, source_target_pairs={{254,255},{255,254},{0,1},{1,0},{2,3},{3,2},{4,5},{5,4},{6,7},{7,6... | collective-permute-start | bytes 786440 | tf_op jit(solution)/shard_map/ppermute | solution.py:210
  153.4 37.4 %collective-permute-start.22 = (bf16[4,128,256]{2,1,0:T(8,128)(2,1)S(1)}, bf16[4,128,256]{2,1,0:T(8,128)(2,1)S(1)}, u32[]{:S(2)}, u32[]{:S(2)}) collective-permute-start(bf16[4,128,256]{2,1,0:T(8,128)(2,1)S(1)} %get-tuple-element.90), channel_id=1, source_target_pairs={{254,0},{255,1},{0,254},{1,255},{2,4},{3,5},{4,2},{5,3},{6,8},{7,9... | collective-permute-start | bytes 786440 | tf_op jit(solution)/shard_map/ppermute | solution.py:210
  159.7 44.2 %collective-permute-start.23 = (bf16[4,128,256]{2,1,0:T(8,128)(2,1)S(1)}, bf16[4,128,256]{2,1,0:T(8,128)(2,1)S(1)}, u32[]{:S(2)}, u32[]{:S(2)}) collective-permute-start(bf16[4,128,256]{2,1,0:T(8,128)(2,1)S(1)} %get-tuple-element.91), channel_id=1, source_target_pairs={{254,1},{255,0},{0,255},{1,254},{2,5},{3,4},{4,3},{5,2},{6,9},{7,8... | collective-permute-start | bytes 786440 | tf_op jit(solution)/shard_map/ppermute | solution.py:210
  167.2 36.7 %collective-permute-start.18 = (bf16[4,128,256]{2,1,0:T(8,128)(2,1)S(1)}, bf16[4,128,256]{2,1,0:T(8,128)(2,1)S(1)}, u32[]{:S(2)}, u32[]{:S(2)}) collective-permute-start(bf16[4,128,256]{2,1,0:T(8,128)(2,1)S(1)} %get-tuple-element.86), channel_id=1, source_target_pairs={{254,255},{255,254},{0,1},{1,0},{2,3},{3,2},{4,5},{5,4},{6,7},{7,6... | collective-permute-start | bytes 786440 | tf_op jit(solution)/shard_map/ppermute | solution.py:210
  181.5 31.8 %collective-permute-start.19 = (bf16[4,128,256]{2,1,0:T(8,128)(2,1)S(1)}, bf16[4,128,256]{2,1,0:T(8,128)(2,1)S(1)}, u32[]{:S(2)}, u32[]{:S(2)}) collective-permute-start(bf16[4,128,256]{2,1,0:T(8,128)(2,1)S(1)} %get-tuple-element.87), channel_id=1, source_target_pairs={{254,0},{255,1},{0,254},{1,255},{2,4},{3,5},{4,2},{5,3},{6,8},{7,9... | collective-permute-start | bytes 786440 | tf_op jit(solution)/shard_map/ppermute | solution.py:210
  181.5 45.0 %collective-permute-start.20 = (bf16[4,128,256]{2,1,0:T(8,128)(2,1)S(1)}, bf16[4,128,256]{2,1,0:T(8,128)(2,1)S(1)}, u32[]{:S(2)}, u32[]{:S(2)}) collective-permute-start(bf16[4,128,256]{2,1,0:T(8,128)(2,1)S(1)} %get-tuple-element.88), channel_id=1, source_target_pairs={{254,1},{255,0},{0,255},{1,254},{2,5},{3,4},{4,3},{5,2},{6,9},{7,8... | collective-permute-start | bytes 786440 | tf_op jit(solution)/shard_map/ppermute | solution.py:210
  190.8 36.8 %collective-permute-start.17 = (bf16[4,128,256]{2,1,0:T(8,128)(2,1)S(1)}, bf16[4,128,256]{2,1,0:T(8,128)(2,1)S(1)}, u32[]{:S(2)}, u32[]{:S(2)}) collective-permute-start(bf16[4,128,256]{2,1,0:T(8,128)(2,1)S(1)} %get-tuple-element.85), channel_id=1, source_target_pairs={{254,255},{255,254},{0,1},{1,0},{2,3},{3,2},{4,5},{5,4},{6,7},{7,6... | collective-permute-start | bytes 786440 | tf_op jit(solution)/shard_map/ppermute | solution.py:210
  203.9 24.5 %collective-permute-start.16 = (bf16[4,128,256]{2,1,0:T(8,128)(2,1)S(1)}, bf16[4,128,256]{2,1,0:T(8,128)(2,1)S(1)}, u32[]{:S(2)}, u32[]{:S(2)}) collective-permute-start(bf16[4,128,256]{2,1,0:T(8,128)(2,1)S(1)} %get-tuple-element.83), channel_id=1, source_target_pairs={{254,0},{255,1},{0,254},{1,255},{2,4},{3,5},{4,2},{5,3},{6,8},{7,9... | collective-permute-start | bytes 786440 | tf_op jit(solution)/shard_map/ppermute | solution.py:210
  203.9 32.4 %collective-permute-start.15 = (bf16[4,128,256]{2,1,0:T(8,128)(2,1)S(1)}, bf16[4,128,256]{2,1,0:T(8,128)(2,1)S(1)}, u32[]{:S(2)}, u32[]{:S(2)}) collective-permute-start(bf16[4,128,256]{2,1,0:T(8,128)(2,1)S(1)} %get-tuple-element.82), channel_id=1, source_target_pairs={{254,1},{255,0},{0,255},{1,254},{2,5},{3,4},{4,3},{5,2},{6,9},{7,8... | collective-permute-start | bytes 786440 | tf_op jit(solution)/shard_map/ppermute | solution.py:210

commit v3 on v2

--- a/solution.py
+++ b/solution.py
@@ -12,45 +12,41 @@
 MOST = 4
 AXES = ("seq", "uly")
 CHUNKS = (2, 2, 2, 2, 2)
-TURNING = (True, False, False, False, False)
+SWAPS = ((0, 3, 2, 1),) + ((0, 1, 2, 3),) * 4
 LAST = [(0, 1), (2,), (3,)]
 
 
-def partner(place, step, turning):
-    return (place + step) % MOST if turning else place ^ step
-
-
-def routes(step, tiles, turning):
+def routes(swap, tiles):
     def tile_at(window, place):
         return (MOST * window + place - MOST // 2) % tiles
 
     return [
-        (tile_at(window, place), tile_at(window, partner(place, step, turning)))
+        (tile_at(window, place), tile_at(window, place ^ swap))
         for window in range(tiles // MOST)
         for place in range(MOST)
     ]
 
 
-def head_columns(step, turning, begin, heads_each, width):
+def head_columns(swap, begin, heads_each, width):
     place = (lax.axis_index("uly") + MOST // 2) % MOST
-    return pl.ds(pl.multiple_of((partner(place, step, turning) * heads_each + begin) * HD, HD), width)
+    return pl.ds(pl.multiple_of(((place ^ swap) * heads_each + begin) * HD, HD), width)
 
 
 def small_grant():
     return pltpu.CompilerParams(vmem_limit_bytes=16 * 1024 * 1024)
 
 
-def pack_kernel(turning, begin, heads_each, width, q_ref, k_ref, v_ref, g_ref, *rest):
+def pack_kernel(swaps, begin, heads_each, width, q_ref, k_ref, v_ref, g_ref, *rest):
     outs, sems = rest[-4:-1], rest[-1]
     copies = []
-    for step in range(1, MOST):
-        columns = head_columns(step, turning, begin, heads_each, width)
+    for out, swap in enumerate(swaps[1:]):
+        columns = head_columns(swap, begin, heads_each, width)
         for member, source in enumerate((q_ref, k_ref, v_ref, g_ref)):
             copies.append(
                 pltpu.make_async_copy(
                     source.at[:, columns],
-                    outs[step - 1].at[member],
-                    sems.at[step - 1, member],
+                    outs[out].at[member],
+                    sems.at[out, member],
                 )
             )
     for copy in copies:
@@ -59,12 +55,12 @@
         copy.wait()
 
 
-def pack(turning, arrays, after, begin, heads, heads_each):
+def pack(swaps, arrays, after, begin, heads, heads_each):
     width = heads * HD
     piece = pltpu.VMEM((4, TILE, width), jnp.bfloat16)
     arrays = [pltpu.with_memory_space_constraint(array, pltpu.HBM) for array in arrays]
     return pl.pallas_call(
-        partial(pack_kernel, turning, begin, heads_each, width),
+        partial(pack_kernel, swaps, begin, heads_each, width),
         out_shape=(piece,) * 3,
         in_specs=[pl.BlockSpec(memory_space=pl.ANY)] * (4 + len(after)),
         out_specs=(pl.BlockSpec(memory_space=pltpu.VMEM),) * 3,
@@ -75,12 +71,12 @@
     )(*arrays, *after)
 
 
-def unpack_kernel(turning, steps, begin, heads_each, width, *rest):
-    pieces = rest[: len(steps)]
+def unpack_kernel(swaps, begin, heads_each, width, *rest):
+    pieces = rest[: len(swaps)]
     outs, sems = rest[-5:-1], rest[-1]
     copies = []
-    for index, step in enumerate(steps):
-        columns = head_columns(step, turning, begin, heads_each, width)
+    for index, swap in enumerate(swaps):
+        columns = head_columns(swap, begin, heads_each, width)
         for member, target in enumerate(outs):
             copies.append(
                 pltpu.make_async_copy(
@@ -95,19 +91,19 @@
         copy.wait()
 
 
-def unpack(turning, steps, pieces, held, begin, heads, heads_each, columns):
+def unpack(swaps, pieces, held, begin, heads, heads_each, columns):
     width = heads * HD
     whole = jax.ShapeDtypeStruct((TILE, columns), jnp.bfloat16)
     return pl.pallas_call(
-        partial(unpack_kernel, turning, steps, begin, heads_each, width),
+        partial(unpack_kernel, swaps, begin, heads_each, width),
         out_shape=(whole,) * 4,
-        in_specs=[pl.BlockSpec(memory_space=pltpu.VMEM)] * len(steps)
+        in_specs=[pl.BlockSpec(memory_space=pltpu.VMEM)] * len(swaps)
         + [pl.BlockSpec(memory_space=pl.ANY)] * len(held),
         out_specs=(pl.BlockSpec(memory_space=pl.ANY),) * 4,
-        scratch_shapes=[pltpu.SemaphoreType.DMA((len(steps), 4))],
+        scratch_shapes=[pltpu.SemaphoreType.DMA((len(swaps), 4))],
         compiler_params=small_grant(),
-        input_output_aliases={len(steps) + i: i for i in range(len(held))},
-        cost_estimate=pl.CostEstimate(flops=0, bytes_accessed=8 * len(steps) * TILE * width * 2, transcendentals=0),
+        input_output_aliases={len(swaps) + i: i for i in range(len(held))},
+        cost_estimate=pl.CostEstimate(flops=0, bytes_accessed=8 * len(swaps) * TILE * width * 2, transcendentals=0),
         name="unpack",
     )(*pieces, *held)
 
@@ -198,35 +194,31 @@
     place = (device + MOST // 2) % MOST
     firsts = jnp.arange(tiles, dtype=jnp.int32) - tile_offset
 
-    def describe(turning):
-        slots = jnp.arange(MOST)
-        sources = (place - slots) % MOST if turning else place ^ slots
+    def describe(swaps):
+        sources = place ^ jnp.array(swaps)
         return jnp.concatenate((place[None], firsts[(device - place + sources + tiles) % tiles])).astype(jnp.int32)
 
-    infos = {turning: describe(turning) for turning in set(TURNING)}
-
-    def exchange(pieces, turning, sign):
-        return [
-            lax.ppermute(piece, AXES, routes(sign * step if turning else step, tiles, turning))
-            for step, piece in zip((1, 2, 3), pieces)
-        ]
+    infos = {swaps: describe(swaps) for swaps in dict.fromkeys(SWAPS)}
+
+    def exchange(pieces, swaps):
+        return [lax.ppermute(piece, AXES, routes(swap, tiles)) for swap, piece in zip(swaps[1:], pieces)]
 
     begins = [sum(CHUNKS[:i]) for i in range(len(CHUNKS))]
     received, after = [], ()
-    for turning, begin, heads in zip(TURNING, begins, CHUNKS):
-        pieces = pack(turning, arrays, after, begin, heads, heads_each)
+    for swaps, begin, heads in zip(SWAPS, begins, CHUNKS):
+        pieces = pack(swaps, arrays, after, begin, heads, heads_each)
         after = pieces[:1]
-        received.append(exchange(pieces, turning, 1))
+        received.append(exchange(pieces, swaps))
     results, after = [], ()
-    for turning, begin, heads, pieces in zip(TURNING, begins, CHUNKS, received):
-        own, *others = attend(infos[turning], arrays, pieces, after, begin, heads, heads_each)
+    for swaps, begin, heads, pieces in zip(SWAPS, begins, CHUNKS, received):
+        own, *others = attend(infos[swaps], arrays, pieces, after, begin, heads, heads_each)
         after = (own,)
-        results.append((own, *exchange(others, turning, -1)))
+        results.append((own, *exchange(others, swaps)))
     held = ()
-    for index, (turning, begin, heads, pieces) in enumerate(zip(TURNING, begins, CHUNKS, results)):
+    for index, (swaps, begin, heads, pieces) in enumerate(zip(SWAPS, begins, CHUNKS, results)):
         for steps in [(0, 1, 2, 3)] if index < len(CHUNKS) - 1 else LAST:
-            parts = [pieces[step] for step in steps]
-            held = unpack(turning, steps, parts, held, begin, heads, heads_each, columns)
+            parts, to = [pieces[step] for step in steps], [swaps[step] for step in steps]
+            held = unpack(to, parts, held, begin, heads, heads_each, columns)
     return tuple(held)
 
 

time: 238 us -> 237 us (level)
  starting transfers between devices: 99.9 us -> 85.5 us
  waiting for transfers between devices: 75.9 us -> 90 us
    ppermute x30, starting transfers between devices: 99.9 us -> 85.5 us  [exchange(): lax.ppermute(piece, AXES, routes(swap, tiles))]
    ppermute x30, waiting for transfers between devices: 75.9 us -> 90 us  [exchange(): lax.ppermute(piece, AXES, routes(swap, tiles))]
    unnamed x28 -> x30, local copies, waits for them, and re-layouts: 8.78 us -> 8.76 us
  transfers between devices with their start and end apart: 30 -> 30, of which waited for: 12 -> 16; matrix products, arithmetic and copies ran while one was open for 1% -> 1% of each run, Pallas kernels for 20% -> 20%
where the time goes in v3:
time: 237 us
  waiting for transfers between devices  90 us (38%)
  starting transfers between devices  85.5 us (36%)
  Pallas kernels  50 us (21%)
  local copies, waits for them, and re-layouts  10 us (4%)
    ppermute x30, waiting for transfers between devices, exchange(): lax.ppermute(piece, AXES, routes(swap, tiles))  90 us
    ppermute x30, starting transfers between devices, exchange(): lax.ppermute(piece, AXES, routes(swap, tiles))  85.5 us
    pallas_call x5, Pallas kernels, attend(): pl.pallas_call(attend_kernel, out_shape=(piece,) * 4, grid_spec=pltpu.Pre...  34.5 us
    pallas_call x5, Pallas kernels, pack(): pl.pallas_call(partial(pack_kernel, swaps, begin, heads_each, width), out...  8.83 us
    unnamed x30, local copies, waits for them, and re-layouts  8.76 us
    pallas_call x7, Pallas kernels, unpack(): pl.pallas_call(partial(unpack_kernel, swaps, begin, heads_each, width), o...  6.71 us
  transfers between devices with their start and end apart: 30, of which 16 were waited for; matrix products, arithmetic and copies ran while one was open for 1% of the time, Pallas kernels for 20%

profile of v3, /device:TPU:0, one launch (start us, length us, event | category | flops | bytes accessed | tf_op | source)
XLA Modules:
  0.0 236.8 jit_solution(16348154208219807415)
XLA Ops:
  0.6 1.3 pack.5
  1.9 8.3 %collective-permute-start.12 = (bf16[4,128,256]{2,1,0:T(8,128)(2,1)S(1)}, bf16[4,128,256]{2,1,0:T(8,128)(2,1)S(1)}, u32[]{:S(2)}, u32[]{:S(2)}) collective-permute-start(bf16[4,128,256]{2,1,0:T(8,128)(2,1)S(1)} %get-tuple-element.63.rest_0_), channel_id=1, source_target_pairs={{254,1},{255,0},{0,255},{1,254},{2,5},{3,4},{4,3},{5,2},{6,9},{7,8... | collective-permute-start | bytes 786440 | tf_op jit(solution)/shard_map/ppermute | solution.py:204
  10.8 1.4 collective-permute-start.14
  12.1 2.0 pack.6
  14.1 0.7 collective-permute-start.9
  14.9 7.2 %collective-permute-start.10 = (bf16[4,128,256]{2,1,0:T(8,128)(2,1)S(1)}, bf16[4,128,256]{2,1,0:T(8,128)(2,1)S(1)}, u32[]{:S(2)}, u32[]{:S(2)}) collective-permute-start(bf16[4,128,256]{2,1,0:T(8,128)(2,1)S(1)} %get-tuple-element.74), channel_id=1, source_target_pairs={{254,0},{255,1},{0,254},{1,255},{2,4},{3,5},{4,2},{5,3},{6,8},{7,9... | collective-permute-start | bytes 786440 | tf_op jit(solution)/shard_map/ppermute | solution.py:204
  22.1 2.2 pack.7
  24.3 3.5 %collective-permute-done.12.one = bf16[4,128,256]{2,1,0:T(8,128)(2,1)S(1)} collective-permute-done((bf16[4,128,256]{2,1,0:T(8,128)(2,1)S(1)}, bf16[4,128,256]{2,1,0:T(8,128)(2,1)S(1)}, u32[]{:S(2)}, u32[]{:S(2)}) %collective-permute-start.12) | collective-permute-done | bytes 262176 | tf_op jit(solution)/shard_map/ppermute | solution.py:204
  27.8 4.5 %collective-permute-start.11 = (bf16[4,128,256]{2,1,0:T(8,128)(2,1)}, bf16[4,128,256]{2,1,0:T(8,128)(2,1)}, u32[]{:S(2)}, u32[]{:S(2)}) collective-permute-start(bf16[4,128,256]{2,1,0:T(8,128)(2,1)} %get-tuple-element.75), channel_id=1, source_target_pairs={{254,1},{255,0},{0,255},{1,254},{2,5},{3,4},{4,3},{5,2},{6,9},{7,8... | collective-permute-start | bytes 786440 | tf_op jit(solution)/shard_map/ppermute | solution.py:204
  32.3 2.6 %collective-permute-done.13.two = bf16[4,128,256]{2,1,0:T(8,128)(2,1)S(1)} collective-permute-done((bf16[4,128,256]{2,1,0:T(8,128)(2,1)S(1)}, bf16[4,128,256]{2,1,0:T(8,128)(2,1)S(1)}, u32[]{:S(2)}, u32[]{:S(2)}) %collective-permute-start.13) | collective-permute-done | bytes 262176 | tf_op jit(solution)/shard_map/ppermute | solution.py:204
  34.9 0.9 collective-permute-start.6
  35.9 2.0 pack.8
  37.9 0.7 copy-done.9
  38.6 0.7 copy-done.11
  39.3 0.7 copy-done.6
  40.0 9.7 %collective-permute-start.7 = (bf16[4,128,256]{2,1,0:T(8,128)(2,1)}, bf16[4,128,256]{2,1,0:T(8,128)(2,1)}, u32[]{:S(2)}, u32[]{:S(2)}) collective-permute-start(bf16[4,128,256]{2,1,0:T(8,128)(2,1)} %get-tuple-element.72), channel_id=1, source_target_pairs={{254,0},{255,1},{0,254},{1,255},{2,4},{3,5},{4,2},{5,3},{6,8},{7,9... | collective-permute-start | bytes 786440 | tf_op jit(solution)/shard_map/ppermute | solution.py:204
  49.9 1.8 collective-permute-done.10.two
  51.7 1.0 collective-permute-start.3
  52.8 1.4 pack.9
  54.2 0.7 copy-done.8
  54.9 0.7 copy-done.10
  55.6 0.7 copy-done.12
  57.6 9.7 %collective-permute-done.11.three = bf16[4,128,256]{2,1,0:T(8,128)(2,1)} collective-permute-done((bf16[4,128,256]{2,1,0:T(8,128)(2,1)}, bf16[4,128,256]{2,1,0:T(8,128)(2,1)}, u32[]{:S(2)}, u32[]{:S(2)}) %collective-permute-start.11) | collective-permute-done | bytes 262176 | tf_op jit(solution)/shard_map/ppermute | solution.py:204
  67.3 4.5 %collective-permute-start.5 = (bf16[4,128,256]{2,1,0:T(8,128)(2,1)}, bf16[4,128,256]{2,1,0:T(8,128)(2,1)S(1)}, u32[]{:S(2)}, u32[]{:S(2)}) collective-permute-start(bf16[4,128,256]{2,1,0:T(8,128)(2,1)} %copy-done.9), channel_id=1, source_target_pairs={{254,1},{255,0},{0,255},{1,254},{2,5},{3,4},{4,3},{5,2},{6,9},{7,8... | collective-permute-start | bytes 786440 | tf_op jit(solution)/shard_map/ppermute | solution.py:204
  71.8 9.3 %collective-permute-done.7.two = bf16[4,128,256]{2,1,0:T(8,128)(2,1)} collective-permute-done((bf16[4,128,256]{2,1,0:T(8,128)(2,1)}, bf16[4,128,256]{2,1,0:T(8,128)(2,1)}, u32[]{:S(2)}, u32[]{:S(2)}) %collective-permute-start.7) | collective-permute-done | bytes 262176 | tf_op jit(solution)/shard_map/ppermute | solution.py:204
  81.2 8.6 %collective-permute-done.8.three = bf16[4,128,256]{2,1,0:T(8,128)(2,1)} collective-permute-done((bf16[4,128,256]{2,1,0:T(8,128)(2,1)}, bf16[4,128,256]{2,1,0:T(8,128)(2,1)}, u32[]{:S(2)}, u32[]{:S(2)}) %collective-permute-start.8) | collective-permute-done | bytes 262176 | tf_op jit(solution)/shard_map/ppermute | solution.py:204
  89.8 4.5 %collective-permute-start.2 = (bf16[4,128,256]{2,1,0:T(8,128)(2,1)}, bf16[4,128,256]{2,1,0:T(8,128)(2,1)S(1)}, u32[]{:S(2)}, u32[]{:S(2)}) collective-permute-start(bf16[4,128,256]{2,1,0:T(8,128)(2,1)} %copy-done.8), channel_id=1, source_target_pairs={{254,1},{255,0},{0,255},{1,254},{2,5},{3,4},{4,3},{5,2},{6,9},{7,8... | collective-permute-start | bytes 786440 | tf_op jit(solution)/shard_map/ppermute | solution.py:204
  94.4 1.3 copy-done.2
  95.7 1.3 copy-done.3
  97.0 0.9 copy-done.5
  97.9 0.9 copy-done.7
  98.9 6.5 %attend.5 = (bf16[4,128,256]{2,1,0:T(8,128)(2,1)S(1)}, bf16[4,128,256]{2,1,0:T(8,128)(2,1)S(1)}, bf16[4,128,256]{2,1,0:T(8,128)(2,1)S(1)}, bf16[4,128,256]{2,1,0:T(8,128)(2,1)S(1)}) custom-call(s32[5]{0:T(128)S(1)} %pad_add_fusion.1.info, bf16[128,5120]{1,0:T(8,128)(2,1)S(1)} %copy-done, bf16[128,5120]{1,0:T(8,128)(2,1)S(1)} %copy-done.1, ...), custom_call_target="tpu_custom_call" | custom-call | flops 805306368 | bytes 2097152 | tf_op jit(solution)/shard_map/attend/pallas_call | solution.py:167
  105.4 2.8 %collective-permute-start.27 = (bf16[4,128,256]{2,1,0:T(8,128)(2,1)S(1)}, bf16[4,128,256]{2,1,0:T(8,128)(2,1)S(1)}, u32[]{:S(2)}, u32[]{:S(2)}) collective-permute-start(bf16[4,128,256]{2,1,0:T(8,128)(2,1)S(1)} %get-tuple-element.95), channel_id=1, source_target_pairs={{254,1},{255,0},{0,255},{1,254},{2,5},{3,4},{4,3},{5,2},{6,9},{7,8... | collective-permute-start | bytes 786440 | tf_op jit(solution)/shard_map/ppermute | solution.py:204
  108.2 4.1 %collective-permute-done.5.three = bf16[4,128,256]{2,1,0:T(8,128)(2,1)S(1)} collective-permute-done((bf16[4,128,256]{2,1,0:T(8,128)(2,1)}, bf16[4,128,256]{2,1,0:T(8,128)(2,1)S(1)}, u32[]{:S(2)}, u32[]{:S(2)}) %collective-permute-start.5) | collective-permute-done | bytes 262176 | tf_op jit(solution)/shard_map/ppermute | solution.py:204
  112.2 5.8 %collective-permute-start.28 = (bf16[4,128,256]{2,1,0:T(8,128)(2,1)S(1)}, bf16[4,128,256]{2,1,0:T(8,128)(2,1)S(1)}, u32[]{:S(2)}, u32[]{:S(2)}) collective-permute-start(bf16[4,128,256]{2,1,0:T(8,128)(2,1)S(1)} %get-tuple-element.96), channel_id=1, source_target_pairs={{254,0},{255,1},{0,254},{1,255},{2,4},{3,5},{4,2},{5,3},{6,8},{7,9... | collective-permute-start | bytes 786440 | tf_op jit(solution)/shard_map/ppermute | solution.py:204
  118.0 7.2 %attend.6 = (bf16[4,128,256]{2,1,0:T(8,128)(2,1)S(1)}, bf16[4,128,256]{2,1,0:T(8,128)(2,1)S(1)}, bf16[4,128,256]{2,1,0:T(8,128)(2,1)S(1)}, bf16[4,128,256]{2,1,0:T(8,128)(2,1)S(1)}) custom-call(s32[5]{0:T(128)S(1)} %pad_add_fusion.info, bf16[128,5120]{1,0:T(8,128)(2,1)S(1)} %copy-done, bf16[128,5120]{1,0:T(8,128)(2,1)S(1)} %copy-done.1, ...), custom_call_target="tpu_custom_call" | custom-call | flops 805306368 | bytes 2097152 | tf_op jit(solution)/shard_map/attend/pallas_call | solution.py:167
  125.2 3.0 %collective-permute-start.29 = (bf16[4,128,256]{2,1,0:T(8,128)(2,1)S(1)}, bf16[4,128,256]{2,1,0:T(8,128)(2,1)S(1)}, u32[]{:S(2)}, u32[]{:S(2)}) collective-permute-start(bf16[4,128,256]{2,1,0:T(8,128)(2,1)S(1)} %get-tuple-element.97), channel_id=1, source_target_pairs={{254,255},{255,254},{0,1},{1,0},{2,3},{3,2},{4,5},{5,4},{6,7},{7,6... | collective-permute-start | bytes 786440 | tf_op jit(solution)/shard_map/ppermute | solution.py:204
  128.2 2.4 %collective-permute-start.24 = (bf16[4,128,256]{2,1,0:T(8,128)(2,1)S(1)}, bf16[4,128,256]{2,1,0:T(8,128)(2,1)S(1)}, u32[]{:S(2)}, u32[]{:S(2)}) collective-permute-start(bf16[4,128,256]{2,1,0:T(8,128)(2,1)S(1)} %get-tuple-element.92), channel_id=1, source_target_pairs={{254,255},{255,254},{0,1},{1,0},{2,3},{3,2},{4,5},{5,4},{6,7},{7,6... | collective-permute-start | bytes 786440 | tf_op jit(solution)/shard_map/ppermute | solution.py:204
  130.6 4.1 %collective-permute-done.2.three = bf16[4,128,256]{2,1,0:T(8,128)(2,1)S(1)} collective-permute-done((bf16[4,128,256]{2,1,0:T(8,128)(2,1)}, bf16[4,128,256]{2,1,0:T(8,128)(2,1)S(1)}, u32[]{:S(2)}, u32[]{:S(2)}) %collective-permute-start.2) | collective-permute-done | bytes 262176 | tf_op jit(solution)/shard_map/ppermute | solution.py:204
  134.6 7.2 %attend.7 = (bf16[4,128,256]{2,1,0:T(8,128)(2,1)S(1)}, bf16[4,128,256]{2,1,0:T(8,128)(2,1)S(1)}, bf16[4,128,256]{2,1,0:T(8,128)(2,1)S(1)}, bf16[4,128,256]{2,1,0:T(8,128)(2,1)S(1)}) custom-call(s32[5]{0:T(128)S(1)} %pad_add_fusion.info, bf16[128,5120]{1,0:T(8,128)(2,1)S(1)} %copy-done, bf16[128,5120]{1,0:T(8,128)(2,1)S(1)} %copy-done.1, ...), custom_call_target="tpu_custom_call" | custom-call | flops 805306368 | bytes 2097152 | tf_op jit(solution)/shard_map/attend/pallas_call | solution.py:167
  141.9 5.7 %collective-permute-start.26 = (bf16[4,128,256]{2,1,0:T(8,128)(2,1)S(1)}, bf16[4,128,256]{2,1,0:T(8,128)(2,1)S(1)}, u32[]{:S(2)}, u32[]{:S(2)}) collective-permute-start(bf16[4,128,256]{2,1,0:T(8,128)(2,1)S(1)} %get-tuple-element.94), channel_id=1, source_target_pairs={{254,1},{255,0},{0,255},{1,254},{2,5},{3,4},{4,3},{5,2},{6,9},{7,8... | collective-permute-start | bytes 786440 | tf_op jit(solution)/shard_map/ppermute | solution.py:204
  147.5 3.9 %collective-permute-done.28.rest_2_ = bf16[4,128,256]{2,1,0:T(8,128)(2,1)S(1)} collective-permute-done((bf16[4,128,256]{2,1,0:T(8,128)(2,1)S(1)}, bf16[4,128,256]{2,1,0:T(8,128)(2,1)S(1)}, u32[]{:S(2)}, u32[]{:S(2)}) %collective-permute-start.28) | collective-permute-done | bytes 262176 | tf_op jit(solution)/shard_map/ppermute | solution.py:204
  151.4 1.5 collective-permute-start.21
  152.9 6.7 %collective-permute-start.22 = (bf16[4,128,256]{2,1,0:T(8,128)(2,1)S(1)}, bf16[4,128,256]{2,1,0:T(8,128)(2,1)S(1)}, u32[]{:S(2)}, u32[]{:S(2)}) collective-permute-start(bf16[4,128,256]{2,1,0:T(8,128)(2,1)S(1)} %get-tuple-element.90), channel_id=1, source_target_pairs={{254,0},{255,1},{0,254},{1,255},{2,4},{3,5},{4,2},{5,3},{6,8},{7,9... | collective-permute-start | bytes 786440 | tf_op jit(solution)/shard_map/ppermute | solution.py:204
  160.1 7.1 %attend.8 = (bf16[4,128,256]{2,1,0:T(8,128)(2,1)S(1)}, bf16[4,128,256]{2,1,0:T(8,128)(2,1)S(1)}, bf16[4,128,256]{2,1,0:T(8,128)(2,1)S(1)}, bf16[4,128,256]{2,1,0:T(8,128)(2,1)S(1)}) custom-call(s32[5]{0:T(128)S(1)} %pad_add_fusion.info, bf16[128,5120]{1,0:T(8,128)(2,1)S(1)} %copy-done, bf16[128,5120]{1,0:T(8,128)(2,1)S(1)} %copy-done.1, ...), custom_call_target="tpu_custom_call" | custom-call | flops 805306368 | bytes 2097152 | tf_op jit(solution)/shard_map/attend/pallas_call | solution.py:167
  167.2 2.5 %collective-permute-start.18 = (bf16[4,128,256]{2,1,0:T(8,128)(2,1)S(1)}, bf16[4,128,256]{2,1,0:T(8,128)(2,1)S(1)}, u32[]{:S(2)}, u32[]{:S(2)}) collective-permute-start(bf16[4,128,256]{2,1,0:T(8,128)(2,1)S(1)} %get-tuple-element.86), channel_id=1, source_target_pairs={{254,255},{255,254},{0,1},{1,0},{2,3},{3,2},{4,5},{5,4},{6,7},{7,6... | collective-permute-start | bytes 786440 | tf_op jit(solution)/shard_map/ppermute | solution.py:204
  169.7 9.9 %collective-permute-done.26.rest_3_ = bf16[4,128,256]{2,1,0:T(8,128)(2,1)S(1)} collective-permute-done((bf16[4,128,256]{2,1,0:T(8,128)(2,1)S(1)}, bf16[4,128,256]{2,1,0:T(8,128)(2,1)S(1)}, u32[]{:S(2)}, u32[]{:S(2)}) %collective-permute-start.26) | collective-permute-done | bytes 262176 | tf_op jit(solution)/shard_map/ppermute | solution.py:204
  179.6 4.5 %collective-permute-start.20 = (bf16[4,128,256]{2,1,0:T(8,128)(2,1)S(1)}, bf16[4,128,256]{2,1,0:T(8,128)(2,1)S(1)}, u32[]{:S(2)}, u32[]{:S(2)}) collective-permute-start(bf16[4,128,256]{2,1,0:T(8,128)(2,1)S(1)} %get-tuple-element.88), channel_id=1, source_target_pairs={{254,1},{255,0},{0,255},{1,254},{2,5},{3,4},{4,3},{5,2},{6,9},{7,8... | collective-permute-start | bytes 786440 | tf_op jit(solution)/shard_map/ppermute | solution.py:204
  184.1 6.5 %attend.9 = (bf16[4,128,256]{2,1,0:T(8,128)(2,1)S(1)}, bf16[4,128,256]{2,1,0:T(8,128)(2,1)S(1)}, bf16[4,128,256]{2,1,0:T(8,128)(2,1)S(1)}, bf16[4,128,256]{2,1,0:T(8,128)(2,1)S(1)}) custom-call(s32[5]{0:T(128)S(1)} %pad_add_fusion.info, bf16[128,5120]{1,0:T(8,128)(2,1)S(1)} %copy-done, bf16[128,5120]{1,0:T(8,128)(2,1)S(1)} %copy-done.1, ...), custom_call_target="tpu_custom_call" | custom-call | flops 805306368 | bytes 2097152 | tf_op jit(solution)/shard_map/attend/pallas_call | solution.py:167
  190.6 2.9 %collective-permute-done.22.rest_2_ = bf16[4,128,256]{2,1,0:T(8,128)(2,1)S(1)} collective-permute-done((bf16[4,128,256]{2,1,0:T(8,128)(2,1)S(1)}, bf16[4,128,256]{2,1,0:T(8,128)(2,1)S(1)}, u32[]{:S(2)}, u32[]{:S(2)}) %collective-permute-start.22) | collective-permute-done | bytes 262176 | tf_op jit(solution)/shard_map/ppermute | solution.py:204
  193.5 2.2 collective-permute-start.17
  195.7 6.4 %collective-permute-done.23.rest_3_ = bf16[4,128,256]{2,1,0:T(8,128)(2,1)S(1)} collective-permute-done((bf16[4,128,256]{2,1,0:T(8,128)(2,1)S(1)}, bf16[4,128,256]{2,1,0:T(8,128)(2,1)S(1)}, u32[]{:S(2)}, u32[]{:S(2)}) %collective-permute-start.23) | collective-permute-done | bytes 262176 | tf_op jit(solution)/shard_map/ppermute | solution.py:204
  202.1 4.5 %collective-permute-start.15 = (bf16[4,128,256]{2,1,0:T(8,128)(2,1)S(1)}, bf16[4,128,256]{2,1,0:T(8,128)(2,1)S(1)}, u32[]{:S(2)}, u32[]{:S(2)}) collective-permute-start(bf16[4,128,256]{2,1,0:T(8,128)(2,1)S(1)} %get-tuple-element.82), channel_id=1, source_target_pairs={{254,1},{255,0},{0,255},{1,254},{2,5},{3,4},{4,3},{5,2},{6,9},{7,8... | collective-permute-start | bytes 786440 | tf_op jit(solution)/shard_map/ppermute | solution.py:204
  206.6 1.1 unpack.7
  207.7 1.1 unpack.8
  208.8 1.1 unpack.9
  209.9 6.0 %collective-permute-done.19.rest_2_ = bf16[4,128,256]{2,1,0:T(8,128)(2,1)S(1)} collective-permute-done((bf16[4,128,256]{2,1,0:T(8,128)(2,1)S(1)}, bf16[4,128,256]{2,1,0:T(8,128)(2,1)S(1)}, u32[]{:S(2)}, u32[]{:S(2)}) %collective-permute-start.19) | collective-permute-done | bytes 262176 | tf_op jit(solution)/shard_map/ppermute | solution.py:204
  215.9 8.7 %collective-permute-done.20.rest_3_ = bf16[4,128,256]{2,1,0:T(8,128)(2,1)S(1)} collective-permute-done((bf16[4,128,256]{2,1,0:T(8,128)(2,1)S(1)}, bf16[4,128,256]{2,1,0:T(8,128)(2,1)S(1)}, u32[]{:S(2)}, u32[]{:S(2)}) %collective-permute-start.20) | collective-permute-done | bytes 262176 | tf_op jit(solution)/shard_map/ppermute | solution.py:204
  224.6 1.1 unpack.10
  225.7 0.9 unpack.11
  226.6 0.7 collective-permute-done.16.rest_0_
  227.3 0.7 unpack.12
  228.0 7.8 %collective-permute-done.15.rest_0_ = bf16[4,128,256]{2,1,0:T(8,128)(2,1)S(1)} collective-permute-done((bf16[4,128,256]{2,1,0:T(8,128)(2,1)S(1)}, bf16[4,128,256]{2,1,0:T(8,128)(2,1)S(1)}, u32[]{:S(2)}, u32[]{:S(2)}) %collective-permute-start.15) | collective-permute-done | bytes 262176 | tf_op jit(solution)/shard_map/ppermute | solution.py:204
  235.9 0.7 unpack.13
  (51 shorter events, 2.7 us)
Async XLA Ops:
  1.9 25.9 %collective-permute-start.12 = (bf16[4,128,256]{2,1,0:T(8,128)(2,1)S(1)}, bf16[4,128,256]{2,1,0:T(8,128)(2,1)S(1)}, u32[]{:S(2)}, u32[]{:S(2)}) collective-permute-start(bf16[4,128,256]{2,1,0:T(8,128)(2,1)S(1)} %get-tuple-element.63.rest_0_), channel_id=1, source_target_pairs={{254,1},{255,0},{0,255},{1,254},{2,5},{3,4},{4,3},{5,2},{6,9},{7,8... | collective-permute-start | bytes 786440 | tf_op jit(solution)/shard_map/ppermute | solution.py:204
  10.2 24.7 %collective-permute-start.13 = (bf16[4,128,256]{2,1,0:T(8,128)(2,1)S(1)}, bf16[4,128,256]{2,1,0:T(8,128)(2,1)S(1)}, u32[]{:S(2)}, u32[]{:S(2)}) collective-permute-start(bf16[4,128,256]{2,1,0:T(8,128)(2,1)S(1)} %get-tuple-element.76), channel_id=1, source_target_pairs={{254,0},{255,1},{0,254},{1,255},{2,4},{3,5},{4,2},{5,3},{6,8},{7,9... | collective-permute-start | bytes 786440 | tf_op jit(solution)/shard_map/ppermute | solution.py:204
  10.8 11.3 %copy-start.13 = (s32[256]{0:T(256)S(1)}, s32[256]{0:T(256)}, u32[]{:S(2)}) copy-start(s32[256]{0:T(256)} %param.11) | copy-start | bytes 3076
  10.8 28.5 %collective-permute-start.14 = (bf16[4,128,256]{2,1,0:T(8,128)(2,1)S(1)}, bf16[4,128,256]{2,1,0:T(8,128)(2,1)S(1)}, u32[]{:S(2)}, u32[]{:S(2)}) collective-permute-start(bf16[4,128,256]{2,1,0:T(8,128)(2,1)S(1)} %get-tuple-element.77), channel_id=1, source_target_pairs={{254,255},{255,254},{0,1},{1,0},{2,3},{3,2},{4,5},{5,4},{6,7},{7,6... | collective-permute-start | bytes 786440 | tf_op jit(solution)/shard_map/ppermute | solution.py:204
  14.1 35.6 %collective-permute-start.9 = (bf16[4,128,256]{2,1,0:T(8,128)(2,1)S(1)}, bf16[4,128,256]{2,1,0:T(8,128)(2,1)S(1)}, u32[]{:S(2)}, u32[]{:S(2)}) collective-permute-start(bf16[4,128,256]{2,1,0:T(8,128)(2,1)S(1)} %get-tuple-element.64.rest_0_), channel_id=1, source_target_pairs={{254,255},{255,254},{0,1},{1,0},{2,3},{3,2},{4,5},{5,4},{6,7},{7,6... | collective-permute-start | bytes 786440 | tf_op jit(solution)/shard_map/ppermute | solution.py:204
  14.9 36.9 %collective-permute-start.10 = (bf16[4,128,256]{2,1,0:T(8,128)(2,1)S(1)}, bf16[4,128,256]{2,1,0:T(8,128)(2,1)S(1)}, u32[]{:S(2)}, u32[]{:S(2)}) collective-permute-start(bf16[4,128,256]{2,1,0:T(8,128)(2,1)S(1)} %get-tuple-element.74), channel_id=1, source_target_pairs={{254,0},{255,1},{0,254},{1,255},{2,4},{3,5},{4,2},{5,3},{6,8},{7,9... | collective-permute-start | bytes 786440 | tf_op jit(solution)/shard_map/ppermute | solution.py:204
  22.1 13.8 %copy-start.14 = (s32[4]{0:T(128)S(1)}, s32[4]{0:T(128)}, u32[]{:S(2)}) copy-start(s32[4]{0:T(128)} %constant.51.clone) | copy-start | bytes 52
  27.8 39.5 %collective-permute-start.11 = (bf16[4,128,256]{2,1,0:T(8,128)(2,1)}, bf16[4,128,256]{2,1,0:T(8,128)(2,1)}, u32[]{:S(2)}, u32[]{:S(2)}) collective-permute-start(bf16[4,128,256]{2,1,0:T(8,128)(2,1)} %get-tuple-element.75), channel_id=1, source_target_pairs={{254,1},{255,0},{0,255},{1,254},{2,5},{3,4},{4,3},{5,2},{6,9},{7,8... | collective-permute-start | bytes 786440 | tf_op jit(solution)/shard_map/ppermute | solution.py:204
  34.9 3.0 %copy-start.4 = (bf16[4,128,256]{2,1,0:T(8,128)(2,1)}, bf16[4,128,256]{2,1,0:T(8,128)(2,1)S(1)}, u32[]{:S(2)}) copy-start(bf16[4,128,256]{2,1,0:T(8,128)(2,1)S(1)} %collective-permute-done.13.two) | copy-start | bytes 786436
  34.9 32.4 %collective-permute-start.6 = (bf16[4,128,256]{2,1,0:T(8,128)(2,1)}, bf16[4,128,256]{2,1,0:T(8,128)(2,1)}, u32[]{:S(2)}, u32[]{:S(2)}) collective-permute-start(bf16[4,128,256]{2,1,0:T(8,128)(2,1)} %get-tuple-element.65.rest_0_), channel_id=1, source_target_pairs={{254,255},{255,254},{0,1},{1,0},{2,3},{3,2},{4,5},{5,4},{6,7},{7,6... | collective-permute-start | bytes 786440 | tf_op jit(solution)/shard_map/ppermute | solution.py:204
  37.9 0.7 copy-start.9
  38.6 0.7 copy-start.11
  39.3 0.7 copy-start.6
  40.0 41.2 %collective-permute-start.7 = (bf16[4,128,256]{2,1,0:T(8,128)(2,1)}, bf16[4,128,256]{2,1,0:T(8,128)(2,1)}, u32[]{:S(2)}, u32[]{:S(2)}) collective-permute-start(bf16[4,128,256]{2,1,0:T(8,128)(2,1)} %get-tuple-element.72), channel_id=1, source_target_pairs={{254,0},{255,1},{0,254},{1,255},{2,4},{3,5},{4,2},{5,3},{6,8},{7,9... | collective-permute-start | bytes 786440 | tf_op jit(solution)/shard_map/ppermute | solution.py:204
  49.7 40.1 %collective-permute-start.8 = (bf16[4,128,256]{2,1,0:T(8,128)(2,1)}, bf16[4,128,256]{2,1,0:T(8,128)(2,1)}, u32[]{:S(2)}, u32[]{:S(2)}) collective-permute-start(bf16[4,128,256]{2,1,0:T(8,128)(2,1)} %get-tuple-element.73), channel_id=1, source_target_pairs={{254,1},{255,0},{0,255},{1,254},{2,5},{3,4},{4,3},{5,2},{6,9},{7,8... | collective-permute-start | bytes 786440 | tf_op jit(solution)/shard_map/ppermute | solution.py:204
  51.7 38.1 %collective-permute-start.3 = (bf16[4,128,256]{2,1,0:T(8,128)(2,1)}, bf16[4,128,256]{2,1,0:T(8,128)(2,1)}, u32[]{:S(2)}, u32[]{:S(2)}) collective-permute-start(bf16[4,128,256]{2,1,0:T(8,128)(2,1)} %get-tuple-element.66.rest_0_), channel_id=1, source_target_pairs={{254,255},{255,254},{0,1},{1,0},{2,3},{3,2},{4,5},{5,4},{6,7},{7,6... | collective-permute-start | bytes 786440 | tf_op jit(solution)/shard_map/ppermute | solution.py:204
  52.8 41.6 %copy-start = (bf16[128,5120]{1,0:T(8,128)(2,1)S(1)}, bf16[128,5120]{1,0:T(8,128)(2,1)}, u32[]{:S(2)}) copy-start(bf16[128,5120]{1,0:T(8,128)(2,1)} %q_ref.19) | copy-start | bytes 3932164
  52.8 41.6 %copy-start.1 = (bf16[128,5120]{1,0:T(8,128)(2,1)S(1)}, bf16[128,5120]{1,0:T(8,128)(2,1)}, u32[]{:S(2)}) copy-start(bf16[128,5120]{1,0:T(8,128)(2,1)} %k_ref.19) | copy-start | bytes 3932164
  54.2 0.7 copy-start.8
  54.9 0.7 copy-start.10
  55.6 0.7 copy-start.12
  67.3 38.1 %collective-permute-start.4 = (bf16[4,128,256]{2,1,0:T(8,128)(2,1)}, bf16[4,128,256]{2,1,0:T(8,128)(2,1)S(1)}, u32[]{:S(2)}, u32[]{:S(2)}) collective-permute-start(bf16[4,128,256]{2,1,0:T(8,128)(2,1)} %copy-done.11), channel_id=1, source_target_pairs={{254,0},{255,1},{0,254},{1,255},{2,4},{3,5},{4,2},{5,3},{6,8},{7,9... | collective-permute-start | bytes 786440 | tf_op jit(solution)/shard_map/ppermute | solution.py:204
  67.3 44.9 %collective-permute-start.5 = (bf16[4,128,256]{2,1,0:T(8,128)(2,1)}, bf16[4,128,256]{2,1,0:T(8,128)(2,1)S(1)}, u32[]{:S(2)}, u32[]{:S(2)}) collective-permute-start(bf16[4,128,256]{2,1,0:T(8,128)(2,1)} %copy-done.9), channel_id=1, source_target_pairs={{254,1},{255,0},{0,255},{1,254},{2,5},{3,4},{4,3},{5,2},{6,9},{7,8... | collective-permute-start | bytes 786440 | tf_op jit(solution)/shard_map/ppermute | solution.py:204
  81.2 44.0 %collective-permute-start = (bf16[4,128,256]{2,1,0:T(8,128)(2,1)}, bf16[4,128,256]{2,1,0:T(8,128)(2,1)S(1)}, u32[]{:S(2)}, u32[]{:S(2)}) collective-permute-start(bf16[4,128,256]{2,1,0:T(8,128)(2,1)} %copy-done.12), channel_id=1, source_target_pairs={{254,255},{255,254},{0,1},{1,0},{2,3},{3,2},{4,5},{5,4},{6,7},{7,6... | collective-permute-start | bytes 786440 | tf_op jit(solution)/shard_map/ppermute | solution.py:204
  89.8 38.4 %collective-permute-start.1 = (bf16[4,128,256]{2,1,0:T(8,128)(2,1)}, bf16[4,128,256]{2,1,0:T(8,128)(2,1)S(1)}, u32[]{:S(2)}, u32[]{:S(2)}) collective-permute-start(bf16[4,128,256]{2,1,0:T(8,128)(2,1)} %copy-done.10), channel_id=1, source_target_pairs={{254,0},{255,1},{0,254},{1,255},{2,4},{3,5},{4,2},{5,3},{6,8},{7,9... | collective-permute-start | bytes 786440 | tf_op jit(solution)/shard_map/ppermute | solution.py:204
  89.8 44.8 %collective-permute-start.2 = (bf16[4,128,256]{2,1,0:T(8,128)(2,1)}, bf16[4,128,256]{2,1,0:T(8,128)(2,1)S(1)}, u32[]{:S(2)}, u32[]{:S(2)}) collective-permute-start(bf16[4,128,256]{2,1,0:T(8,128)(2,1)} %copy-done.8), channel_id=1, source_target_pairs={{254,1},{255,0},{0,255},{1,254},{2,5},{3,4},{4,3},{5,2},{6,9},{7,8... | collective-permute-start | bytes 786440 | tf_op jit(solution)/shard_map/ppermute | solution.py:204
  94.4 1.3 copy-start.2
  95.7 1.3 copy-start.3
  97.0 0.9 copy-start.5
  97.9 0.9 copy-start.7
  105.4 36.5 %collective-permute-start.27 = (bf16[4,128,256]{2,1,0:T(8,128)(2,1)S(1)}, bf16[4,128,256]{2,1,0:T(8,128)(2,1)S(1)}, u32[]{:S(2)}, u32[]{:S(2)}) collective-permute-start(bf16[4,128,256]{2,1,0:T(8,128)(2,1)S(1)} %get-tuple-element.95), channel_id=1, source_target_pairs={{254,1},{255,0},{0,255},{1,254},{2,5},{3,4},{4,3},{5,2},{6,9},{7,8... | collective-permute-start | bytes 786440 | tf_op jit(solution)/shard_map/ppermute | solution.py:204
  112.2 39.2 %collective-permute-start.28 = (bf16[4,128,256]{2,1,0:T(8,128)(2,1)S(1)}, bf16[4,128,256]{2,1,0:T(8,128)(2,1)S(1)}, u32[]{:S(2)}, u32[]{:S(2)}) collective-permute-start(bf16[4,128,256]{2,1,0:T(8,128)(2,1)S(1)} %get-tuple-element.96), channel_id=1, source_target_pairs={{254,0},{255,1},{0,254},{1,255},{2,4},{3,5},{4,2},{5,3},{6,8},{7,9... | collective-permute-start | bytes 786440 | tf_op jit(solution)/shard_map/ppermute | solution.py:204
  125.2 27.7 %collective-permute-start.29 = (bf16[4,128,256]{2,1,0:T(8,128)(2,1)S(1)}, bf16[4,128,256]{2,1,0:T(8,128)(2,1)S(1)}, u32[]{:S(2)}, u32[]{:S(2)}) collective-permute-start(bf16[4,128,256]{2,1,0:T(8,128)(2,1)S(1)} %get-tuple-element.97), channel_id=1, source_target_pairs={{254,255},{255,254},{0,1},{1,0},{2,3},{3,2},{4,5},{5,4},{6,7},{7,6... | collective-permute-start | bytes 786440 | tf_op jit(solution)/shard_map/ppermute | solution.py:204
  128.2 31.5 %collective-permute-start.24 = (bf16[4,128,256]{2,1,0:T(8,128)(2,1)S(1)}, bf16[4,128,256]{2,1,0:T(8,128)(2,1)S(1)}, u32[]{:S(2)}, u32[]{:S(2)}) collective-permute-start(bf16[4,128,256]{2,1,0:T(8,128)(2,1)S(1)} %get-tuple-element.92), channel_id=1, source_target_pairs={{254,255},{255,254},{0,1},{1,0},{2,3},{3,2},{4,5},{5,4},{6,7},{7,6... | collective-permute-start | bytes 786440 | tf_op jit(solution)/shard_map/ppermute | solution.py:204
  134.6 32.6 %collective-permute-start.25 = (bf16[4,128,256]{2,1,0:T(8,128)(2,1)S(1)}, bf16[4,128,256]{2,1,0:T(8,128)(2,1)S(1)}, u32[]{:S(2)}, u32[]{:S(2)}) collective-permute-start(bf16[4,128,256]{2,1,0:T(8,128)(2,1)S(1)} %get-tuple-element.93), channel_id=1, source_target_pairs={{254,0},{255,1},{0,254},{1,255},{2,4},{3,5},{4,2},{5,3},{6,8},{7,9... | collective-permute-start | bytes 786440 | tf_op jit(solution)/shard_map/ppermute | solution.py:204
  141.9 37.7 %collective-permute-start.26 = (bf16[4,128,256]{2,1,0:T(8,128)(2,1)S(1)}, bf16[4,128,256]{2,1,0:T(8,128)(2,1)S(1)}, u32[]{:S(2)}, u32[]{:S(2)}) collective-permute-start(bf16[4,128,256]{2,1,0:T(8,128)(2,1)S(1)} %get-tuple-element.94), channel_id=1, source_target_pairs={{254,1},{255,0},{0,255},{1,254},{2,5},{3,4},{4,3},{5,2},{6,9},{7,8... | collective-permute-start | bytes 786440 | tf_op jit(solution)/shard_map/ppermute | solution.py:204
  151.4 28.2 %collective-permute-start.21 = (bf16[4,128,256]{2,1,0:T(8,128)(2,1)S(1)}, bf16[4,128,256]{2,1,0:T(8,128)(2,1)S(1)}, u32[]{:S(2)}, u32[]{:S(2)}) collective-permute-start(bf16[4,128,256]{2,1,0:T(8,128)(2,1)S(1)} %get-tuple-element.89), channel_id=1, source_target_pairs={{254,255},{255,254},{0,1},{1,0},{2,3},{3,2},{4,5},{5,4},{6,7},{7,6... | collective-permute-start | bytes 786440 | tf_op jit(solution)/shard_map/ppermute | solution.py:204
  152.9 40.5 %collective-permute-start.22 = (bf16[4,128,256]{2,1,0:T(8,128)(2,1)S(1)}, bf16[4,128,256]{2,1,0:T(8,128)(2,1)S(1)}, u32[]{:S(2)}, u32[]{:S(2)}) collective-permute-start(bf16[4,128,256]{2,1,0:T(8,128)(2,1)S(1)} %get-tuple-element.90), channel_id=1, source_target_pairs={{254,0},{255,1},{0,254},{1,255},{2,4},{3,5},{4,2},{5,3},{6,8},{7,9... | collective-permute-start | bytes 786440 | tf_op jit(solution)/shard_map/ppermute | solution.py:204
  159.7 42.4 %collective-permute-start.23 = (bf16[4,128,256]{2,1,0:T(8,128)(2,1)S(1)}, bf16[4,128,256]{2,1,0:T(8,128)(2,1)S(1)}, u32[]{:S(2)}, u32[]{:S(2)}) collective-permute-start(bf16[4,128,256]{2,1,0:T(8,128)(2,1)S(1)} %get-tuple-element.91), channel_id=1, source_target_pairs={{254,1},{255,0},{0,255},{1,254},{2,5},{3,4},{4,3},{5,2},{6,9},{7,8... | collective-permute-start | bytes 786440 | tf_op jit(solution)/shard_map/ppermute | solution.py:204
  167.2 34.9 %collective-permute-start.18 = (bf16[4,128,256]{2,1,0:T(8,128)(2,1)S(1)}, bf16[4,128,256]{2,1,0:T(8,128)(2,1)S(1)}, u32[]{:S(2)}, u32[]{:S(2)}) collective-permute-start(bf16[4,128,256]{2,1,0:T(8,128)(2,1)S(1)} %get-tuple-element.86), channel_id=1, source_target_pairs={{254,255},{255,254},{0,1},{1,0},{2,3},{3,2},{4,5},{5,4},{6,7},{7,6... | collective-permute-start | bytes 786440 | tf_op jit(solution)/shard_map/ppermute | solution.py:204
  179.6 36.3 %collective-permute-start.19 = (bf16[4,128,256]{2,1,0:T(8,128)(2,1)S(1)}, bf16[4,128,256]{2,1,0:T(8,128)(2,1)S(1)}, u32[]{:S(2)}, u32[]{:S(2)}) collective-permute-start(bf16[4,128,256]{2,1,0:T(8,128)(2,1)S(1)} %get-tuple-element.87), channel_id=1, source_target_pairs={{254,0},{255,1},{0,254},{1,255},{2,4},{3,5},{4,2},{5,3},{6,8},{7,9... | collective-permute-start | bytes 786440 | tf_op jit(solution)/shard_map/ppermute | solution.py:204
  179.6 45.0 %collective-permute-start.20 = (bf16[4,128,256]{2,1,0:T(8,128)(2,1)S(1)}, bf16[4,128,256]{2,1,0:T(8,128)(2,1)S(1)}, u32[]{:S(2)}, u32[]{:S(2)}) collective-permute-start(bf16[4,128,256]{2,1,0:T(8,128)(2,1)S(1)} %get-tuple-element.88), channel_id=1, source_target_pairs={{254,1},{255,0},{0,255},{1,254},{2,5},{3,4},{4,3},{5,2},{6,9},{7,8... | collective-permute-start | bytes 786440 | tf_op jit(solution)/shard_map/ppermute | solution.py:204
  193.5 32.3 %collective-permute-start.17 = (bf16[4,128,256]{2,1,0:T(8,128)(2,1)S(1)}, bf16[4,128,256]{2,1,0:T(8,128)(2,1)S(1)}, u32[]{:S(2)}, u32[]{:S(2)}) collective-permute-start(bf16[4,128,256]{2,1,0:T(8,128)(2,1)S(1)} %get-tuple-element.85), channel_id=1, source_target_pairs={{254,255},{255,254},{0,1},{1,0},{2,3},{3,2},{4,5},{5,4},{6,7},{7,6... | collective-permute-start | bytes 786440 | tf_op jit(solution)/shard_map/ppermute | solution.py:204
  202.1 25.2 %collective-permute-start.16 = (bf16[4,128,256]{2,1,0:T(8,128)(2,1)S(1)}, bf16[4,128,256]{2,1,0:T(8,128)(2,1)S(1)}, u32[]{:S(2)}, u32[]{:S(2)}) collective-permute-start(bf16[4,128,256]{2,1,0:T(8,128)(2,1)S(1)} %get-tuple-element.83), channel_id=1, source_target_pairs={{254,0},{255,1},{0,254},{1,255},{2,4},{3,5},{4,2},{5,3},{6,8},{7,9... | collective-permute-start | bytes 786440 | tf_op jit(solution)/shard_map/ppermute | solution.py:204
  202.1 33.7 %collective-permute-start.15 = (bf16[4,128,256]{2,1,0:T(8,128)(2,1)S(1)}, bf16[4,128,256]{2,1,0:T(8,128)(2,1)S(1)}, u32[]{:S(2)}, u32[]{:S(2)}) collective-permute-start(bf16[4,128,256]{2,1,0:T(8,128)(2,1)S(1)} %get-tuple-element.82), channel_id=1, source_target_pairs={{254,1},{255,0},{0,255},{1,254},{2,5},{3,4},{4,3},{5,2},{6,9},{7,8... | collective-permute-start | bytes 786440 | tf_op jit(solution)/shard_map/ppermute | solution.py:204

commit v4 on v3

--- a/solution.py
+++ b/solution.py
@@ -12,7 +12,7 @@
 MOST = 4
 AXES = ("seq", "uly")
 CHUNKS = (2, 2, 2, 2, 2)
-SWAPS = ((0, 3, 2, 1),) + ((0, 1, 2, 3),) * 4
+SWAPS = ((0, 3, 2, 1),) + ((0, 2, 1, 3),) * 4
 LAST = [(0, 1), (2,), (3,)]
 
 

time: 237 us -> 237 us (level)
  starting transfers between devices: 85.5 us -> 118 us
  waiting for transfers between devices: 90 us -> 57.7 us
    ppermute x30, waiting for transfers between devices: 90 us -> 57.7 us  [exchange(): lax.ppermute(piece, AXES, routes(swap, tiles))]
    ppermute x30, starting transfers between devices: 85.5 us -> 118 us  [exchange(): lax.ppermute(piece, AXES, routes(swap, tiles))]
    unnamed x30 -> x32, local copies, waits for them, and re-layouts: 8.76 us -> 8.8 us
  transfers between devices with their start and end apart: 30 -> 30, of which waited for: 16 -> 10; matrix products, arithmetic and copies ran while one was open for 1% -> 1% of each run, Pallas kernels for 20% -> 20%
where the time goes in v4:
time: 237 us
  starting transfers between devices  118 us (50%)
  waiting for transfers between devices  57.7 us (24%)
  Pallas kernels  50 us (21%)
  local copies, waits for them, and re-layouts  10.1 us (4%)
    ppermute x30, starting transfers between devices, exchange(): lax.ppermute(piece, AXES, routes(swap, tiles))  118 us
    ppermute x30, waiting for transfers between devices, exchange(): lax.ppermute(piece, AXES, routes(swap, tiles))  57.7 us
    pallas_call x5, Pallas kernels, attend(): pl.pallas_call(attend_kernel, out_shape=(piece,) * 4, grid_spec=pltpu.Pre...  34.5 us
    pallas_call x5, Pallas kernels, pack(): pl.pallas_call(partial(pack_kernel, swaps, begin, heads_each, width), out...  8.84 us
    unnamed x32, local copies, waits for them, and re-layouts  8.8 us
    pallas_call x7, Pallas kernels, unpack(): pl.pallas_call(partial(unpack_kernel, swaps, begin, heads_each, width), o...  6.71 us
  transfers between devices with their start and end apart: 30, of which 10 were waited for; matrix products, arithmetic and copies ran while one was open for 1% of the time, Pallas kernels for 20%

profile of v4, /device:TPU:0, one launch (start us, length us, event | category | flops | bytes accessed | tf_op | source)
XLA Modules:
  0.0 236.7 jit_solution(15623538799817064766)
XLA Ops:
  0.6 1.3 pack.5
  1.9 8.3 %collective-permute-start.12 = (bf16[4,128,256]{2,1,0:T(8,128)(2,1)S(1)}, bf16[4,128,256]{2,1,0:T(8,128)(2,1)S(1)}, u32[]{:S(2)}, u32[]{:S(2)}) collective-permute-start(bf16[4,128,256]{2,1,0:T(8,128)(2,1)S(1)} %get-tuple-element.63.rest_0_), channel_id=1, source_target_pairs={{254,1},{255,0},{0,255},{1,254},{2,5},{3,4},{4,3},{5,2},{6,9},{7,8... | collective-permute-start | bytes 786440 | tf_op jit(solution)/shard_map/ppermute | solution.py:204
  10.2 0.5 collective-permute-start.13
  10.8 1.4 collective-permute-start.14
  12.1 2.0 pack.6
  14.1 7.9 %collective-permute-start.9 = (bf16[4,128,256]{2,1,0:T(8,128)(2,1)S(1)}, bf16[4,128,256]{2,1,0:T(8,128)(2,1)S(1)}, u32[]{:S(2)}, u32[]{:S(2)}) collective-permute-start(bf16[4,128,256]{2,1,0:T(8,128)(2,1)S(1)} %get-tuple-element.64.rest_0_), channel_id=1, source_target_pairs={{254,0},{255,1},{0,254},{1,255},{2,4},{3,5},{4,2},{5,3},{6,8},{7,9... | collective-permute-start | bytes 786440 | tf_op jit(solution)/shard_map/ppermute | solution.py:204
  22.0 0.3 collective-permute-start.10
  22.3 2.2 pack.7
  24.5 4.2 %collective-permute-done.12.one = bf16[4,128,256]{2,1,0:T(8,128)(2,1)S(1)} collective-permute-done((bf16[4,128,256]{2,1,0:T(8,128)(2,1)S(1)}, bf16[4,128,256]{2,1,0:T(8,128)(2,1)S(1)}, u32[]{:S(2)}, u32[]{:S(2)}) %collective-permute-start.12) | collective-permute-done | bytes 262176 | tf_op jit(solution)/shard_map/ppermute | solution.py:204
  28.7 6.4 %collective-permute-start.11 = (bf16[4,128,256]{2,1,0:T(8,128)(2,1)}, bf16[4,128,256]{2,1,0:T(8,128)(2,1)}, u32[]{:S(2)}, u32[]{:S(2)}) collective-permute-start(bf16[4,128,256]{2,1,0:T(8,128)(2,1)} %get-tuple-element.75), channel_id=1, source_target_pairs={{254,1},{255,0},{0,255},{1,254},{2,5},{3,4},{4,3},{5,2},{6,9},{7,8... | collective-permute-start | bytes 786440 | tf_op jit(solution)/shard_map/ppermute | solution.py:204
  35.1 5.0 %collective-permute-done.13.two = bf16[4,128,256]{2,1,0:T(8,128)(2,1)S(1)} collective-permute-done((bf16[4,128,256]{2,1,0:T(8,128)(2,1)S(1)}, bf16[4,128,256]{2,1,0:T(8,128)(2,1)S(1)}, u32[]{:S(2)}, u32[]{:S(2)}) %collective-permute-start.13) | collective-permute-done | bytes 262176 | tf_op jit(solution)/shard_map/ppermute | solution.py:204
  40.1 11.5 %collective-permute-start.6 = (bf16[4,128,256]{2,1,0:T(8,128)(2,1)}, bf16[4,128,256]{2,1,0:T(8,128)(2,1)}, u32[]{:S(2)}, u32[]{:S(2)}) collective-permute-start(bf16[4,128,256]{2,1,0:T(8,128)(2,1)} %get-tuple-element.65.rest_0_), channel_id=1, source_target_pairs={{254,0},{255,1},{0,254},{1,255},{2,4},{3,5},{4,2},{5,3},{6,8},{7,9... | collective-permute-start | bytes 786440 | tf_op jit(solution)/shard_map/ppermute | solution.py:204
  51.6 2.0 pack.8
  53.6 0.7 copy-done.9
  54.3 0.7 copy-done.11
  55.0 0.7 copy-done.6
  55.8 0.3 collective-permute-start.8
  56.1 9.2 %collective-permute-start.3 = (bf16[4,128,256]{2,1,0:T(8,128)(2,1)}, bf16[4,128,256]{2,1,0:T(8,128)(2,1)}, u32[]{:S(2)}, u32[]{:S(2)}) collective-permute-start(bf16[4,128,256]{2,1,0:T(8,128)(2,1)} %get-tuple-element.66.rest_0_), channel_id=1, source_target_pairs={{254,0},{255,1},{0,254},{1,255},{2,4},{3,5},{4,2},{5,3},{6,8},{7,9... | collective-permute-start | bytes 786440 | tf_op jit(solution)/shard_map/ppermute | solution.py:204
  65.3 1.4 pack.9
  66.8 0.7 copy-done.8
  67.5 0.7 copy-done.10
  68.2 0.7 copy-done.12
  68.9 0.6 gather_fusion.1
  69.5 0.6 gather_fusion
  70.2 5.5 %collective-permute-done.6.one = bf16[4,128,256]{2,1,0:T(8,128)(2,1)} collective-permute-done((bf16[4,128,256]{2,1,0:T(8,128)(2,1)}, bf16[4,128,256]{2,1,0:T(8,128)(2,1)}, u32[]{:S(2)}, u32[]{:S(2)}) %collective-permute-start.6) | collective-permute-done | bytes 262176 | tf_op jit(solution)/shard_map/ppermute | solution.py:204
  75.7 2.1 collective-permute-start.5
  77.8 0.1 pad_add_fusion.1.info
  77.9 9.8 %collective-permute-start = (bf16[4,128,256]{2,1,0:T(8,128)(2,1)}, bf16[4,128,256]{2,1,0:T(8,128)(2,1)S(1)}, u32[]{:S(2)}, u32[]{:S(2)}) collective-permute-start(bf16[4,128,256]{2,1,0:T(8,128)(2,1)} %copy-done.12), channel_id=1, source_target_pairs={{254,0},{255,1},{0,254},{1,255},{2,4},{3,5},{4,2},{5,3},{6,8},{7,9... | collective-permute-start | bytes 786440 | tf_op jit(solution)/shard_map/ppermute | solution.py:204
  87.7 10.5 %collective-permute-done.3.one = bf16[4,128,256]{2,1,0:T(8,128)(2,1)} collective-permute-done((bf16[4,128,256]{2,1,0:T(8,128)(2,1)}, bf16[4,128,256]{2,1,0:T(8,128)(2,1)}, u32[]{:S(2)}, u32[]{:S(2)}) %collective-permute-start.3) | collective-permute-done | bytes 262176 | tf_op jit(solution)/shard_map/ppermute | solution.py:204
  98.2 1.9 collective-permute-start.2
  100.2 1.3 copy-done.2
  101.5 1.3 copy-done.3
  102.9 0.9 copy-done.5
  103.8 0.9 copy-done.7
  104.8 6.5 %attend.5 = (bf16[4,128,256]{2,1,0:T(8,128)(2,1)S(1)}, bf16[4,128,256]{2,1,0:T(8,128)(2,1)S(1)}, bf16[4,128,256]{2,1,0:T(8,128)(2,1)S(1)}, bf16[4,128,256]{2,1,0:T(8,128)(2,1)S(1)}) custom-call(s32[5]{0:T(128)S(1)} %pad_add_fusion.1.info, bf16[128,5120]{1,0:T(8,128)(2,1)S(1)} %copy-done, bf16[128,5120]{1,0:T(8,128)(2,1)S(1)} %copy-done.1, ...), custom_call_target="tpu_custom_call" | custom-call | flops 805306368 | bytes 2097152 | tf_op jit(solution)/shard_map/attend/pallas_call | solution.py:167
  111.2 5.4 %collective-permute-start.27 = (bf16[4,128,256]{2,1,0:T(8,128)(2,1)S(1)}, bf16[4,128,256]{2,1,0:T(8,128)(2,1)S(1)}, u32[]{:S(2)}, u32[]{:S(2)}) collective-permute-start(bf16[4,128,256]{2,1,0:T(8,128)(2,1)S(1)} %get-tuple-element.95), channel_id=1, source_target_pairs={{254,1},{255,0},{0,255},{1,254},{2,5},{3,4},{4,3},{5,2},{6,9},{7,8... | collective-permute-start | bytes 786440 | tf_op jit(solution)/shard_map/ppermute | solution.py:204
  116.6 10.0 %collective-permute-start.28 = (bf16[4,128,256]{2,1,0:T(8,128)(2,1)S(1)}, bf16[4,128,256]{2,1,0:T(8,128)(2,1)S(1)}, u32[]{:S(2)}, u32[]{:S(2)}) collective-permute-start(bf16[4,128,256]{2,1,0:T(8,128)(2,1)S(1)} %get-tuple-element.96), channel_id=1, source_target_pairs={{254,0},{255,1},{0,254},{1,255},{2,4},{3,5},{4,2},{5,3},{6,8},{7,9... | collective-permute-start | bytes 786440 | tf_op jit(solution)/shard_map/ppermute | solution.py:204
  126.6 7.2 %attend.6 = (bf16[4,128,256]{2,1,0:T(8,128)(2,1)S(1)}, bf16[4,128,256]{2,1,0:T(8,128)(2,1)S(1)}, bf16[4,128,256]{2,1,0:T(8,128)(2,1)S(1)}, bf16[4,128,256]{2,1,0:T(8,128)(2,1)S(1)}) custom-call(s32[5]{0:T(128)S(1)} %pad_add_fusion.info, bf16[128,5120]{1,0:T(8,128)(2,1)S(1)} %copy-done, bf16[128,5120]{1,0:T(8,128)(2,1)S(1)} %copy-done.1, ...), custom_call_target="tpu_custom_call" | custom-call | flops 805306368 | bytes 2097152 | tf_op jit(solution)/shard_map/attend/pallas_call | solution.py:167
  133.8 0.1 collective-permute-start.29
  133.9 3.8 %collective-permute-start.24 = (bf16[4,128,256]{2,1,0:T(8,128)(2,1)S(1)}, bf16[4,128,256]{2,1,0:T(8,128)(2,1)S(1)}, u32[]{:S(2)}, u32[]{:S(2)}) collective-permute-start(bf16[4,128,256]{2,1,0:T(8,128)(2,1)S(1)} %get-tuple-element.92), channel_id=1, source_target_pairs={{254,0},{255,1},{0,254},{1,255},{2,4},{3,5},{4,2},{5,3},{6,8},{7,9... | collective-permute-start | bytes 786440 | tf_op jit(solution)/shard_map/ppermute | solution.py:204
  137.7 0.4 collective-permute-start.25
  138.1 7.2 %attend.7 = (bf16[4,128,256]{2,1,0:T(8,128)(2,1)S(1)}, bf16[4,128,256]{2,1,0:T(8,128)(2,1)S(1)}, bf16[4,128,256]{2,1,0:T(8,128)(2,1)S(1)}, bf16[4,128,256]{2,1,0:T(8,128)(2,1)S(1)}) custom-call(s32[5]{0:T(128)S(1)} %pad_add_fusion.info, bf16[128,5120]{1,0:T(8,128)(2,1)S(1)} %copy-done, bf16[128,5120]{1,0:T(8,128)(2,1)S(1)} %copy-done.1, ...), custom_call_target="tpu_custom_call" | custom-call | flops 805306368 | bytes 2097152 | tf_op jit(solution)/shard_map/attend/pallas_call | solution.py:167
  145.4 6.8 %collective-permute-start.26 = (bf16[4,128,256]{2,1,0:T(8,128)(2,1)S(1)}, bf16[4,128,256]{2,1,0:T(8,128)(2,1)S(1)}, u32[]{:S(2)}, u32[]{:S(2)}) collective-permute-start(bf16[4,128,256]{2,1,0:T(8,128)(2,1)S(1)} %get-tuple-element.94), channel_id=1, source_target_pairs={{254,1},{255,0},{0,255},{1,254},{2,5},{3,4},{4,3},{5,2},{6,9},{7,8... | collective-permute-start | bytes 786440 | tf_op jit(solution)/shard_map/ppermute | solution.py:204
  152.1 7.6 %collective-permute-start.21 = (bf16[4,128,256]{2,1,0:T(8,128)(2,1)S(1)}, bf16[4,128,256]{2,1,0:T(8,128)(2,1)S(1)}, u32[]{:S(2)}, u32[]{:S(2)}) collective-permute-start(bf16[4,128,256]{2,1,0:T(8,128)(2,1)S(1)} %get-tuple-element.89), channel_id=1, source_target_pairs={{254,0},{255,1},{0,254},{1,255},{2,4},{3,5},{4,2},{5,3},{6,8},{7,9... | collective-permute-start | bytes 786440 | tf_op jit(solution)/shard_map/ppermute | solution.py:204
  159.7 5.8 %collective-permute-done.24.rest_1_ = bf16[4,128,256]{2,1,0:T(8,128)(2,1)S(1)} collective-permute-done((bf16[4,128,256]{2,1,0:T(8,128)(2,1)S(1)}, bf16[4,128,256]{2,1,0:T(8,128)(2,1)S(1)}, u32[]{:S(2)}, u32[]{:S(2)}) %collective-permute-start.24) | collective-permute-done | bytes 262176 | tf_op jit(solution)/shard_map/ppermute | solution.py:204
  165.5 7.1 %attend.8 = (bf16[4,128,256]{2,1,0:T(8,128)(2,1)S(1)}, bf16[4,128,256]{2,1,0:T(8,128)(2,1)S(1)}, bf16[4,128,256]{2,1,0:T(8,128)(2,1)S(1)}, bf16[4,128,256]{2,1,0:T(8,128)(2,1)S(1)}) custom-call(s32[5]{0:T(128)S(1)} %pad_add_fusion.info, bf16[128,5120]{1,0:T(8,128)(2,1)S(1)} %copy-done, bf16[128,5120]{1,0:T(8,128)(2,1)S(1)} %copy-done.1, ...), custom_call_target="tpu_custom_call" | custom-call | flops 805306368 | bytes 2097152 | tf_op jit(solution)/shard_map/attend/pallas_call | solution.py:167
  172.7 9.0 %collective-permute-start.18 = (bf16[4,128,256]{2,1,0:T(8,128)(2,1)S(1)}, bf16[4,128,256]{2,1,0:T(8,128)(2,1)S(1)}, u32[]{:S(2)}, u32[]{:S(2)}) collective-permute-start(bf16[4,128,256]{2,1,0:T(8,128)(2,1)S(1)} %get-tuple-element.86), channel_id=1, source_target_pairs={{254,0},{255,1},{0,254},{1,255},{2,4},{3,5},{4,2},{5,3},{6,8},{7,9... | collective-permute-start | bytes 786440 | tf_op jit(solution)/shard_map/ppermute | solution.py:204
  181.7 0.8 collective-permute-start.19
  182.6 5.3 %collective-permute-done.21.rest_1_ = bf16[4,128,256]{2,1,0:T(8,128)(2,1)S(1)} collective-permute-done((bf16[4,128,256]{2,1,0:T(8,128)(2,1)S(1)}, bf16[4,128,256]{2,1,0:T(8,128)(2,1)S(1)}, u32[]{:S(2)}, u32[]{:S(2)}) %collective-permute-start.21) | collective-permute-done | bytes 262176 | tf_op jit(solution)/shard_map/ppermute | solution.py:204
  187.9 2.3 collective-permute-start.20
  190.1 6.5 %attend.9 = (bf16[4,128,256]{2,1,0:T(8,128)(2,1)S(1)}, bf16[4,128,256]{2,1,0:T(8,128)(2,1)S(1)}, bf16[4,128,256]{2,1,0:T(8,128)(2,1)S(1)}, bf16[4,128,256]{2,1,0:T(8,128)(2,1)S(1)}) custom-call(s32[5]{0:T(128)S(1)} %pad_add_fusion.info, bf16[128,5120]{1,0:T(8,128)(2,1)S(1)} %copy-done, bf16[128,5120]{1,0:T(8,128)(2,1)S(1)} %copy-done.1, ...), custom_call_target="tpu_custom_call" | custom-call | flops 805306368 | bytes 2097152 | tf_op jit(solution)/shard_map/attend/pallas_call | solution.py:167
  196.6 9.9 %collective-permute-start.17 = (bf16[4,128,256]{2,1,0:T(8,128)(2,1)S(1)}, bf16[4,128,256]{2,1,0:T(8,128)(2,1)S(1)}, u32[]{:S(2)}, u32[]{:S(2)}) collective-permute-start(bf16[4,128,256]{2,1,0:T(8,128)(2,1)S(1)} %get-tuple-element.85), channel_id=1, source_target_pairs={{254,0},{255,1},{0,254},{1,255},{2,4},{3,5},{4,2},{5,3},{6,8},{7,9... | collective-permute-start | bytes 786440 | tf_op jit(solution)/shard_map/ppermute | solution.py:204
  206.4 4.1 %collective-permute-done.18.rest_1_ = bf16[4,128,256]{2,1,0:T(8,128)(2,1)S(1)} collective-permute-done((bf16[4,128,256]{2,1,0:T(8,128)(2,1)S(1)}, bf16[4,128,256]{2,1,0:T(8,128)(2,1)S(1)}, u32[]{:S(2)}, u32[]{:S(2)}) %collective-permute-start.18) | collective-permute-done | bytes 262176 | tf_op jit(solution)/shard_map/ppermute | solution.py:204
  210.5 1.9 collective-permute-start.15
  212.4 1.1 unpack.7
  213.5 1.1 unpack.8
  214.6 1.1 unpack.9
  215.8 3.2 %collective-permute-done.20.rest_3_ = bf16[4,128,256]{2,1,0:T(8,128)(2,1)S(1)} collective-permute-done((bf16[4,128,256]{2,1,0:T(8,128)(2,1)S(1)}, bf16[4,128,256]{2,1,0:T(8,128)(2,1)S(1)}, u32[]{:S(2)}, u32[]{:S(2)}) %collective-permute-start.20) | collective-permute-done | bytes 262176 | tf_op jit(solution)/shard_map/ppermute | solution.py:204
  218.9 1.1 unpack.10
  220.0 7.3 %collective-permute-done.17.rest_1_ = bf16[4,128,256]{2,1,0:T(8,128)(2,1)S(1)} collective-permute-done((bf16[4,128,256]{2,1,0:T(8,128)(2,1)S(1)}, bf16[4,128,256]{2,1,0:T(8,128)(2,1)S(1)}, u32[]{:S(2)}, u32[]{:S(2)}) %collective-permute-start.17) | collective-permute-done | bytes 262176 | tf_op jit(solution)/shard_map/ppermute | solution.py:204
  227.4 0.8 unpack.11
  228.2 0.7 unpack.12
  229.0 6.8 %collective-permute-done.15.rest_0_ = bf16[4,128,256]{2,1,0:T(8,128)(2,1)S(1)} collective-permute-done((bf16[4,128,256]{2,1,0:T(8,128)(2,1)S(1)}, bf16[4,128,256]{2,1,0:T(8,128)(2,1)S(1)}, u32[]{:S(2)}, u32[]{:S(2)}) %collective-permute-start.15) | collective-permute-done | bytes 262176 | tf_op jit(solution)/shard_map/ppermute | solution.py:204
  235.8 0.7 unpack.13
  (53 shorter events, 0.3 us)
Async XLA Ops:
  1.9 26.8 %collective-permute-start.12 = (bf16[4,128,256]{2,1,0:T(8,128)(2,1)S(1)}, bf16[4,128,256]{2,1,0:T(8,128)(2,1)S(1)}, u32[]{:S(2)}, u32[]{:S(2)}) collective-permute-start(bf16[4,128,256]{2,1,0:T(8,128)(2,1)S(1)} %get-tuple-element.63.rest_0_), channel_id=1, source_target_pairs={{254,1},{255,0},{0,255},{1,254},{2,5},{3,4},{4,3},{5,2},{6,9},{7,8... | collective-permute-start | bytes 786440 | tf_op jit(solution)/shard_map/ppermute | solution.py:204
  10.2 29.9 %collective-permute-start.13 = (bf16[4,128,256]{2,1,0:T(8,128)(2,1)S(1)}, bf16[4,128,256]{2,1,0:T(8,128)(2,1)S(1)}, u32[]{:S(2)}, u32[]{:S(2)}) collective-permute-start(bf16[4,128,256]{2,1,0:T(8,128)(2,1)S(1)} %get-tuple-element.76), channel_id=1, source_target_pairs={{254,0},{255,1},{0,254},{1,255},{2,4},{3,5},{4,2},{5,3},{6,8},{7,9... | collective-permute-start | bytes 786440 | tf_op jit(solution)/shard_map/ppermute | solution.py:204
  10.8 11.5 %copy-start.13 = (s32[256]{0:T(256)S(1)}, s32[256]{0:T(256)}, u32[]{:S(2)}) copy-start(s32[256]{0:T(256)} %param.11) | copy-start | bytes 3076
  10.8 44.3 %collective-permute-start.14 = (bf16[4,128,256]{2,1,0:T(8,128)(2,1)S(1)}, bf16[4,128,256]{2,1,0:T(8,128)(2,1)S(1)}, u32[]{:S(2)}, u32[]{:S(2)}) collective-permute-start(bf16[4,128,256]{2,1,0:T(8,128)(2,1)S(1)} %get-tuple-element.77), channel_id=1, source_target_pairs={{254,255},{255,254},{0,1},{1,0},{2,3},{3,2},{4,5},{5,4},{6,7},{7,6... | collective-permute-start | bytes 786440 | tf_op jit(solution)/shard_map/ppermute | solution.py:204
  14.1 41.7 %collective-permute-start.9 = (bf16[4,128,256]{2,1,0:T(8,128)(2,1)S(1)}, bf16[4,128,256]{2,1,0:T(8,128)(2,1)S(1)}, u32[]{:S(2)}, u32[]{:S(2)}) collective-permute-start(bf16[4,128,256]{2,1,0:T(8,128)(2,1)S(1)} %get-tuple-element.64.rest_0_), channel_id=1, source_target_pairs={{254,0},{255,1},{0,254},{1,255},{2,4},{3,5},{4,2},{5,3},{6,8},{7,9... | collective-permute-start | bytes 786440 | tf_op jit(solution)/shard_map/ppermute | solution.py:204
  22.0 34.1 %collective-permute-start.10 = (bf16[4,128,256]{2,1,0:T(8,128)(2,1)S(1)}, bf16[4,128,256]{2,1,0:T(8,128)(2,1)S(1)}, u32[]{:S(2)}, u32[]{:S(2)}) collective-permute-start(bf16[4,128,256]{2,1,0:T(8,128)(2,1)S(1)} %get-tuple-element.74), channel_id=1, source_target_pairs={{254,255},{255,254},{0,1},{1,0},{2,3},{3,2},{4,5},{5,4},{6,7},{7,6... | collective-permute-start | bytes 786440 | tf_op jit(solution)/shard_map/ppermute | solution.py:204
  22.3 29.3 %copy-start.14 = (s32[4]{0:T(128)S(1)}, s32[4]{0:T(128)}, u32[]{:S(2)}) copy-start(s32[4]{0:T(128)} %constant.51.clone) | copy-start | bytes 52
  22.3 29.3 %copy-start.15 = (s32[4]{0:T(128)S(1)}, s32[4]{0:T(128)}, u32[]{:S(2)}) copy-start(s32[4]{0:T(128)} %constant.52.clone) | copy-start | bytes 52
  28.7 41.5 %collective-permute-start.11 = (bf16[4,128,256]{2,1,0:T(8,128)(2,1)}, bf16[4,128,256]{2,1,0:T(8,128)(2,1)}, u32[]{:S(2)}, u32[]{:S(2)}) collective-permute-start(bf16[4,128,256]{2,1,0:T(8,128)(2,1)} %get-tuple-element.75), channel_id=1, source_target_pairs={{254,1},{255,0},{0,255},{1,254},{2,5},{3,4},{4,3},{5,2},{6,9},{7,8... | collective-permute-start | bytes 786440 | tf_op jit(solution)/shard_map/ppermute | solution.py:204
  40.1 13.5 %copy-start.4 = (bf16[4,128,256]{2,1,0:T(8,128)(2,1)}, bf16[4,128,256]{2,1,0:T(8,128)(2,1)S(1)}, u32[]{:S(2)}) copy-start(bf16[4,128,256]{2,1,0:T(8,128)(2,1)S(1)} %collective-permute-done.13.two) | copy-start | bytes 786436
  40.1 35.6 %collective-permute-start.6 = (bf16[4,128,256]{2,1,0:T(8,128)(2,1)}, bf16[4,128,256]{2,1,0:T(8,128)(2,1)}, u32[]{:S(2)}, u32[]{:S(2)}) collective-permute-start(bf16[4,128,256]{2,1,0:T(8,128)(2,1)} %get-tuple-element.65.rest_0_), channel_id=1, source_target_pairs={{254,0},{255,1},{0,254},{1,255},{2,4},{3,5},{4,2},{5,3},{6,8},{7,9... | collective-permute-start | bytes 786440 | tf_op jit(solution)/shard_map/ppermute | solution.py:204
  53.6 0.7 copy-start.9
  54.3 0.7 copy-start.11
  55.0 0.7 copy-start.6
  55.8 22.1 %collective-permute-start.7 = (bf16[4,128,256]{2,1,0:T(8,128)(2,1)}, bf16[4,128,256]{2,1,0:T(8,128)(2,1)}, u32[]{:S(2)}, u32[]{:S(2)}) collective-permute-start(bf16[4,128,256]{2,1,0:T(8,128)(2,1)} %get-tuple-element.72), channel_id=1, source_target_pairs={{254,255},{255,254},{0,1},{1,0},{2,3},{3,2},{4,5},{5,4},{6,7},{7,6... | collective-permute-start | bytes 786440 | tf_op jit(solution)/shard_map/ppermute | solution.py:204
  55.8 31.9 %collective-permute-start.8 = (bf16[4,128,256]{2,1,0:T(8,128)(2,1)}, bf16[4,128,256]{2,1,0:T(8,128)(2,1)}, u32[]{:S(2)}, u32[]{:S(2)}) collective-permute-start(bf16[4,128,256]{2,1,0:T(8,128)(2,1)} %get-tuple-element.73), channel_id=1, source_target_pairs={{254,1},{255,0},{0,255},{1,254},{2,5},{3,4},{4,3},{5,2},{6,9},{7,8... | collective-permute-start | bytes 786440 | tf_op jit(solution)/shard_map/ppermute | solution.py:204
  56.1 42.1 %collective-permute-start.3 = (bf16[4,128,256]{2,1,0:T(8,128)(2,1)}, bf16[4,128,256]{2,1,0:T(8,128)(2,1)}, u32[]{:S(2)}, u32[]{:S(2)}) collective-permute-start(bf16[4,128,256]{2,1,0:T(8,128)(2,1)} %get-tuple-element.66.rest_0_), channel_id=1, source_target_pairs={{254,0},{255,1},{0,254},{1,255},{2,4},{3,5},{4,2},{5,3},{6,8},{7,9... | collective-permute-start | bytes 786440 | tf_op jit(solution)/shard_map/ppermute | solution.py:204
  65.3 34.9 %copy-start = (bf16[128,5120]{1,0:T(8,128)(2,1)S(1)}, bf16[128,5120]{1,0:T(8,128)(2,1)}, u32[]{:S(2)}) copy-start(bf16[128,5120]{1,0:T(8,128)(2,1)} %q_ref.19) | copy-start | bytes 3932164
  65.3 34.9 %copy-start.1 = (bf16[128,5120]{1,0:T(8,128)(2,1)S(1)}, bf16[128,5120]{1,0:T(8,128)(2,1)}, u32[]{:S(2)}) copy-start(bf16[128,5120]{1,0:T(8,128)(2,1)} %k_ref.19) | copy-start | bytes 3932164
  66.8 0.7 copy-start.8
  67.5 0.7 copy-start.10
  68.2 0.7 copy-start.12
  70.2 41.1 %collective-permute-start.4 = (bf16[4,128,256]{2,1,0:T(8,128)(2,1)}, bf16[4,128,256]{2,1,0:T(8,128)(2,1)S(1)}, u32[]{:S(2)}, u32[]{:S(2)}) collective-permute-start(bf16[4,128,256]{2,1,0:T(8,128)(2,1)} %copy-done.11), channel_id=1, source_target_pairs={{254,255},{255,254},{0,1},{1,0},{2,3},{3,2},{4,5},{5,4},{6,7},{7,6... | collective-permute-start | bytes 786440 | tf_op jit(solution)/shard_map/ppermute | solution.py:204
  75.7 40.8 %collective-permute-start.5 = (bf16[4,128,256]{2,1,0:T(8,128)(2,1)}, bf16[4,128,256]{2,1,0:T(8,128)(2,1)S(1)}, u32[]{:S(2)}, u32[]{:S(2)}) collective-permute-start(bf16[4,128,256]{2,1,0:T(8,128)(2,1)} %copy-done.9), channel_id=1, source_target_pairs={{254,1},{255,0},{0,255},{1,254},{2,5},{3,4},{4,3},{5,2},{6,9},{7,8... | collective-permute-start | bytes 786440 | tf_op jit(solution)/shard_map/ppermute | solution.py:204
  77.9 55.9 %collective-permute-start = (bf16[4,128,256]{2,1,0:T(8,128)(2,1)}, bf16[4,128,256]{2,1,0:T(8,128)(2,1)S(1)}, u32[]{:S(2)}, u32[]{:S(2)}) collective-permute-start(bf16[4,128,256]{2,1,0:T(8,128)(2,1)} %copy-done.12), channel_id=1, source_target_pairs={{254,0},{255,1},{0,254},{1,255},{2,4},{3,5},{4,2},{5,3},{6,8},{7,9... | collective-permute-start | bytes 786440 | tf_op jit(solution)/shard_map/ppermute | solution.py:204
  87.7 46.2 %collective-permute-start.1 = (bf16[4,128,256]{2,1,0:T(8,128)(2,1)}, bf16[4,128,256]{2,1,0:T(8,128)(2,1)S(1)}, u32[]{:S(2)}, u32[]{:S(2)}) collective-permute-start(bf16[4,128,256]{2,1,0:T(8,128)(2,1)} %copy-done.10), channel_id=1, source_target_pairs={{254,255},{255,254},{0,1},{1,0},{2,3},{3,2},{4,5},{5,4},{6,7},{7,6... | collective-permute-start | bytes 786440 | tf_op jit(solution)/shard_map/ppermute | solution.py:204
  98.2 39.5 %collective-permute-start.2 = (bf16[4,128,256]{2,1,0:T(8,128)(2,1)}, bf16[4,128,256]{2,1,0:T(8,128)(2,1)S(1)}, u32[]{:S(2)}, u32[]{:S(2)}) collective-permute-start(bf16[4,128,256]{2,1,0:T(8,128)(2,1)} %copy-done.8), channel_id=1, source_target_pairs={{254,1},{255,0},{0,255},{1,254},{2,5},{3,4},{4,3},{5,2},{6,9},{7,8... | collective-permute-start | bytes 786440 | tf_op jit(solution)/shard_map/ppermute | solution.py:204
  100.2 1.3 copy-start.2
  101.5 1.3 copy-start.3
  102.9 0.9 copy-start.5
  103.8 0.9 copy-start.7
  111.2 34.1 %collective-permute-start.27 = (bf16[4,128,256]{2,1,0:T(8,128)(2,1)S(1)}, bf16[4,128,256]{2,1,0:T(8,128)(2,1)S(1)}, u32[]{:S(2)}, u32[]{:S(2)}) collective-permute-start(bf16[4,128,256]{2,1,0:T(8,128)(2,1)S(1)} %get-tuple-element.95), channel_id=1, source_target_pairs={{254,1},{255,0},{0,255},{1,254},{2,5},{3,4},{4,3},{5,2},{6,9},{7,8... | collective-permute-start | bytes 786440 | tf_op jit(solution)/shard_map/ppermute | solution.py:204
  116.6 35.6 %collective-permute-start.28 = (bf16[4,128,256]{2,1,0:T(8,128)(2,1)S(1)}, bf16[4,128,256]{2,1,0:T(8,128)(2,1)S(1)}, u32[]{:S(2)}, u32[]{:S(2)}) collective-permute-start(bf16[4,128,256]{2,1,0:T(8,128)(2,1)S(1)} %get-tuple-element.96), channel_id=1, source_target_pairs={{254,0},{255,1},{0,254},{1,255},{2,4},{3,5},{4,2},{5,3},{6,8},{7,9... | collective-permute-start | bytes 786440 | tf_op jit(solution)/shard_map/ppermute | solution.py:204
  133.8 25.9 %collective-permute-start.29 = (bf16[4,128,256]{2,1,0:T(8,128)(2,1)S(1)}, bf16[4,128,256]{2,1,0:T(8,128)(2,1)S(1)}, u32[]{:S(2)}, u32[]{:S(2)}) collective-permute-start(bf16[4,128,256]{2,1,0:T(8,128)(2,1)S(1)} %get-tuple-element.97), channel_id=1, source_target_pairs={{254,255},{255,254},{0,1},{1,0},{2,3},{3,2},{4,5},{5,4},{6,7},{7,6... | collective-permute-start | bytes 786440 | tf_op jit(solution)/shard_map/ppermute | solution.py:204
  133.9 31.6 %collective-permute-start.24 = (bf16[4,128,256]{2,1,0:T(8,128)(2,1)S(1)}, bf16[4,128,256]{2,1,0:T(8,128)(2,1)S(1)}, u32[]{:S(2)}, u32[]{:S(2)}) collective-permute-start(bf16[4,128,256]{2,1,0:T(8,128)(2,1)S(1)} %get-tuple-element.92), channel_id=1, source_target_pairs={{254,0},{255,1},{0,254},{1,255},{2,4},{3,5},{4,2},{5,3},{6,8},{7,9... | collective-permute-start | bytes 786440 | tf_op jit(solution)/shard_map/ppermute | solution.py:204
  137.7 34.9 %collective-permute-start.25 = (bf16[4,128,256]{2,1,0:T(8,128)(2,1)S(1)}, bf16[4,128,256]{2,1,0:T(8,128)(2,1)S(1)}, u32[]{:S(2)}, u32[]{:S(2)}) collective-permute-start(bf16[4,128,256]{2,1,0:T(8,128)(2,1)S(1)} %get-tuple-element.93), channel_id=1, source_target_pairs={{254,255},{255,254},{0,1},{1,0},{2,3},{3,2},{4,5},{5,4},{6,7},{7,6... | collective-permute-start | bytes 786440 | tf_op jit(solution)/shard_map/ppermute | solution.py:204
  145.4 36.3 %collective-permute-start.26 = (bf16[4,128,256]{2,1,0:T(8,128)(2,1)S(1)}, bf16[4,128,256]{2,1,0:T(8,128)(2,1)S(1)}, u32[]{:S(2)}, u32[]{:S(2)}) collective-permute-start(bf16[4,128,256]{2,1,0:T(8,128)(2,1)S(1)} %get-tuple-element.94), channel_id=1, source_target_pairs={{254,1},{255,0},{0,255},{1,254},{2,5},{3,4},{4,3},{5,2},{6,9},{7,8... | collective-permute-start | bytes 786440 | tf_op jit(solution)/shard_map/ppermute | solution.py:204
  152.1 35.7 %collective-permute-start.21 = (bf16[4,128,256]{2,1,0:T(8,128)(2,1)S(1)}, bf16[4,128,256]{2,1,0:T(8,128)(2,1)S(1)}, u32[]{:S(2)}, u32[]{:S(2)}) collective-permute-start(bf16[4,128,256]{2,1,0:T(8,128)(2,1)S(1)} %get-tuple-element.89), channel_id=1, source_target_pairs={{254,0},{255,1},{0,254},{1,255},{2,4},{3,5},{4,2},{5,3},{6,8},{7,9... | collective-permute-start | bytes 786440 | tf_op jit(solution)/shard_map/ppermute | solution.py:204
  159.7 36.9 %collective-permute-start.22 = (bf16[4,128,256]{2,1,0:T(8,128)(2,1)S(1)}, bf16[4,128,256]{2,1,0:T(8,128)(2,1)S(1)}, u32[]{:S(2)}, u32[]{:S(2)}) collective-permute-start(bf16[4,128,256]{2,1,0:T(8,128)(2,1)S(1)} %get-tuple-element.90), channel_id=1, source_target_pairs={{254,255},{255,254},{0,1},{1,0},{2,3},{3,2},{4,5},{5,4},{6,7},{7,6... | collective-permute-start | bytes 786440 | tf_op jit(solution)/shard_map/ppermute | solution.py:204
  165.5 40.9 %collective-permute-start.23 = (bf16[4,128,256]{2,1,0:T(8,128)(2,1)S(1)}, bf16[4,128,256]{2,1,0:T(8,128)(2,1)S(1)}, u32[]{:S(2)}, u32[]{:S(2)}) collective-permute-start(bf16[4,128,256]{2,1,0:T(8,128)(2,1)S(1)} %get-tuple-element.91), channel_id=1, source_target_pairs={{254,1},{255,0},{0,255},{1,254},{2,5},{3,4},{4,3},{5,2},{6,9},{7,8... | collective-permute-start | bytes 786440 | tf_op jit(solution)/shard_map/ppermute | solution.py:204
  172.7 37.8 %collective-permute-start.18 = (bf16[4,128,256]{2,1,0:T(8,128)(2,1)S(1)}, bf16[4,128,256]{2,1,0:T(8,128)(2,1)S(1)}, u32[]{:S(2)}, u32[]{:S(2)}) collective-permute-start(bf16[4,128,256]{2,1,0:T(8,128)(2,1)S(1)} %get-tuple-element.86), channel_id=1, source_target_pairs={{254,0},{255,1},{0,254},{1,255},{2,4},{3,5},{4,2},{5,3},{6,8},{7,9... | collective-permute-start | bytes 786440 | tf_op jit(solution)/shard_map/ppermute | solution.py:204
  181.7 34.1 %collective-permute-start.19 = (bf16[4,128,256]{2,1,0:T(8,128)(2,1)S(1)}, bf16[4,128,256]{2,1,0:T(8,128)(2,1)S(1)}, u32[]{:S(2)}, u32[]{:S(2)}) collective-permute-start(bf16[4,128,256]{2,1,0:T(8,128)(2,1)S(1)} %get-tuple-element.87), channel_id=1, source_target_pairs={{254,255},{255,254},{0,1},{1,0},{2,3},{3,2},{4,5},{5,4},{6,7},{7,6... | collective-permute-start | bytes 786440 | tf_op jit(solution)/shard_map/ppermute | solution.py:204
  187.9 31.1 %collective-permute-start.20 = (bf16[4,128,256]{2,1,0:T(8,128)(2,1)S(1)}, bf16[4,128,256]{2,1,0:T(8,128)(2,1)S(1)}, u32[]{:S(2)}, u32[]{:S(2)}) collective-permute-start(bf16[4,128,256]{2,1,0:T(8,128)(2,1)S(1)} %get-tuple-element.88), channel_id=1, source_target_pairs={{254,1},{255,0},{0,255},{1,254},{2,5},{3,4},{4,3},{5,2},{6,9},{7,8... | collective-permute-start | bytes 786440 | tf_op jit(solution)/shard_map/ppermute | solution.py:204
  196.6 30.8 %collective-permute-start.17 = (bf16[4,128,256]{2,1,0:T(8,128)(2,1)S(1)}, bf16[4,128,256]{2,1,0:T(8,128)(2,1)S(1)}, u32[]{:S(2)}, u32[]{:S(2)}) collective-permute-start(bf16[4,128,256]{2,1,0:T(8,128)(2,1)S(1)} %get-tuple-element.85), channel_id=1, source_target_pairs={{254,0},{255,1},{0,254},{1,255},{2,4},{3,5},{4,2},{5,3},{6,8},{7,9... | collective-permute-start | bytes 786440 | tf_op jit(solution)/shard_map/ppermute | solution.py:204
  206.4 21.8 %collective-permute-start.16 = (bf16[4,128,256]{2,1,0:T(8,128)(2,1)S(1)}, bf16[4,128,256]{2,1,0:T(8,128)(2,1)S(1)}, u32[]{:S(2)}, u32[]{:S(2)}) collective-permute-start(bf16[4,128,256]{2,1,0:T(8,128)(2,1)S(1)} %get-tuple-element.83), channel_id=1, source_target_pairs={{254,255},{255,254},{0,1},{1,0},{2,3},{3,2},{4,5},{5,4},{6,7},{7,6... | collective-permute-start | bytes 786440 | tf_op jit(solution)/shard_map/ppermute | solution.py:204
  210.5 25.3 %collective-permute-start.15 = (bf16[4,128,256]{2,1,0:T(8,128)(2,1)S(1)}, bf16[4,128,256]{2,1,0:T(8,128)(2,1)S(1)}, u32[]{:S(2)}, u32[]{:S(2)}) collective-permute-start(bf16[4,128,256]{2,1,0:T(8,128)(2,1)S(1)} %get-tuple-element.82), channel_id=1, source_target_pairs={{254,1},{255,0},{0,255},{1,254},{2,5},{3,4},{4,3},{5,2},{6,9},{7,8... | collective-permute-start | bytes 786440 | tf_op jit(solution)/shard_map/ppermute | solution.py:204

commit v5 on v4

--- a/solution.py
+++ b/solution.py
@@ -12,7 +12,7 @@
 MOST = 4
 AXES = ("seq", "uly")
 CHUNKS = (2, 2, 2, 2, 2)
-SWAPS = ((0, 3, 2, 1),) + ((0, 2, 1, 3),) * 4
+SWAPS = ((0, 3, 2, 1),) + ((0, 2, 3, 1),) * 4
 LAST = [(0, 1), (2,), (3,)]
 
 

time: 237 us -> 239 us (level)
  waiting for transfers between devices: 57.7 us -> 74.6 us
  starting transfers between devices: 118 us -> 103 us
    ppermute x30, waiting for transfers between devices: 57.7 us -> 74.6 us  [exchange(): lax.ppermute(piece, AXES, routes(swap, tiles))]
    ppermute x30, starting transfers between devices: 118 us -> 103 us  [exchange(): lax.ppermute(piece, AXES, routes(swap, tiles))]
  transfers between devices with their start and end apart: 30 -> 30, of which waited for: 10 -> 13; matrix products, arithmetic and copies ran while one was open for 1% -> 1% of each run, Pallas kernels for 20% -> 20%
where the time goes in v5:
time: 239 us
  starting transfers between devices  103 us (43%)
  waiting for transfers between devices  74.6 us (31%)
  Pallas kernels  50 us (21%)
  local copies, waits for them, and re-layouts  10.1 us (4%)
    ppermute x30, starting transfers between devices, exchange(): lax.ppermute(piece, AXES, routes(swap, tiles))  103 us
    ppermute x30, waiting for transfers between devices, exchange(): lax.ppermute(piece, AXES, routes(swap, tiles))  74.6 us
    pallas_call x5, Pallas kernels, attend(): pl.pallas_call(attend_kernel, out_shape=(piece,) * 4, grid_spec=pltpu.Pre...  34.5 us
    pallas_call x5, Pallas kernels, pack(): pl.pallas_call(partial(pack_kernel, swaps, begin, heads_each, width), out...  8.83 us
    unnamed x32, local copies, waits for them, and re-layouts  8.81 us
    pallas_call x7, Pallas kernels, unpack(): pl.pallas_call(partial(unpack_kernel, swaps, begin, heads_each, width), o...  6.71 us
  transfers between devices with their start and end apart: 30, of which 13 were waited for; matrix products, arithmetic and copies ran while one was open for 1% of the time, Pallas kernels for 20%

profile of v5, /device:TPU:0, one launch (start us, length us, event | category | flops | bytes accessed | tf_op | source)
XLA Modules:
  0.0 238.8 jit_solution(7532978858774604979)
XLA Ops:
  0.6 1.3 pack.5
  1.9 8.3 %collective-permute-start.12 = (bf16[4,128,256]{2,1,0:T(8,128)(2,1)S(1)}, bf16[4,128,256]{2,1,0:T(8,128)(2,1)S(1)}, u32[]{:S(2)}, u32[]{:S(2)}) collective-permute-start(bf16[4,128,256]{2,1,0:T(8,128)(2,1)S(1)} %get-tuple-element.63.rest_0_), channel_id=1, source_target_pairs={{254,1},{255,0},{0,255},{1,254},{2,5},{3,4},{4,3},{5,2},{6,9},{7,8... | collective-permute-start | bytes 786440 | tf_op jit(solution)/shard_map/ppermute | solution.py:204
  10.2 0.5 collective-permute-start.13
  10.8 1.4 collective-permute-start.14
  12.1 2.0 pack.6
  14.1 7.9 %collective-permute-start.9 = (bf16[4,128,256]{2,1,0:T(8,128)(2,1)S(1)}, bf16[4,128,256]{2,1,0:T(8,128)(2,1)S(1)}, u32[]{:S(2)}, u32[]{:S(2)}) collective-permute-start(bf16[4,128,256]{2,1,0:T(8,128)(2,1)S(1)} %get-tuple-element.64.rest_0_), channel_id=1, source_target_pairs={{254,0},{255,1},{0,254},{1,255},{2,4},{3,5},{4,2},{5,3},{6,8},{7,9... | collective-permute-start | bytes 786440 | tf_op jit(solution)/shard_map/ppermute | solution.py:204
  22.0 2.2 pack.7
  24.2 5.1 %collective-permute-done.12.one = bf16[4,128,256]{2,1,0:T(8,128)(2,1)S(1)} collective-permute-done((bf16[4,128,256]{2,1,0:T(8,128)(2,1)S(1)}, bf16[4,128,256]{2,1,0:T(8,128)(2,1)S(1)}, u32[]{:S(2)}, u32[]{:S(2)}) %collective-permute-start.12) | collective-permute-done | bytes 262176 | tf_op jit(solution)/shard_map/ppermute | solution.py:204
  29.3 12.5 %collective-permute-done.13.two = bf16[4,128,256]{2,1,0:T(8,128)(2,1)S(1)} collective-permute-done((bf16[4,128,256]{2,1,0:T(8,128)(2,1)S(1)}, bf16[4,128,256]{2,1,0:T(8,128)(2,1)S(1)}, u32[]{:S(2)}, u32[]{:S(2)}) %collective-permute-start.13) | collective-permute-done | bytes 262176 | tf_op jit(solution)/shard_map/ppermute | solution.py:204
  41.9 8.2 %collective-permute-start.6 = (bf16[4,128,256]{2,1,0:T(8,128)(2,1)}, bf16[4,128,256]{2,1,0:T(8,128)(2,1)}, u32[]{:S(2)}, u32[]{:S(2)}) collective-permute-start(bf16[4,128,256]{2,1,0:T(8,128)(2,1)} %get-tuple-element.65.rest_0_), channel_id=1, source_target_pairs={{254,0},{255,1},{0,254},{1,255},{2,4},{3,5},{4,2},{5,3},{6,8},{7,9... | collective-permute-start | bytes 786440 | tf_op jit(solution)/shard_map/ppermute | solution.py:204
  50.1 2.0 pack.8
  52.1 0.7 copy-done.9
  52.8 0.7 copy-done.11
  53.5 0.7 copy-done.6
  54.3 2.7 %collective-permute-start.7 = (bf16[4,128,256]{2,1,0:T(8,128)(2,1)}, bf16[4,128,256]{2,1,0:T(8,128)(2,1)}, u32[]{:S(2)}, u32[]{:S(2)}) collective-permute-start(bf16[4,128,256]{2,1,0:T(8,128)(2,1)} %get-tuple-element.72), channel_id=1, source_target_pairs={{254,1},{255,0},{0,255},{1,254},{2,5},{3,4},{4,3},{5,2},{6,9},{7,8... | collective-permute-start | bytes 786440 | tf_op jit(solution)/shard_map/ppermute | solution.py:204
  57.0 10.1 %collective-permute-done.10.two = bf16[4,128,256]{2,1,0:T(8,128)(2,1)S(1)} collective-permute-done((bf16[4,128,256]{2,1,0:T(8,128)(2,1)S(1)}, bf16[4,128,256]{2,1,0:T(8,128)(2,1)S(1)}, u32[]{:S(2)}, u32[]{:S(2)}) %collective-permute-start.10) | collective-permute-done | bytes 262176 | tf_op jit(solution)/shard_map/ppermute | solution.py:204
  67.2 1.4 pack.9
  68.6 0.7 copy-done.8
  69.3 0.7 copy-done.10
  70.0 0.7 copy-done.12
  70.7 0.6 gather_fusion.1
  71.4 0.6 gather_fusion
  72.0 4.6 %collective-permute-start.4 = (bf16[4,128,256]{2,1,0:T(8,128)(2,1)}, bf16[4,128,256]{2,1,0:T(8,128)(2,1)S(1)}, u32[]{:S(2)}, u32[]{:S(2)}) collective-permute-start(bf16[4,128,256]{2,1,0:T(8,128)(2,1)} %copy-done.11), channel_id=1, source_target_pairs={{254,1},{255,0},{0,255},{1,254},{2,5},{3,4},{4,3},{5,2},{6,9},{7,8... | collective-permute-start | bytes 786440 | tf_op jit(solution)/shard_map/ppermute | solution.py:204
  76.6 5.0 %collective-permute-start.5 = (bf16[4,128,256]{2,1,0:T(8,128)(2,1)}, bf16[4,128,256]{2,1,0:T(8,128)(2,1)S(1)}, u32[]{:S(2)}, u32[]{:S(2)}) collective-permute-start(bf16[4,128,256]{2,1,0:T(8,128)(2,1)} %copy-done.9), channel_id=1, source_target_pairs={{254,255},{255,254},{0,1},{1,0},{2,3},{3,2},{4,5},{5,4},{6,7},{7,6... | collective-permute-start | bytes 786440 | tf_op jit(solution)/shard_map/ppermute | solution.py:204
  81.7 5.3 %collective-permute-done.7.two = bf16[4,128,256]{2,1,0:T(8,128)(2,1)} collective-permute-done((bf16[4,128,256]{2,1,0:T(8,128)(2,1)}, bf16[4,128,256]{2,1,0:T(8,128)(2,1)}, u32[]{:S(2)}, u32[]{:S(2)}) %collective-permute-start.7) | collective-permute-done | bytes 262176 | tf_op jit(solution)/shard_map/ppermute | solution.py:204
  87.0 7.3 %collective-permute-start.1 = (bf16[4,128,256]{2,1,0:T(8,128)(2,1)}, bf16[4,128,256]{2,1,0:T(8,128)(2,1)S(1)}, u32[]{:S(2)}, u32[]{:S(2)}) collective-permute-start(bf16[4,128,256]{2,1,0:T(8,128)(2,1)} %copy-done.10), channel_id=1, source_target_pairs={{254,1},{255,0},{0,255},{1,254},{2,5},{3,4},{4,3},{5,2},{6,9},{7,8... | collective-permute-start | bytes 786440 | tf_op jit(solution)/shard_map/ppermute | solution.py:204
  94.3 9.6 %collective-permute-done.3.one = bf16[4,128,256]{2,1,0:T(8,128)(2,1)} collective-permute-done((bf16[4,128,256]{2,1,0:T(8,128)(2,1)}, bf16[4,128,256]{2,1,0:T(8,128)(2,1)}, u32[]{:S(2)}, u32[]{:S(2)}) %collective-permute-start.3) | collective-permute-done | bytes 262176 | tf_op jit(solution)/shard_map/ppermute | solution.py:204
  103.9 1.3 copy-done.2
  105.2 1.3 copy-done.3
  106.6 0.9 copy-done.5
  107.5 0.9 copy-done.7
  108.5 6.5 %attend.5 = (bf16[4,128,256]{2,1,0:T(8,128)(2,1)S(1)}, bf16[4,128,256]{2,1,0:T(8,128)(2,1)S(1)}, bf16[4,128,256]{2,1,0:T(8,128)(2,1)S(1)}, bf16[4,128,256]{2,1,0:T(8,128)(2,1)S(1)}) custom-call(s32[5]{0:T(128)S(1)} %pad_add_fusion.1.info, bf16[128,5120]{1,0:T(8,128)(2,1)S(1)} %copy-done, bf16[128,5120]{1,0:T(8,128)(2,1)S(1)} %copy-done.1, ...), custom_call_target="tpu_custom_call" | custom-call | flops 805306368 | bytes 2097152 | tf_op jit(solution)/shard_map/attend/pallas_call | solution.py:167
  114.9 8.6 %collective-permute-start.27 = (bf16[4,128,256]{2,1,0:T(8,128)(2,1)S(1)}, bf16[4,128,256]{2,1,0:T(8,128)(2,1)S(1)}, u32[]{:S(2)}, u32[]{:S(2)}) collective-permute-start(bf16[4,128,256]{2,1,0:T(8,128)(2,1)S(1)} %get-tuple-element.95), channel_id=1, source_target_pairs={{254,1},{255,0},{0,255},{1,254},{2,5},{3,4},{4,3},{5,2},{6,9},{7,8... | collective-permute-start | bytes 786440 | tf_op jit(solution)/shard_map/ppermute | solution.py:204
  123.5 1.0 collective-permute-start.28
  124.6 7.2 %attend.6 = (bf16[4,128,256]{2,1,0:T(8,128)(2,1)S(1)}, bf16[4,128,256]{2,1,0:T(8,128)(2,1)S(1)}, bf16[4,128,256]{2,1,0:T(8,128)(2,1)S(1)}, bf16[4,128,256]{2,1,0:T(8,128)(2,1)S(1)}) custom-call(s32[5]{0:T(128)S(1)} %pad_add_fusion.info, bf16[128,5120]{1,0:T(8,128)(2,1)S(1)} %copy-done, bf16[128,5120]{1,0:T(8,128)(2,1)S(1)} %copy-done.1, ...), custom_call_target="tpu_custom_call" | custom-call | flops 805306368 | bytes 2097152 | tf_op jit(solution)/shard_map/attend/pallas_call | solution.py:167
  131.8 0.8 collective-permute-start.29
  132.6 7.2 %collective-permute-start.24 = (bf16[4,128,256]{2,1,0:T(8,128)(2,1)S(1)}, bf16[4,128,256]{2,1,0:T(8,128)(2,1)S(1)}, u32[]{:S(2)}, u32[]{:S(2)}) collective-permute-start(bf16[4,128,256]{2,1,0:T(8,128)(2,1)S(1)} %get-tuple-element.92), channel_id=1, source_target_pairs={{254,0},{255,1},{0,254},{1,255},{2,4},{3,5},{4,2},{5,3},{6,8},{7,9... | collective-permute-start | bytes 786440 | tf_op jit(solution)/shard_map/ppermute | solution.py:204
  139.8 0.7 collective-permute-start.25
  140.5 7.3 %attend.7 = (bf16[4,128,256]{2,1,0:T(8,128)(2,1)S(1)}, bf16[4,128,256]{2,1,0:T(8,128)(2,1)S(1)}, bf16[4,128,256]{2,1,0:T(8,128)(2,1)S(1)}, bf16[4,128,256]{2,1,0:T(8,128)(2,1)S(1)}) custom-call(s32[5]{0:T(128)S(1)} %pad_add_fusion.info, bf16[128,5120]{1,0:T(8,128)(2,1)S(1)} %copy-done, bf16[128,5120]{1,0:T(8,128)(2,1)S(1)} %copy-done.1, ...), custom_call_target="tpu_custom_call" | custom-call | flops 805306368 | bytes 2097152 | tf_op jit(solution)/shard_map/attend/pallas_call | solution.py:167
  147.7 0.8 collective-permute-done.27.rest_1_
  148.5 0.9 collective-permute-start.26
  149.5 4.8 %collective-permute-done.28.rest_2_ = bf16[4,128,256]{2,1,0:T(8,128)(2,1)S(1)} collective-permute-done((bf16[4,128,256]{2,1,0:T(8,128)(2,1)S(1)}, bf16[4,128,256]{2,1,0:T(8,128)(2,1)S(1)}, u32[]{:S(2)}, u32[]{:S(2)}) %collective-permute-start.28) | collective-permute-done | bytes 262176 | tf_op jit(solution)/shard_map/ppermute | solution.py:204
  154.3 8.3 %collective-permute-start.21 = (bf16[4,128,256]{2,1,0:T(8,128)(2,1)S(1)}, bf16[4,128,256]{2,1,0:T(8,128)(2,1)S(1)}, u32[]{:S(2)}, u32[]{:S(2)}) collective-permute-start(bf16[4,128,256]{2,1,0:T(8,128)(2,1)S(1)} %get-tuple-element.89), channel_id=1, source_target_pairs={{254,0},{255,1},{0,254},{1,255},{2,4},{3,5},{4,2},{5,3},{6,8},{7,9... | collective-permute-start | bytes 786440 | tf_op jit(solution)/shard_map/ppermute | solution.py:204
  162.6 4.0 %collective-permute-start.22 = (bf16[4,128,256]{2,1,0:T(8,128)(2,1)S(1)}, bf16[4,128,256]{2,1,0:T(8,128)(2,1)S(1)}, u32[]{:S(2)}, u32[]{:S(2)}) collective-permute-start(bf16[4,128,256]{2,1,0:T(8,128)(2,1)S(1)} %get-tuple-element.90), channel_id=1, source_target_pairs={{254,1},{255,0},{0,255},{1,254},{2,5},{3,4},{4,3},{5,2},{6,9},{7,8... | collective-permute-start | bytes 786440 | tf_op jit(solution)/shard_map/ppermute | solution.py:204
  166.6 4.6 %collective-permute-done.24.rest_1_ = bf16[4,128,256]{2,1,0:T(8,128)(2,1)S(1)} collective-permute-done((bf16[4,128,256]{2,1,0:T(8,128)(2,1)S(1)}, bf16[4,128,256]{2,1,0:T(8,128)(2,1)S(1)}, u32[]{:S(2)}, u32[]{:S(2)}) %collective-permute-start.24) | collective-permute-done | bytes 262176 | tf_op jit(solution)/shard_map/ppermute | solution.py:204
  171.2 5.6 %collective-permute-start.23 = (bf16[4,128,256]{2,1,0:T(8,128)(2,1)S(1)}, bf16[4,128,256]{2,1,0:T(8,128)(2,1)S(1)}, u32[]{:S(2)}, u32[]{:S(2)}) collective-permute-start(bf16[4,128,256]{2,1,0:T(8,128)(2,1)S(1)} %get-tuple-element.91), channel_id=1, source_target_pairs={{254,255},{255,254},{0,1},{1,0},{2,3},{3,2},{4,5},{5,4},{6,7},{7,6... | collective-permute-start | bytes 786440 | tf_op jit(solution)/shard_map/ppermute | solution.py:204
  176.8 7.1 %attend.8 = (bf16[4,128,256]{2,1,0:T(8,128)(2,1)S(1)}, bf16[4,128,256]{2,1,0:T(8,128)(2,1)S(1)}, bf16[4,128,256]{2,1,0:T(8,128)(2,1)S(1)}, bf16[4,128,256]{2,1,0:T(8,128)(2,1)S(1)}) custom-call(s32[5]{0:T(128)S(1)} %pad_add_fusion.info, bf16[128,5120]{1,0:T(8,128)(2,1)S(1)} %copy-done, bf16[128,5120]{1,0:T(8,128)(2,1)S(1)} %copy-done.1, ...), custom_call_target="tpu_custom_call" | custom-call | flops 805306368 | bytes 2097152 | tf_op jit(solution)/shard_map/attend/pallas_call | solution.py:167
  183.9 2.7 %collective-permute-start.18 = (bf16[4,128,256]{2,1,0:T(8,128)(2,1)S(1)}, bf16[4,128,256]{2,1,0:T(8,128)(2,1)S(1)}, u32[]{:S(2)}, u32[]{:S(2)}) collective-permute-start(bf16[4,128,256]{2,1,0:T(8,128)(2,1)S(1)} %get-tuple-element.86), channel_id=1, source_target_pairs={{254,0},{255,1},{0,254},{1,255},{2,4},{3,5},{4,2},{5,3},{6,8},{7,9... | collective-permute-start | bytes 786440 | tf_op jit(solution)/shard_map/ppermute | solution.py:204
  186.6 4.0 %collective-permute-start.19 = (bf16[4,128,256]{2,1,0:T(8,128)(2,1)S(1)}, bf16[4,128,256]{2,1,0:T(8,128)(2,1)S(1)}, u32[]{:S(2)}, u32[]{:S(2)}) collective-permute-start(bf16[4,128,256]{2,1,0:T(8,128)(2,1)S(1)} %get-tuple-element.87), channel_id=1, source_target_pairs={{254,1},{255,0},{0,255},{1,254},{2,5},{3,4},{4,3},{5,2},{6,9},{7,8... | collective-permute-start | bytes 786440 | tf_op jit(solution)/shard_map/ppermute | solution.py:204
  190.6 2.9 %collective-permute-start.20 = (bf16[4,128,256]{2,1,0:T(8,128)(2,1)S(1)}, bf16[4,128,256]{2,1,0:T(8,128)(2,1)S(1)}, u32[]{:S(2)}, u32[]{:S(2)}) collective-permute-start(bf16[4,128,256]{2,1,0:T(8,128)(2,1)S(1)} %get-tuple-element.88), channel_id=1, source_target_pairs={{254,255},{255,254},{0,1},{1,0},{2,3},{3,2},{4,5},{5,4},{6,7},{7,6... | collective-permute-start | bytes 786440 | tf_op jit(solution)/shard_map/ppermute | solution.py:204
  193.6 6.5 %attend.9 = (bf16[4,128,256]{2,1,0:T(8,128)(2,1)S(1)}, bf16[4,128,256]{2,1,0:T(8,128)(2,1)S(1)}, bf16[4,128,256]{2,1,0:T(8,128)(2,1)S(1)}, bf16[4,128,256]{2,1,0:T(8,128)(2,1)S(1)}) custom-call(s32[5]{0:T(128)S(1)} %pad_add_fusion.info, bf16[128,5120]{1,0:T(8,128)(2,1)S(1)} %copy-done, bf16[128,5120]{1,0:T(8,128)(2,1)S(1)} %copy-done.1, ...), custom_call_target="tpu_custom_call" | custom-call | flops 805306368 | bytes 2097152 | tf_op jit(solution)/shard_map/attend/pallas_call | solution.py:167
  200.0 2.4 %collective-permute-done.22.rest_2_ = bf16[4,128,256]{2,1,0:T(8,128)(2,1)S(1)} collective-permute-done((bf16[4,128,256]{2,1,0:T(8,128)(2,1)S(1)}, bf16[4,128,256]{2,1,0:T(8,128)(2,1)S(1)}, u32[]{:S(2)}, u32[]{:S(2)}) %collective-permute-start.22) | collective-permute-done | bytes 262176 | tf_op jit(solution)/shard_map/ppermute | solution.py:204
  202.9 3.8 %collective-permute-start.16 = (bf16[4,128,256]{2,1,0:T(8,128)(2,1)S(1)}, bf16[4,128,256]{2,1,0:T(8,128)(2,1)S(1)}, u32[]{:S(2)}, u32[]{:S(2)}) collective-permute-start(bf16[4,128,256]{2,1,0:T(8,128)(2,1)S(1)} %get-tuple-element.83), channel_id=1, source_target_pairs={{254,1},{255,0},{0,255},{1,254},{2,5},{3,4},{4,3},{5,2},{6,9},{7,8... | collective-permute-start | bytes 786440 | tf_op jit(solution)/shard_map/ppermute | solution.py:204
  206.8 9.3 %collective-permute-done.18.rest_1_ = bf16[4,128,256]{2,1,0:T(8,128)(2,1)S(1)} collective-permute-done((bf16[4,128,256]{2,1,0:T(8,128)(2,1)S(1)}, bf16[4,128,256]{2,1,0:T(8,128)(2,1)S(1)}, u32[]{:S(2)}, u32[]{:S(2)}) %collective-permute-start.18) | collective-permute-done | bytes 262176 | tf_op jit(solution)/shard_map/ppermute | solution.py:204
  216.1 5.7 %collective-permute-start.15 = (bf16[4,128,256]{2,1,0:T(8,128)(2,1)S(1)}, bf16[4,128,256]{2,1,0:T(8,128)(2,1)S(1)}, u32[]{:S(2)}, u32[]{:S(2)}) collective-permute-start(bf16[4,128,256]{2,1,0:T(8,128)(2,1)S(1)} %get-tuple-element.82), channel_id=1, source_target_pairs={{254,255},{255,254},{0,1},{1,0},{2,3},{3,2},{4,5},{5,4},{6,7},{7,6... | collective-permute-start | bytes 786440 | tf_op jit(solution)/shard_map/ppermute | solution.py:204
  221.8 1.1 unpack.7
  222.9 1.1 unpack.8
  224.0 1.1 unpack.9
  225.1 0.8 collective-permute-done.19.rest_2_
  225.9 1.1 unpack.10
  227.5 0.8 unpack.11
  228.3 8.8 %collective-permute-done.16.rest_0_ = bf16[4,128,256]{2,1,0:T(8,128)(2,1)S(1)} collective-permute-done((bf16[4,128,256]{2,1,0:T(8,128)(2,1)S(1)}, bf16[4,128,256]{2,1,0:T(8,128)(2,1)S(1)}, u32[]{:S(2)}, u32[]{:S(2)}) %collective-permute-start.16) | collective-permute-done | bytes 262176 | tf_op jit(solution)/shard_map/ppermute | solution.py:204
  237.2 0.7 unpack.12
  237.9 0.7 unpack.13
  (53 shorter events, 1.2 us)
Async XLA Ops:
  1.9 27.4 %collective-permute-start.12 = (bf16[4,128,256]{2,1,0:T(8,128)(2,1)S(1)}, bf16[4,128,256]{2,1,0:T(8,128)(2,1)S(1)}, u32[]{:S(2)}, u32[]{:S(2)}) collective-permute-start(bf16[4,128,256]{2,1,0:T(8,128)(2,1)S(1)} %get-tuple-element.63.rest_0_), channel_id=1, source_target_pairs={{254,1},{255,0},{0,255},{1,254},{2,5},{3,4},{4,3},{5,2},{6,9},{7,8... | collective-permute-start | bytes 786440 | tf_op jit(solution)/shard_map/ppermute | solution.py:204
  10.2 31.6 %collective-permute-start.13 = (bf16[4,128,256]{2,1,0:T(8,128)(2,1)S(1)}, bf16[4,128,256]{2,1,0:T(8,128)(2,1)S(1)}, u32[]{:S(2)}, u32[]{:S(2)}) collective-permute-start(bf16[4,128,256]{2,1,0:T(8,128)(2,1)S(1)} %get-tuple-element.76), channel_id=1, source_target_pairs={{254,0},{255,1},{0,254},{1,255},{2,4},{3,5},{4,2},{5,3},{6,8},{7,9... | collective-permute-start | bytes 786440 | tf_op jit(solution)/shard_map/ppermute | solution.py:204
  10.8 11.2 %copy-start.13 = (s32[256]{0:T(256)S(1)}, s32[256]{0:T(256)}, u32[]{:S(2)}) copy-start(s32[256]{0:T(256)} %param.11) | copy-start | bytes 3076
  10.8 42.8 %collective-permute-start.14 = (bf16[4,128,256]{2,1,0:T(8,128)(2,1)S(1)}, bf16[4,128,256]{2,1,0:T(8,128)(2,1)S(1)}, u32[]{:S(2)}, u32[]{:S(2)}) collective-permute-start(bf16[4,128,256]{2,1,0:T(8,128)(2,1)S(1)} %get-tuple-element.77), channel_id=1, source_target_pairs={{254,255},{255,254},{0,1},{1,0},{2,3},{3,2},{4,5},{5,4},{6,7},{7,6... | collective-permute-start | bytes 786440 | tf_op jit(solution)/shard_map/ppermute | solution.py:204
  14.1 42.9 %collective-permute-start.9 = (bf16[4,128,256]{2,1,0:T(8,128)(2,1)S(1)}, bf16[4,128,256]{2,1,0:T(8,128)(2,1)S(1)}, u32[]{:S(2)}, u32[]{:S(2)}) collective-permute-start(bf16[4,128,256]{2,1,0:T(8,128)(2,1)S(1)} %get-tuple-element.64.rest_0_), channel_id=1, source_target_pairs={{254,0},{255,1},{0,254},{1,255},{2,4},{3,5},{4,2},{5,3},{6,8},{7,9... | collective-permute-start | bytes 786440 | tf_op jit(solution)/shard_map/ppermute | solution.py:204
  22.0 45.2 %collective-permute-start.10 = (bf16[4,128,256]{2,1,0:T(8,128)(2,1)S(1)}, bf16[4,128,256]{2,1,0:T(8,128)(2,1)S(1)}, u32[]{:S(2)}, u32[]{:S(2)}) collective-permute-start(bf16[4,128,256]{2,1,0:T(8,128)(2,1)S(1)} %get-tuple-element.74), channel_id=1, source_target_pairs={{254,1},{255,0},{0,255},{1,254},{2,5},{3,4},{4,3},{5,2},{6,9},{7,8... | collective-permute-start | bytes 786440 | tf_op jit(solution)/shard_map/ppermute | solution.py:204
  22.0 28.1 %copy-start.14 = (s32[4]{0:T(128)S(1)}, s32[4]{0:T(128)}, u32[]{:S(2)}) copy-start(s32[4]{0:T(128)} %constant.51.clone) | copy-start | bytes 52
  22.0 28.1 %copy-start.15 = (s32[4]{0:T(128)S(1)}, s32[4]{0:T(128)}, u32[]{:S(2)}) copy-start(s32[4]{0:T(128)} %constant.52.clone) | copy-start | bytes 52
  29.3 42.7 %collective-permute-start.11 = (bf16[4,128,256]{2,1,0:T(8,128)(2,1)}, bf16[4,128,256]{2,1,0:T(8,128)(2,1)}, u32[]{:S(2)}, u32[]{:S(2)}) collective-permute-start(bf16[4,128,256]{2,1,0:T(8,128)(2,1)} %get-tuple-element.75), channel_id=1, source_target_pairs={{254,255},{255,254},{0,1},{1,0},{2,3},{3,2},{4,5},{5,4},{6,7},{7,6... | collective-permute-start | bytes 786440 | tf_op jit(solution)/shard_map/ppermute | solution.py:204
  41.8 10.3 %copy-start.4 = (bf16[4,128,256]{2,1,0:T(8,128)(2,1)}, bf16[4,128,256]{2,1,0:T(8,128)(2,1)S(1)}, u32[]{:S(2)}) copy-start(bf16[4,128,256]{2,1,0:T(8,128)(2,1)S(1)} %collective-permute-done.13.two) | copy-start | bytes 786436
  41.9 34.7 %collective-permute-start.6 = (bf16[4,128,256]{2,1,0:T(8,128)(2,1)}, bf16[4,128,256]{2,1,0:T(8,128)(2,1)}, u32[]{:S(2)}, u32[]{:S(2)}) collective-permute-start(bf16[4,128,256]{2,1,0:T(8,128)(2,1)} %get-tuple-element.65.rest_0_), channel_id=1, source_target_pairs={{254,0},{255,1},{0,254},{1,255},{2,4},{3,5},{4,2},{5,3},{6,8},{7,9... | collective-permute-start | bytes 786440 | tf_op jit(solution)/shard_map/ppermute | solution.py:204
  52.1 0.7 copy-start.9
  52.8 0.7 copy-start.11
  53.5 0.7 copy-start.6
  54.3 32.7 %collective-permute-start.7 = (bf16[4,128,256]{2,1,0:T(8,128)(2,1)}, bf16[4,128,256]{2,1,0:T(8,128)(2,1)}, u32[]{:S(2)}, u32[]{:S(2)}) collective-permute-start(bf16[4,128,256]{2,1,0:T(8,128)(2,1)} %get-tuple-element.72), channel_id=1, source_target_pairs={{254,1},{255,0},{0,255},{1,254},{2,5},{3,4},{4,3},{5,2},{6,9},{7,8... | collective-permute-start | bytes 786440 | tf_op jit(solution)/shard_map/ppermute | solution.py:204
  57.0 30.0 %collective-permute-start.8 = (bf16[4,128,256]{2,1,0:T(8,128)(2,1)}, bf16[4,128,256]{2,1,0:T(8,128)(2,1)}, u32[]{:S(2)}, u32[]{:S(2)}) collective-permute-start(bf16[4,128,256]{2,1,0:T(8,128)(2,1)} %get-tuple-element.73), channel_id=1, source_target_pairs={{254,255},{255,254},{0,1},{1,0},{2,3},{3,2},{4,5},{5,4},{6,7},{7,6... | collective-permute-start | bytes 786440 | tf_op jit(solution)/shard_map/ppermute | solution.py:204
  67.2 36.7 %collective-permute-start.3 = (bf16[4,128,256]{2,1,0:T(8,128)(2,1)}, bf16[4,128,256]{2,1,0:T(8,128)(2,1)}, u32[]{:S(2)}, u32[]{:S(2)}) collective-permute-start(bf16[4,128,256]{2,1,0:T(8,128)(2,1)} %get-tuple-element.66.rest_0_), channel_id=1, source_target_pairs={{254,0},{255,1},{0,254},{1,255},{2,4},{3,5},{4,2},{5,3},{6,8},{7,9... | collective-permute-start | bytes 786440 | tf_op jit(solution)/shard_map/ppermute | solution.py:204
  67.2 36.7 %copy-start = (bf16[128,5120]{1,0:T(8,128)(2,1)S(1)}, bf16[128,5120]{1,0:T(8,128)(2,1)}, u32[]{:S(2)}) copy-start(bf16[128,5120]{1,0:T(8,128)(2,1)} %q_ref.19) | copy-start | bytes 3932164
  67.2 36.7 %copy-start.1 = (bf16[128,5120]{1,0:T(8,128)(2,1)S(1)}, bf16[128,5120]{1,0:T(8,128)(2,1)}, u32[]{:S(2)}) copy-start(bf16[128,5120]{1,0:T(8,128)(2,1)} %k_ref.19) | copy-start | bytes 3932164
  68.6 0.7 copy-start.8
  69.3 0.7 copy-start.10
  70.0 0.7 copy-start.12
  72.0 42.9 %collective-permute-start.4 = (bf16[4,128,256]{2,1,0:T(8,128)(2,1)}, bf16[4,128,256]{2,1,0:T(8,128)(2,1)S(1)}, u32[]{:S(2)}, u32[]{:S(2)}) collective-permute-start(bf16[4,128,256]{2,1,0:T(8,128)(2,1)} %copy-done.11), channel_id=1, source_target_pairs={{254,1},{255,0},{0,255},{1,254},{2,5},{3,4},{4,3},{5,2},{6,9},{7,8... | collective-permute-start | bytes 786440 | tf_op jit(solution)/shard_map/ppermute | solution.py:204
  76.6 47.0 %collective-permute-start.5 = (bf16[4,128,256]{2,1,0:T(8,128)(2,1)}, bf16[4,128,256]{2,1,0:T(8,128)(2,1)S(1)}, u32[]{:S(2)}, u32[]{:S(2)}) collective-permute-start(bf16[4,128,256]{2,1,0:T(8,128)(2,1)} %copy-done.9), channel_id=1, source_target_pairs={{254,255},{255,254},{0,1},{1,0},{2,3},{3,2},{4,5},{5,4},{6,7},{7,6... | collective-permute-start | bytes 786440 | tf_op jit(solution)/shard_map/ppermute | solution.py:204
  87.0 44.8 %collective-permute-start = (bf16[4,128,256]{2,1,0:T(8,128)(2,1)}, bf16[4,128,256]{2,1,0:T(8,128)(2,1)S(1)}, u32[]{:S(2)}, u32[]{:S(2)}) collective-permute-start(bf16[4,128,256]{2,1,0:T(8,128)(2,1)} %copy-done.12), channel_id=1, source_target_pairs={{254,0},{255,1},{0,254},{1,255},{2,4},{3,5},{4,2},{5,3},{6,8},{7,9... | collective-permute-start | bytes 786440 | tf_op jit(solution)/shard_map/ppermute | solution.py:204
  87.0 45.6 %collective-permute-start.1 = (bf16[4,128,256]{2,1,0:T(8,128)(2,1)}, bf16[4,128,256]{2,1,0:T(8,128)(2,1)S(1)}, u32[]{:S(2)}, u32[]{:S(2)}) collective-permute-start(bf16[4,128,256]{2,1,0:T(8,128)(2,1)} %copy-done.10), channel_id=1, source_target_pairs={{254,1},{255,0},{0,255},{1,254},{2,5},{3,4},{4,3},{5,2},{6,9},{7,8... | collective-permute-start | bytes 786440 | tf_op jit(solution)/shard_map/ppermute | solution.py:204
  103.8 36.0 %collective-permute-start.2 = (bf16[4,128,256]{2,1,0:T(8,128)(2,1)}, bf16[4,128,256]{2,1,0:T(8,128)(2,1)S(1)}, u32[]{:S(2)}, u32[]{:S(2)}) collective-permute-start(bf16[4,128,256]{2,1,0:T(8,128)(2,1)} %copy-done.8), channel_id=1, source_target_pairs={{254,255},{255,254},{0,1},{1,0},{2,3},{3,2},{4,5},{5,4},{6,7},{7,6... | collective-permute-start | bytes 786440 | tf_op jit(solution)/shard_map/ppermute | solution.py:204
  103.9 1.3 copy-start.2
  105.2 1.3 copy-start.3
  106.6 0.9 copy-start.5
  107.5 0.9 copy-start.7
  114.9 33.6 %collective-permute-start.27 = (bf16[4,128,256]{2,1,0:T(8,128)(2,1)S(1)}, bf16[4,128,256]{2,1,0:T(8,128)(2,1)S(1)}, u32[]{:S(2)}, u32[]{:S(2)}) collective-permute-start(bf16[4,128,256]{2,1,0:T(8,128)(2,1)S(1)} %get-tuple-element.95), channel_id=1, source_target_pairs={{254,1},{255,0},{0,255},{1,254},{2,5},{3,4},{4,3},{5,2},{6,9},{7,8... | collective-permute-start | bytes 786440 | tf_op jit(solution)/shard_map/ppermute | solution.py:204
  123.5 30.7 %collective-permute-start.28 = (bf16[4,128,256]{2,1,0:T(8,128)(2,1)S(1)}, bf16[4,128,256]{2,1,0:T(8,128)(2,1)S(1)}, u32[]{:S(2)}, u32[]{:S(2)}) collective-permute-start(bf16[4,128,256]{2,1,0:T(8,128)(2,1)S(1)} %get-tuple-element.96), channel_id=1, source_target_pairs={{254,0},{255,1},{0,254},{1,255},{2,4},{3,5},{4,2},{5,3},{6,8},{7,9... | collective-permute-start | bytes 786440 | tf_op jit(solution)/shard_map/ppermute | solution.py:204
  131.8 30.8 %collective-permute-start.29 = (bf16[4,128,256]{2,1,0:T(8,128)(2,1)S(1)}, bf16[4,128,256]{2,1,0:T(8,128)(2,1)S(1)}, u32[]{:S(2)}, u32[]{:S(2)}) collective-permute-start(bf16[4,128,256]{2,1,0:T(8,128)(2,1)S(1)} %get-tuple-element.97), channel_id=1, source_target_pairs={{254,255},{255,254},{0,1},{1,0},{2,3},{3,2},{4,5},{5,4},{6,7},{7,6... | collective-permute-start | bytes 786440 | tf_op jit(solution)/shard_map/ppermute | solution.py:204
  132.6 38.6 %collective-permute-start.24 = (bf16[4,128,256]{2,1,0:T(8,128)(2,1)S(1)}, bf16[4,128,256]{2,1,0:T(8,128)(2,1)S(1)}, u32[]{:S(2)}, u32[]{:S(2)}) collective-permute-start(bf16[4,128,256]{2,1,0:T(8,128)(2,1)S(1)} %get-tuple-element.92), channel_id=1, source_target_pairs={{254,0},{255,1},{0,254},{1,255},{2,4},{3,5},{4,2},{5,3},{6,8},{7,9... | collective-permute-start | bytes 786440 | tf_op jit(solution)/shard_map/ppermute | solution.py:204
  139.8 44.1 %collective-permute-start.25 = (bf16[4,128,256]{2,1,0:T(8,128)(2,1)S(1)}, bf16[4,128,256]{2,1,0:T(8,128)(2,1)S(1)}, u32[]{:S(2)}, u32[]{:S(2)}) collective-permute-start(bf16[4,128,256]{2,1,0:T(8,128)(2,1)S(1)} %get-tuple-element.93), channel_id=1, source_target_pairs={{254,1},{255,0},{0,255},{1,254},{2,5},{3,4},{4,3},{5,2},{6,9},{7,8... | collective-permute-start | bytes 786440 | tf_op jit(solution)/shard_map/ppermute | solution.py:204
  148.5 38.1 %collective-permute-start.26 = (bf16[4,128,256]{2,1,0:T(8,128)(2,1)S(1)}, bf16[4,128,256]{2,1,0:T(8,128)(2,1)S(1)}, u32[]{:S(2)}, u32[]{:S(2)}) collective-permute-start(bf16[4,128,256]{2,1,0:T(8,128)(2,1)S(1)} %get-tuple-element.94), channel_id=1, source_target_pairs={{254,255},{255,254},{0,1},{1,0},{2,3},{3,2},{4,5},{5,4},{6,7},{7,6... | collective-permute-start | bytes 786440 | tf_op jit(solution)/shard_map/ppermute | solution.py:204
  154.3 36.4 %collective-permute-start.21 = (bf16[4,128,256]{2,1,0:T(8,128)(2,1)S(1)}, bf16[4,128,256]{2,1,0:T(8,128)(2,1)S(1)}, u32[]{:S(2)}, u32[]{:S(2)}) collective-permute-start(bf16[4,128,256]{2,1,0:T(8,128)(2,1)S(1)} %get-tuple-element.89), channel_id=1, source_target_pairs={{254,0},{255,1},{0,254},{1,255},{2,4},{3,5},{4,2},{5,3},{6,8},{7,9... | collective-permute-start | bytes 786440 | tf_op jit(solution)/shard_map/ppermute | solution.py:204
  162.6 39.9 %collective-permute-start.22 = (bf16[4,128,256]{2,1,0:T(8,128)(2,1)S(1)}, bf16[4,128,256]{2,1,0:T(8,128)(2,1)S(1)}, u32[]{:S(2)}, u32[]{:S(2)}) collective-permute-start(bf16[4,128,256]{2,1,0:T(8,128)(2,1)S(1)} %get-tuple-element.90), channel_id=1, source_target_pairs={{254,1},{255,0},{0,255},{1,254},{2,5},{3,4},{4,3},{5,2},{6,9},{7,8... | collective-permute-start | bytes 786440 | tf_op jit(solution)/shard_map/ppermute | solution.py:204
  171.2 31.8 %collective-permute-start.23 = (bf16[4,128,256]{2,1,0:T(8,128)(2,1)S(1)}, bf16[4,128,256]{2,1,0:T(8,128)(2,1)S(1)}, u32[]{:S(2)}, u32[]{:S(2)}) collective-permute-start(bf16[4,128,256]{2,1,0:T(8,128)(2,1)S(1)} %get-tuple-element.91), channel_id=1, source_target_pairs={{254,255},{255,254},{0,1},{1,0},{2,3},{3,2},{4,5},{5,4},{6,7},{7,6... | collective-permute-start | bytes 786440 | tf_op jit(solution)/shard_map/ppermute | solution.py:204
  183.9 32.1 %collective-permute-start.18 = (bf16[4,128,256]{2,1,0:T(8,128)(2,1)S(1)}, bf16[4,128,256]{2,1,0:T(8,128)(2,1)S(1)}, u32[]{:S(2)}, u32[]{:S(2)}) collective-permute-start(bf16[4,128,256]{2,1,0:T(8,128)(2,1)S(1)} %get-tuple-element.86), channel_id=1, source_target_pairs={{254,0},{255,1},{0,254},{1,255},{2,4},{3,5},{4,2},{5,3},{6,8},{7,9... | collective-permute-start | bytes 786440 | tf_op jit(solution)/shard_map/ppermute | solution.py:204
  186.6 39.3 %collective-permute-start.19 = (bf16[4,128,256]{2,1,0:T(8,128)(2,1)S(1)}, bf16[4,128,256]{2,1,0:T(8,128)(2,1)S(1)}, u32[]{:S(2)}, u32[]{:S(2)}) collective-permute-start(bf16[4,128,256]{2,1,0:T(8,128)(2,1)S(1)} %get-tuple-element.87), channel_id=1, source_target_pairs={{254,1},{255,0},{0,255},{1,254},{2,5},{3,4},{4,3},{5,2},{6,9},{7,8... | collective-permute-start | bytes 786440 | tf_op jit(solution)/shard_map/ppermute | solution.py:204
  190.6 35.3 %collective-permute-start.20 = (bf16[4,128,256]{2,1,0:T(8,128)(2,1)S(1)}, bf16[4,128,256]{2,1,0:T(8,128)(2,1)S(1)}, u32[]{:S(2)}, u32[]{:S(2)}) collective-permute-start(bf16[4,128,256]{2,1,0:T(8,128)(2,1)S(1)} %get-tuple-element.88), channel_id=1, source_target_pairs={{254,255},{255,254},{0,1},{1,0},{2,3},{3,2},{4,5},{5,4},{6,7},{7,6... | collective-permute-start | bytes 786440 | tf_op jit(solution)/shard_map/ppermute | solution.py:204
  202.4 25.1 %collective-permute-start.17 = (bf16[4,128,256]{2,1,0:T(8,128)(2,1)S(1)}, bf16[4,128,256]{2,1,0:T(8,128)(2,1)S(1)}, u32[]{:S(2)}, u32[]{:S(2)}) collective-permute-start(bf16[4,128,256]{2,1,0:T(8,128)(2,1)S(1)} %get-tuple-element.85), channel_id=1, source_target_pairs={{254,0},{255,1},{0,254},{1,255},{2,4},{3,5},{4,2},{5,3},{6,8},{7,9... | collective-permute-start | bytes 786440 | tf_op jit(solution)/shard_map/ppermute | solution.py:204
  202.9 34.2 %collective-permute-start.16 = (bf16[4,128,256]{2,1,0:T(8,128)(2,1)S(1)}, bf16[4,128,256]{2,1,0:T(8,128)(2,1)S(1)}, u32[]{:S(2)}, u32[]{:S(2)}) collective-permute-start(bf16[4,128,256]{2,1,0:T(8,128)(2,1)S(1)} %get-tuple-element.83), channel_id=1, source_target_pairs={{254,1},{255,0},{0,255},{1,254},{2,5},{3,4},{4,3},{5,2},{6,9},{7,8... | collective-permute-start | bytes 786440 | tf_op jit(solution)/shard_map/ppermute | solution.py:204
  216.1 21.8 %collective-permute-start.15 = (bf16[4,128,256]{2,1,0:T(8,128)(2,1)S(1)}, bf16[4,128,256]{2,1,0:T(8,128)(2,1)S(1)}, u32[]{:S(2)}, u32[]{:S(2)}) collective-permute-start(bf16[4,128,256]{2,1,0:T(8,128)(2,1)S(1)} %get-tuple-element.82), channel_id=1, source_target_pairs={{254,255},{255,254},{0,1},{1,0},{2,3},{3,2},{4,5},{5,4},{6,7},{7,6... | collective-permute-start | bytes 786440 | tf_op jit(solution)/shard_map/ppermute | solution.py:204
